TPU v7x, 32 devices: a whole 2x2x4 slice. The times are simulated.
32 devices in a mesh: modes: 2 (over x), space: 16 (over z, y, core).
Axes of the slice: x: 2, y: 2, z: 4, core: 2. Of those that a mesh axis runs over, the one named last changes fastest.
Arguments:
- mode_coeffs: float32 [120, 16, 120, 128], P('modes', 'space'), may hold values from -6 to 6
- mean_perm: float32 [16, 120, 128], P('space'), may hold values from 0.5 to 2
- kl_fields: float32 [7, 16, 120, 128], P(None, 'space'), may hold values from -4 to 4
- couplings: float32 [7, 120, 120], replicated, may hold values from -0.5 to 0.5
Outputs:
- applied: float32 [120, 16, 120, 128], P('modes', 'space')
All inputs are finite; a program needn't handle non-finite values.
Results may differ from a plain program's by a relative error of at most 0.0001.
Values sent between devices are 32-bit elements; how exact they have to be, the bound alone decides.
No kernel may reach another device: no remote copies, remote signals or barrier semaphores. Data moves between devices by JAX's collectives and lax.ppermute only.
A program may use at most 448 MiB of HBM per device.

v0:
```python
import jax
import jax.numpy as jnp
from jax import lax
from jax.sharding import PartitionSpec as P


def extended(block, sides, width):
    for axis, dim in sides:
        count = lax.axis_size(axis)
        forward = [(i, i + 1) for i in range(count - 1)]
        backward = [(target, source) for source, target in forward]
        low = lax.ppermute(
            lax.slice_in_dim(block, block.shape[dim] - width, None, axis=dim), axis, forward
        )
        high = lax.ppermute(lax.slice_in_dim(block, 0, width, axis=dim), axis, backward)
        block = jnp.concatenate([low, block, high], axis=dim)
    return block


def shifted(padded, direction, offset):
    result = padded
    base = padded.ndim - 3
    for axis_index in range(3):
        extent = padded.shape[base + axis_index] - 2
        begin = offset if axis_index == direction else 1
        result = lax.slice_in_dim(result, begin, begin + extent, axis=base + axis_index)
    return result


def operate(field_pad, perm_pad):
    centre = shifted(field_pad, 0, 1)
    centre_perm = shifted(perm_pad, 0, 1)
    terms = []
    for direction in range(3):
        for offset in (0, 2):
            face_perm = 0.5 * (centre_perm + shifted(perm_pad, direction, offset))
            terms.append(face_perm * (centre - shifted(field_pad, direction, offset)))
    accum_total = terms[0]
    for extra_term in terms[1:]:
        accum_total = accum_total + extra_term
    return accum_total


def local(mode_coeffs, mean_perm, kl_fields, couplings):
    mode_dev = mode_coeffs.shape[0]
    shape_cells = mode_coeffs.shape[1:]
    term_count = kl_fields.shape[0] + 1
    all_perm = jnp.concatenate([mean_perm[None], kl_fields], 0)
    perm_halo = extended(all_perm, (("space", 1),), 1)
    perm_pad = jnp.pad(perm_halo, ((0, 0), (0, 0), (1, 1), (1, 1)))[:, None]
    first_mode = lax.axis_index("modes") * mode_dev
    own_rows = lax.dynamic_slice_in_dim(couplings, first_mode, mode_dev, 1)
    block_piece = lax.all_gather(mode_coeffs, "modes", axis=0, tiled=True)
    flat_piece = block_piece.reshape(block_piece.shape[0], -1)
    mixed_modes = jnp.einsum("kin,nc->kic", own_rows, flat_piece, precision=lax.Precision.HIGHEST)
    fields = jnp.concatenate(
        [mode_coeffs[None], mixed_modes.reshape((term_count - 1, mode_dev) + shape_cells)], 0
    )
    field_halo = extended(fields, (("space", 2),), 1)
    field_pad = jnp.pad(field_halo, ((0, 0), (0, 0), (0, 0), (1, 1), (1, 1)))
    return jnp.sum(operate(field_pad, perm_pad), axis=0)


def solution(mesh):
    in_specs = (
        P("modes", "space", None, None),
        P("space", None, None),
        P(None, "space", None, None),
        P(),
    )
    out_specs = P("modes", "space", None, None)
    return jax.shard_map(local, mesh=mesh, in_specs=in_specs, out_specs=out_specs, check_vma=False)
```

profile of v0, /device:TPU:17, one launch (start us, length us, event | category | flops | bytes accessed | tf_op | source)
XLA Modules:
  0.0 1091.2 jit_solution(12888793817046607654)
XLA Ops:
  6.5 0.7 all-gather.2.cloned.1.call-update
  7.3 4.8 copy.30
  12.0 90.5 %all-gather.2.cloned.1.call-done = f32[120,1,120,128]{3,2,1,0:T(8,128)} async-done(((f32[60,1,120,128]{3,2,1,0:T(8,128)}), f32[120,1,120,128]{3,2,1,0:T(8,128)}) %all-gather.2.cloned.1.call-update) | async-done | bytes 7372816 | tf_op jit(solution)/shard_map/all_gather | solution.py:53
  102.6 24.9 %convolution_bitcast_fusion = f32[7,60,1,120,128]{4,1,3,0,2:T(8,128)S(1)} fusion(f32[7,120,120]{2,1,0:T(8,128)S(1)} %copy-done, s32[]{:T(128)S(6)} %select_n.3, f32[15,8,120,128]{3,2,1,0:T(8,128)} %bitcast.47), kind=kOutput, calls=%fused_computation.24 | convolution fusion | flops 9289728000 | bytes 33406980 | tf_op jit(solution)/shard_map/kin,nc->kic/dot_general | solution.py:55
  127.5 13.0 %pad_maximum_fusion = f32[8,60,1,120,128]{4,1,3,0,2:T(8,128)} fusion(f32[7,60,1,120,128]{4,1,3,0,2:T(8,128)S(1)} %convolution_bitcast_fusion, f32[1,60,1,120,128]{4,1,3,0,2:T(8,128)S(1)} %bitcast.43), kind=kLoop, calls=%fused_computation.23 | loop fusion | flops 7372800 | bytes 58982400 | tf_op jit(solution)/shard_map/concatenate | solution.py:56
  140.5 5.5 copy-done.2
  146.0 29.0 %copy.10 = f32[8,60,1,120,128]{4,3,2,1,0:T(8,128)} copy(f32[8,60,1,120,128]{4,1,3,0,2:T(8,128)} %pad_maximum_fusion) | data formatting | bytes 58982400 | tf_op jit(solution)/shard_map/concatenate | solution.py:56
  175.0 3.8 collective-permute-start.2
  178.8 1.9 collective-permute-start.3
  180.8 3.6 collective-permute-start
  184.4 1.9 collective-permute-start.1
  186.4 635.5 %collective-permute-done = f32[8,1,120,128]{3,2,1,0:T(8,128)S(1)} collective-permute-done((f32[8,1,120,128]{3,2,1,0:T(8,128)S(1)}, f32[8,1,120,128]{3,2,1,0:T(8,128)S(1)}, u32[]{:S(2)}, u32[]{:S(2)}) %collective-permute-start) | collective-permute-done | bytes 491552 | tf_op jit(solution)/shard_map/ppermute | solution.py:12
  821.8 1.6 collective-permute-done.1
  823.5 2.8 fusion.13
  826.2 5.2 fusion.28
  831.5 0.0 collective-permute-done.2
  831.5 9.7 copy-done.3
  841.2 12.2 %copy.11 = f32[8,60,1,120,128]{4,1,3,0,2:T(8,128)} copy(f32[8,60,1,120,128]{4,3,2,1,0:T(8,128)S(1)} %collective-permute-done.2) | data formatting | bytes 58982400 | tf_op jit(solution)/shard_map/ppermute | solution.py:12
  853.4 0.0 collective-permute-done.3
  853.4 25.7 %copy.13 = f32[8,60,1,120,128]{4,1,3,0,2:T(8,128)} copy(f32[8,60,1,120,128]{4,3,2,1,0:T(8,128)} %collective-permute-done.3) | data formatting | bytes 58982400 | tf_op jit(solution)/shard_map/ppermute | solution.py:15
  879.1 103.3 %select_maximum_fusion = f32[8,60,3,122,130]{4,1,3,0,2:T(8,128)} fusion(f32[8,60,1,120,128]{4,1,3,0,2:T(8,128)} %copy.13, f32[8,60,1,120,128]{4,1,3,0,2:T(8,128)} %copy.11, f32[7,60,1,120,128]{4,1,3,0,2:T(8,128)} %copy-done.2, f32[1,60,1,120,128]{4,1,3,0,2:T(8,128)S(1)} %bitcast.44), kind=kLoop, calls=%fused_computation.4 | loop fusion | flops 411091200 | bytes 179827200 | tf_op jit(solution)/shard_map/concatenate | solution.py:16
  982.4 0.0 copy-start.1
  982.4 95.8 %fusion.5 = f32[60,120,128]{2,0,1:T(8,128)} fusion(f32[8,60,3,122,130]{4,1,3,0,2:T(8,128)} %select_maximum_fusion, f32[8,120,128]{2,1,0:T(8,128)} %get-tuple-element.10, f32[8,120,128]{2,1,0:T(8,128)S(1)} %get-tuple-element.6, f32[8,120,128]{2,1,0:T(8,128)S(1)} %get-tuple-element.7, f32[8,120,128]{2,1,0:T(8,128)S(1)} %get-tuple-element.8, ...), kind=kLoop, calls=%fused_computation.13 | loop fusion | flops 139161600 | bytes 213073920 | tf_op jit(solution)/shard_map/reduce_sum | solution.py:61
  1078.3 6.1 copy.16
  (13 shorter events, 0.1 us)
Async XLA Ops:
  6.5 96.0 %copy-start = (f32[7,120,120]{2,1,0:T(8,128)S(1)}, f32[7,120,120]{2,1,0:T(8,128)}, u32[]{:S(2)}) copy-start(f32[7,120,120]{2,1,0:T(8,128)} %param.7) | copy-start | bytes 1209604
  6.5 96.0 %all-gather.2.cloned.1.call-start = ((), (), s32[]{:S(2)}) async-start(), calls=%async_computation | async-start | bytes 11059200 | tf_op jit(solution)/shard_map/all_gather | solution.py:53
  102.6 24.9 %copy-start.4 = (f32[60,1,120,128]{3,0,2,1:T(8,128)S(1)}, f32[60,1,120,128]{3,0,2,1:T(8,128)}, u32[]{:S(2)}) copy-start(f32[60,1,120,128]{3,0,2,1:T(8,128)} %copy.30) | copy-start | bytes 11059204
  127.5 18.5 %copy-start.2 = (f32[7,60,1,120,128]{4,1,3,0,2:T(8,128)}, f32[7,60,1,120,128]{4,1,3,0,2:T(8,128)S(1)}, u32[]{:S(2)}) copy-start(f32[7,60,1,120,128]{4,1,3,0,2:T(8,128)S(1)} %convolution_bitcast_fusion) | copy-start | bytes 77414400
  146.0 34.7 %copy-start.5 = (f32[7,1,120,128]{3,2,1,0:T(8,128)S(1)}, f32[7,1,120,128]{3,2,1,0:T(8,128)}, u32[]{:S(2)}) copy-start(f32[7,1,120,128]{3,2,1,0:T(8,128)} %param.6) | copy-start | bytes 1290244
  146.0 34.7 %copy-start.6 = (f32[1,120,128]{2,1,0:T(8,128)S(1)}, f32[1,120,128]{2,1,0:T(8,128)}, u32[]{:S(2)}) copy-start(f32[1,120,128]{2,1,0:T(8,128)} %param.5) | copy-start | bytes 184324
  175.0 656.5 %collective-permute-start.2 = (f32[8,60,1,120,128]{4,3,2,1,0:T(8,128)}, f32[8,60,1,120,128]{4,3,2,1,0:T(8,128)S(1)}, u32[]{:S(2)}, u32[]{:S(2)}) collective-permute-start(f32[8,60,1,120,128]{4,3,2,1,0:T(8,128)} %copy.10), channel_id=1, source_target_pairs={{0,1},{1,2},{2,3},{3,4},{4,5},{5,6},{6,7},{7,8},{8,9},{9,10},{10,1... | collective-permute-start | bytes 88473608 | tf_op jit(solution)/shard_map/ppermute | solution.py:12
  178.8 674.6 %collective-permute-start.3 = (f32[8,60,1,120,128]{4,3,2,1,0:T(8,128)}, f32[8,60,1,120,128]{4,3,2,1,0:T(8,128)}, u32[]{:S(2)}, u32[]{:S(2)}) collective-permute-start(f32[8,60,1,120,128]{4,3,2,1,0:T(8,128)} %copy.10), channel_id=1, source_target_pairs={{1,0},{2,1},{3,2},{4,3},{5,4},{6,5},{7,6},{8,7},{9,8},{10,9},{11,1... | collective-permute-start | bytes 88473608 | tf_op jit(solution)/shard_map/ppermute | solution.py:15
  180.8 641.0 %collective-permute-start = (f32[8,1,120,128]{3,2,1,0:T(8,128)S(1)}, f32[8,1,120,128]{3,2,1,0:T(8,128)S(1)}, u32[]{:S(2)}, u32[]{:S(2)}) collective-permute-start(f32[8,1,120,128]{3,2,1,0:T(8,128)S(1)} %pad_maximum_fusion.1), channel_id=1, source_target_pairs={{0,1},{1,2},{2,3},{3,4},{4,5},{5,6},{6,7},{7,8},{8,9},{9,10},{10,1... | collective-permute-start | bytes 1474568 | tf_op jit(solution)/shard_map/ppermute | solution.py:12
  184.4 639.0 %collective-permute-start.1 = (f32[8,1,120,128]{3,2,1,0:T(8,128)S(1)}, f32[8,1,120,128]{3,2,1,0:T(8,128)S(1)}, u32[]{:S(2)}, u32[]{:S(2)}) collective-permute-start(f32[8,1,120,128]{3,2,1,0:T(8,128)S(1)} %pad_maximum_fusion.1), channel_id=1, source_target_pairs={{1,0},{2,1},{3,2},{4,3},{5,4},{6,5},{7,6},{8,7},{9,8},{10,9},{11,1... | collective-permute-start | bytes 1474568 | tf_op jit(solution)/shard_map/ppermute | solution.py:15
  831.5 9.7 copy-start.3
  982.4 101.9 %copy-start.1 = (f32[7,120,120]{2,1,0:T(8,128)S(1)}, f32[7,120,120]{2,1,0:T(8,128)}, u32[]{:S(2)}) copy-start(f32[7,120,120]{2,1,0:T(8,128)} %param.7) | copy-start | bytes 1209604
Sparse Core Ops, SparseCore 0:
  8.9 93.6 all-gather.1
where the time goes:
time: 1090 us
  waiting for transfers between devices  728 us (67%)
  other arithmetic  220 us (20%)
  local copies, waits for them, and re-layouts  93 us (9%)
  matrix products  24.9 us (2%)
  between operations  13.5 us (1%)
  starting transfers between devices  11.3 us (1%)
    ppermute x2, waiting for transfers between devices, extended(): lax.ppermute(lax.slice_in_dim(block, block.shape[dim] - width, None, axis...  635 us
    concatenate x1, other arithmetic, extended(): block = jnp.concatenate([low, block, high], axis=dim)  103 us
    reduce_sum x1, other arithmetic, local(): return jnp.sum(operate(field_pad, perm_pad), axis=0)  95.8 us
    all_gather x1, waiting for transfers between devices, local(): block_piece = lax.all_gather(mode_coeffs, 'modes', axis=0, tiled=True)  90.5 us
    concatenate x1, local copies, waits for them, and re-layouts, local(): jnp.concatenate([mode_coeffs[None], mixed_modes.reshape((term_count - 1,...  29 us
    ppermute x1, local copies, waits for them, and re-layouts, extended(): lax.ppermute(lax.slice_in_dim(block, 0, width, axis=dim), axis, backward)  25.7 us
    dot_general x1, matrix products, local(): jnp.einsum('kin,nc->kic', own_rows, flat_piece, precision=lax.Precision.H...  24.9 us
  transfers between devices with their start and end apart: 5, of which 3 were waited for; matrix products, arithmetic and copies ran while one was open for 2% of the time, Pallas kernels for 0%

commit v1 on v0

v1 whole, which is shorter than its diff:
```python
import functools

import jax
import jax.numpy as jnp
from jax import lax
from jax.experimental import pallas as pl
from jax.experimental.pallas import tpu as pltpu
from jax.sharding import PartitionSpec as P

SUB = 8
PACK = 16
FACES = 6
LIMIT = 48 * 2**20
VMEM = pl.BlockSpec(memory_space=pltpu.VMEM)


def halves(value):
    high = value.astype(jnp.bfloat16)
    low = (value - high.astype(jnp.float32)).astype(jnp.bfloat16)
    return high, low


def face_coefs(coef, perm, perm_up, perm_down, begin, count):
    terms = perm.shape[0]
    lane = lax.broadcasted_iota(jnp.int32, (count, perm.shape[2]), 1)
    width = perm.shape[2]
    for k in range(terms):
        here = perm[k, pl.ds(begin + SUB, count), :]
        others = (
            perm_up[k, pl.ds(begin + SUB, count), :],
            perm_down[k, pl.ds(begin + SUB, count), :],
            perm[k, pl.ds(begin + SUB + 1, count), :],
            perm[k, pl.ds(begin + SUB - 1, count), :],
            jnp.where(lane < width - 1, pltpu.roll(here, width - 1, 1), 0.0),
            jnp.where(lane > 0, pltpu.roll(here, 1, 1), 0.0),
        )
        for f, other in enumerate(others):
            coef[f * terms + k, pl.ds(0, count), :] = 0.5 * (here + other)


def strided_rows(ref, start, count, stride):
    return ref[pl.ds(start, count, stride=stride), :]


def gathered_kernel(first, count, rows, mode_dev, pad, groups, sources, *refs):
    own, perm, perm_up, perm_down, weights = refs[:5]
    pieces = refs[5 : 5 + len(sources) * (groups - 1)]
    out, to_up, to_down = refs[5 + len(pieces) : 8 + len(pieces)]
    coef, cells, stack, mixed, pending, above = refs[8 + len(pieces) :]
    terms = perm.shape[0]
    nz = own.shape[1]
    low_row, last = max(first - 1, 0), min(first + count, rows - 1)
    face_coefs(coef, perm, perm_up, perm_down, low_row, last - low_row + 1)
    cells[...] = jnp.zeros_like(cells)
    pending[...] = jnp.zeros_like(pending)
    above[...] = jnp.zeros_like(above)
    lane = lax.broadcasted_iota(jnp.int32, (SUB, nz), 1)
    wide = groups * pad

    def fill(slot, row, source):
        lanes = pl.ds(slot * nz, nz)
        start, length, at = source
        cells[slot, 0, :mode_dev, :] = strided_rows(own, row, mode_dev, rows)
        for s in range(1, groups):
            piece = pieces[at * (groups - 1) + s - 1]
            cells[slot, s, :mode_dev, :] = strided_rows(piece, row - start, mode_dev, length)
        high, low = halves(cells[slot].reshape(wide, nz))
        stack[0:wide, lanes] = high
        stack[wide : 2 * wide, lanes] = low
        stack[2 * wide : 3 * wide, lanes] = high

    def finish(row, block, value):
        size = min(SUB, mode_dev - block * SUB)
        out[pl.ds(block * SUB * count + row - first, size, stride=count), :] = value[:size]

    def spread(slot, row):
        lanes = pl.ds(slot * nz, nz)
        local_row = row - low_row
        factors = [
            [jnp.broadcast_to(coef[f * terms + k, pl.ds(local_row, 1), :], (SUB, nz)) for k in range(terms)]
            for f in range(FACES)
        ]
        inside = jnp.logical_and(row >= first, row < first + count)
        for block in range(pl.cdiv(mode_dev, SUB)):
            size = min(SUB, mode_dev - block * SUB)
            here = pl.ds(block * SUB, SUB)
            totals = [None] * FACES
            for k in range(terms):
                if k == terms - 1:
                    value = cells[slot, 0, here, :]
                else:
                    value = mixed[pl.ds(k * pad + block * SUB, SUB), lanes]
                for f in range(FACES):
                    part = factors[f][k] * value
                    totals[f] = part if totals[f] is None else totals[f] + part
            up, down, north, south, east, west = totals
            before = pending[here, :] - south

            @pl.when(row > first)
            def _():
                finish(row - 1, block, before)

            @pl.when(inside)
            def _():
                at = pl.ds(block * SUB * count + row - first, size, stride=count)
                to_up[at, :] = -up[:size]
                to_down[at, :] = -down[:size]

            moved_east = jnp.where(lane > 0, pltpu.roll(east, 1, 1), 0.0)
            moved_west = jnp.where(lane < nz - 1, pltpu.roll(west, nz - 1, 1), 0.0)
            total = ((up + down) + (north + south)) + ((east - moved_east) + (west - moved_west))
            pending[here, :] = total - above[here, :]
            above[here, :] = north

    def process(row, number, source):
        for slot in range(number):
            fill(slot, row + slot, source)
        span = number * nz
        mixed[:, 0:span] = jnp.dot(
            weights[...], stack[:, 0:span], preferred_element_type=jnp.float32
        )
        for slot in range(number):
            spread(slot, row + slot)

    at_row = low_row
    for index, (start, length) in enumerate(sources):
        source = (start, length, index)
        end = min(start + length, last + 1)
        pairs = (end - at_row) // 2

        def body(step, carry, source=source, base=at_row):
            process(base + 2 * step, 2, source)
            return carry

        lax.fori_loop(0, pairs, body, 0)
        if (end - at_row) % 2:
            process(jnp.int32(end - 1), 1, source)
        at_row = end
    if first + count == rows:
        for block in range(pl.cdiv(mode_dev, SUB)):
            finish(rows - 1, block, pending[pl.ds(block * SUB, SUB), :])


def partial_kernel(first, count, rows, mode_dev, pad, groups, *refs):
    own, up, down, perm, perm_up, perm_down, weights, out = refs[:8]
    sends = refs[8 : 8 + groups - 1]
    coef, near, high, low = refs[8 + groups - 1 :]
    terms = perm.shape[0]
    nz = own.shape[1]
    face_coefs(coef, perm, perm_up, perm_down, first, count)
    near[...] = jnp.zeros_like(near)
    lane = lax.broadcasted_iota(jnp.int32, (PACK, nz), 1)
    wide = groups * pad

    def process(row, number):
        for slot in range(number + 2):
            at = row + slot - 1
            value = strided_rows(own, jnp.clip(at, 0, rows - 1), mode_dev, rows)
            near[slot, :mode_dev, :] = jnp.where(jnp.logical_and(at >= 0, at < rows), value, 0.0)
        mean_parts = []
        for slot in range(number):
            lanes = pl.ds(slot * nz, nz)
            local_row = row + slot - first
            near[4, :mode_dev, :] = strided_rows(up, local_row, mode_dev, count)
            near[5, :mode_dev, :] = strided_rows(down, local_row, mode_dev, count)
            factors = [
                [jnp.broadcast_to(coef[f * terms + k, pl.ds(local_row, 1), :], (SUB, nz)) for k in range(terms)]
                for f in range(FACES)
            ]
            factors = [[jnp.concatenate([x, x], 0) for x in line] for line in factors]
            blocks = []
            for block in range(pad // PACK):
                here = pl.ds(block * PACK, PACK)
                centre = near[slot + 1, here, :]
                others = (
                    near[4, here, :],
                    near[5, here, :],
                    near[slot + 2, here, :],
                    near[slot, here, :],
                    jnp.where(lane < nz - 1, pltpu.roll(centre, nz - 1, 1), 0.0),
                    jnp.where(lane > 0, pltpu.roll(centre, 1, 1), 0.0),
                )
                steps = [centre - other for other in others]
                for k in range(terms):
                    total = factors[0][k] * steps[0]
                    for f in range(1, FACES):
                        total = total + factors[f][k] * steps[f]
                    if k == terms - 1:
                        blocks.append(total)
                    else:
                        place = pl.ds(k * pad + block * PACK, PACK)
                        high[place, lanes], low[place, lanes] = halves(total)
            mean_parts.append(blocks)
        span = number * nz
        both = jnp.dot(weights[...], high[:, 0:span], preferred_element_type=jnp.float32)
        rest = jnp.dot(weights[0:wide, :], low[:, 0:span], preferred_element_type=jnp.float32)
        result = both[0:wide] + both[wide : 2 * wide] + rest
        for slot in range(number):
            local_row = row + slot - first
            lanes = slice(slot * nz, (slot + 1) * nz)
            mean_part = jnp.concatenate(mean_parts[slot], 0)
            for s in range(groups):
                target = out if s == 0 else sends[s - 1]
                value = result[s * pad : (s + 1) * pad, lanes]
                if s == 0:
                    value = value + mean_part
                target[pl.ds(local_row, mode_dev, stride=count), :] = value[:mode_dev]

    def body(step, carry):
        process(first + 2 * step, 2)
        return carry

    lax.fori_loop(0, count // 2, body, 0)


def sum_kernel(*refs):
    *parts, out = refs
    total = parts[0][...]
    for part in parts[1:]:
        total = total + part[...]
    out[...] = total


def place_sum(result, parts, first, shape):
    modes, count, nz = parts[0].shape
    kept = [] if result is None else [result]

    def kernel(*refs):
        sum_kernel(*refs[len(kept) :])

    return pl.pallas_call(
        kernel,
        grid=(count // SUB,),
        in_specs=[pl.BlockSpec(memory_space=pl.ANY)] * len(kept)
        + [pl.BlockSpec((modes, SUB, nz), lambda i: (0, i, 0))] * len(parts),
        out_specs=pl.BlockSpec((modes, SUB, nz), lambda i: (0, i + first // SUB, 0)),
        out_shape=jax.ShapeDtypeStruct(shape, jnp.float32),
        input_output_aliases={0: 0} if kept else {},
    )(*kept, *parts)


def local(mode_coeffs, mean_perm, kl_fields, couplings):
    mode_dev, _, rows, nz = mode_coeffs.shape
    terms = kl_fields.shape[0] + 1
    groups = lax.axis_size("modes")
    planes = lax.axis_size("space")
    pad = pl.cdiv(mode_dev, PACK) * PACK
    group = lax.axis_index("modes")
    forward = [(i, i + 1) for i in range(planes - 1)]
    backward = [(target, source) for source, target in forward]
    own3 = mode_coeffs.reshape(mode_dev, rows, nz)
    own = own3.reshape(mode_dev * rows, nz)

    def rotated(value, step):
        return lax.ppermute(value, "modes", [(i, (i + step) % groups) for i in range(groups)])

    def widened(value):
        return jnp.pad(value, ((0, 0), (SUB, SUB), (0, 0)))

    def block(row_group, column_group):
        piece = lax.dynamic_slice(
            couplings,
            (0, (row_group % groups) * mode_dev, (column_group % groups) * mode_dev),
            (terms - 1, mode_dev, mode_dev),
        )
        return jnp.pad(piece, ((0, 0), (0, pad - mode_dev), (0, pad - mode_dev)))

    def split(value):
        high = lax.reduce_precision(value, 8, 7)
        return high.astype(jnp.bfloat16), (value - high).astype(jnp.bfloat16)

    cut = 64
    gathered = [(0, 32), (32, 32)]
    partial = [(64, 32), (96, 24)]

    perm = jnp.concatenate([kl_fields, mean_perm[None]], 0).reshape(terms, rows, nz)
    perm_down = widened(lax.ppermute(perm, "space", forward))
    perm_up = widened(lax.ppermute(perm, "space", backward))
    perm = widened(perm)

    received, bounds, low_row = [], [], 0
    for first, count in gathered:
        high_row = min(first + count + 1, rows)
        piece = own3[:, low_row:high_row].reshape(mode_dev * (high_row - low_row), nz)
        received.append([rotated(piece, s) for s in range(1, groups)])
        bounds.append((low_row, high_row - low_row))
        low_row = high_row
    halos = []
    for first, count in partial:
        piece = own3[:, first : first + count]
        halos.append((lax.ppermute(piece, "space", backward), lax.ppermute(piece, "space", forward)))

    high, low = split(jnp.concatenate([block(group, group - s) for s in range(groups)], 2))
    gathered_weights = jnp.concatenate([high, high, low], 2).reshape((terms - 1) * pad, 3 * groups * pad)
    high, low = split(jnp.concatenate([block(group + s, group) for s in range(groups)], 1))
    partial_weights = (
        jnp.concatenate([high, low], 1).transpose(1, 0, 2).reshape(2 * groups * pad, (terms - 1) * pad)
    )

    params = pltpu.CompilerParams(vmem_limit_bytes=LIMIT)
    f32 = jnp.float32
    result = None
    shape = (mode_dev, rows, nz)

    shares = []
    for (first, count), (up, down) in zip(partial, halos):
        flat = jax.ShapeDtypeStruct((mode_dev * count, nz), f32)
        outs = pl.pallas_call(
            functools.partial(partial_kernel, first, count, rows, mode_dev, pad, groups),
            in_specs=[VMEM] * 7,
            out_specs=[VMEM] * groups,
            out_shape=[flat] * groups,
            scratch_shapes=[
                pltpu.VMEM((FACES * terms, count, nz), f32),
                pltpu.VMEM((6, pad, nz), f32),
                pltpu.VMEM(((terms - 1) * pad, 2 * nz), jnp.bfloat16),
                pltpu.VMEM(((terms - 1) * pad, 2 * nz), jnp.bfloat16),
            ],
            compiler_params=params,
            name="partial",
        )(own, up.reshape(mode_dev * count, nz), down.reshape(mode_dev * count, nz), perm, perm_up, perm_down, partial_weights)
        parts = [outs[0]] + [rotated(value, s) for s, value in enumerate(outs[1:], 1)]
        shares.append((first, [part.reshape(mode_dev, count, nz) for part in parts]))

    for index, (first, count) in enumerate(gathered):
        begin = max(index - 1, 0)
        sources = bounds[begin : index + 1]
        pieces = [piece for group_pieces in received[begin : index + 1] for piece in group_pieces]
        flat = jax.ShapeDtypeStruct((mode_dev * count, nz), f32)
        centre, to_up, to_down = pl.pallas_call(
            functools.partial(
                gathered_kernel, first, count, rows, mode_dev, pad, groups, sources
            ),
            in_specs=[VMEM] * (5 + len(pieces)),
            out_specs=[VMEM] * 3,
            out_shape=[flat] * 3,
            scratch_shapes=[
                pltpu.VMEM((FACES * terms, count + SUB, nz), f32),
                pltpu.VMEM((2, groups, pad, nz), f32),
                pltpu.VMEM((3 * groups * pad, 2 * nz), jnp.bfloat16),
                pltpu.VMEM(((terms - 1) * pad, 2 * nz), f32),
                pltpu.VMEM((pad, nz), f32),
                pltpu.VMEM((pad, nz), f32),
            ],
            compiler_params=params,
            name="gathered",
        )(own, perm, perm_up, perm_down, gathered_weights, *pieces)
        parts = [centre, lax.ppermute(to_up, "space", forward), lax.ppermute(to_down, "space", backward)]
        shares.append((first, [part.reshape(mode_dev, count, nz) for part in parts]))

    for first, parts in shares:
        result = place_sum(result, parts, first, shape)
    return result.reshape(mode_coeffs.shape)


def solution(mesh):
    in_specs = (
        P("modes", "space", None, None),
        P("space", None, None),
        P(None, "space", None, None),
        P(),
    )
    out_specs = P("modes", "space", None, None)
    return jax.shard_map(local, mesh=mesh, in_specs=in_specs, out_specs=out_specs, check_vma=False)
```

time: 1090 us -> 186 us (0.17)
  waiting for transfers between devices: 728 us -> 34 us
  other arithmetic: 220 us -> 1.19 us
  Pallas kernels: 0 us -> 99 us
  local copies, waits for them, and re-layouts: 93 us -> 17.1 us
  matrix products: 24.9 us -> 0 us
  starting transfers between devices: 11.3 us -> 33 us
  between operations: 13.5 us -> 0.27 us
    ppermute x4 -> x14, waiting for transfers between devices: 637 us -> 34 us  [the longest x1 20.4 us: local(): perm_down = widened(lax.ppermute(perm, 'space', forward))]
    concatenate x3 -> x2, other arithmetic: 116 us -> 0.07 us  [the longest x1 0.04 us: local(): jnp.concatenate([high, high, low], 2)]
    pallas_call x0 -> x8, Pallas kernels: none -> 99 us  [the longest x2 60.4 us: local(): pl.pallas_call(functools.partial(gathered_kernel, first, count, rows, mod...]
    reduce_sum x1 -> x0, other arithmetic: 95.8 us -> none  [local(): return jnp.sum(operate(field_pad, perm_pad), axis=0)]
    all_gather x1 -> x0, waiting for transfers between devices: 90.5 us -> none  [local(): block_piece = lax.all_gather(mode_coeffs, 'modes', axis=0, tiled=True)]
    ppermute x2 -> x0, local copies, waits for them, and re-layouts: 37.9 us -> none  [the longest x1 25.7 us: extended(): lax.ppermute(lax.slice_in_dim(block, 0, width, axis=dim), axis, backward)]
    concatenate x1 -> x0, local copies, waits for them, and re-layouts: 29 us -> none  [local(): jnp.concatenate([mode_coeffs[None], mixed_modes.reshape((term_count - 1,...]
    dot_general x1 -> x0, matrix products: 24.9 us -> none  [local(): jnp.einsum('kin,nc->kic', own_rows, flat_piece, precision=lax.Precision.H...]
  transfers between devices with their start and end apart: 5 -> 14, of which waited for: 3 -> 2; matrix products, arithmetic and copies ran while one was open for 2% -> 6% of each run, Pallas kernels for 0% -> 52%
where the time goes in v1:
time: 186 us; the launch traced here: 184 us
  Pallas kernels  99 us (53%)
  waiting for transfers between devices  34 us (18%)
  starting transfers between devices  33 us (18%)
  local copies, waits for them, and re-layouts  17.1 us (9%)
    pallas_call x2, Pallas kernels, local(): pl.pallas_call(functools.partial(gathered_kernel, first, count, rows, mod...  60.4 us
    pallas_call x2, Pallas kernels, local(): pl.pallas_call(functools.partial(partial_kernel, first, count, rows, mode...  24.2 us
    ppermute x1, waiting for transfers between devices, local(): perm_down = widened(lax.ppermute(perm, 'space', forward))  20.4 us
    pallas_call x4, Pallas kernels, place_sum(): pl.pallas_call(kernel, grid=(count // SUB,), in_specs=[pl.BlockSpec(memor...  14.4 us
    ppermute x4, waiting for transfers between devices, rotated(): lax.ppermute(value, 'modes', [(i, (i + step) % groups) for i in range(gro...  13.5 us
    ppermute x2, starting transfers between devices, local(): lax.ppermute(piece, 'space', forward)  8.66 us
    ppermute x2, starting transfers between devices, local(): lax.ppermute(to_up, 'space', forward)  7.23 us
    slice x2, local copies, waits for them, and re-layouts, local(): own3[:, low_row:high_row].reshape(mode_dev * (high_row - low_row), nz)  4.63 us
  transfers between devices with their start and end apart: 14, of which 2 were waited for; matrix products, arithmetic and copies ran while one was open for 6% of the time, Pallas kernels for 52%

profile of v1, /device:TPU:17, one launch (start us, length us, event | category | flops | bytes accessed | tf_op | source)
XLA Modules:
  0.0 184.5 jit_solution(5640063236877420205)
XLA Ops:
  0.0 3.2 %fusion.2 = (f32[60,32,128]{2,1,0:T(8,128)}, f32[60,32,128]{2,1,0:T(8,128)}) fusion(f32[60,120,128]{2,1,0:T(8,128)} %bitcast.33), kind=kLoop, calls=%fused_computation.15 | loop fusion | bytes 3932160 | tf_op jit(solution)/shard_map/slice | solution.py:284
  3.3 3.8 %collective-permute-start.1 = (f32[60,32,128]{2,1,0:T(8,128)}, f32[60,32,128]{2,1,0:T(8,128)}, u32[]{:S(2)}, u32[]{:S(2)}) collective-permute-start(f32[60,32,128]{2,1,0:T(8,128)} %get-tuple-element.26), channel_id=1, source_target_pairs={{0,1},{1,2},{2,3},{3,4},{4,5},{5,6},{6,7},{7,8},{8,9},{9,10},{10,1... | collective-permute-start | bytes 2949128 | tf_op jit(solution)/shard_map/ppermute | solution.py:291
  7.1 1.9 %collective-permute-start = (f32[60,32,128]{2,1,0:T(8,128)}, f32[60,32,128]{2,1,0:T(8,128)}, u32[]{:S(2)}, u32[]{:S(2)}) collective-permute-start(f32[60,32,128]{2,1,0:T(8,128)} %get-tuple-element.26), channel_id=1, source_target_pairs={{1,0},{2,1},{3,2},{4,3},{5,4},{6,5},{7,6},{8,7},{9,8},{10,9},{11,1... | collective-permute-start | bytes 2949128 | tf_op jit(solution)/shard_map/ppermute | solution.py:291
  9.9 3.6 %collective-permute-start.3 = (f32[8,120,128]{2,1,0:T(8,128)}, f32[8,120,128]{2,1,0:T(8,128)S(1)}, u32[]{:S(2)}, u32[]{:S(2)}) collective-permute-start(f32[8,120,128]{2,1,0:T(8,128)} %maximum_bitcast_fusion), channel_id=1, source_target_pairs={{0,1},{1,2},{2,3},{3,4},{4,5},{5,6},{6,7},{7,8},{8,9},{9,10},{10,1... | collective-permute-start | bytes 1474568 | tf_op jit(solution)/shard_map/ppermute | solution.py:277
  13.5 1.9 %collective-permute-start.2 = (f32[8,120,128]{2,1,0:T(8,128)}, f32[8,120,128]{2,1,0:T(8,128)}, u32[]{:S(2)}, u32[]{:S(2)}) collective-permute-start(f32[8,120,128]{2,1,0:T(8,128)} %maximum_bitcast_fusion), channel_id=1, source_target_pairs={{1,0},{2,1},{3,2},{4,3},{5,4},{6,5},{7,6},{8,7},{9,8},{10,9},{11,1... | collective-permute-start | bytes 1474568 | tf_op jit(solution)/shard_map/ppermute | solution.py:278
  15.5 1.4 slice.18
  19.1 20.4 %collective-permute-done.3 = f32[8,120,128]{2,1,0:T(8,128)S(1)} collective-permute-done((f32[8,120,128]{2,1,0:T(8,128)}, f32[8,120,128]{2,1,0:T(8,128)S(1)}, u32[]{:S(2)}, u32[]{:S(2)}) %collective-permute-start.3) | collective-permute-done | bytes 491552 | tf_op jit(solution)/shard_map/ppermute | solution.py:277
  45.6 14.8 %partial.2 = (f32[1920,128]{1,0:T(8,128)S(1)}, f32[1920,128]{1,0:T(8,128)}) custom-call(f32[7200,128]{1,0:T(8,128)} %bitcast.35, f32[1920,128]{1,0:T(8,128)} %bitcast.2.refs_1_, f32[1920,128]{1,0:T(8,128)} %bitcast.3.refs_2_, f32[8,136,128]{2,1,0:T(8,128)S(1)} %pad.21.refs_3_.refs_1_, f32[8,136,128]{2,1,0:T(8,128)S(1)} %pad.22.refs_4_.refs_2_, ...), custom_call_target="tpu_custom_call" | custom-call | tf_op jit(solution)/shard_map/partial/pallas_call | solution.py:308
  61.5 2.0 %slice.17 = f32[60,24,128]{2,1,0:T(8,128)} slice(f32[60,120,128]{2,1,0:T(8,128)} %bitcast.36), slice={[0:60], [96:120], [0:128]} | slice | bytes 1474560 | tf_op jit(solution)/shard_map/slice | solution.py:290
  63.6 4.8 %collective-permute-start.6 = (f32[60,24,128]{2,1,0:T(8,128)}, f32[60,24,128]{2,1,0:T(8,128)}, u32[]{:S(2)}, u32[]{:S(2)}) collective-permute-start(f32[60,24,128]{2,1,0:T(8,128)} %slice.17), channel_id=1, source_target_pairs={{0,1},{1,2},{2,3},{3,4},{4,5},{5,6},{6,7},{7,8},{8,9},{9,10},{10,1... | collective-permute-start | bytes 2211848 | tf_op jit(solution)/shard_map/ppermute | solution.py:291
  68.4 1.9 %collective-permute-start.5 = (f32[60,24,128]{2,1,0:T(8,128)}, f32[60,24,128]{2,1,0:T(8,128)}, u32[]{:S(2)}, u32[]{:S(2)}) collective-permute-start(f32[60,24,128]{2,1,0:T(8,128)} %slice.17), channel_id=1, source_target_pairs={{1,0},{2,1},{3,2},{4,3},{5,4},{6,5},{7,6},{8,7},{9,8},{10,9},{11,1... | collective-permute-start | bytes 2211848 | tf_op jit(solution)/shard_map/ppermute | solution.py:291
  71.7 29.7 %gathered.2 = (f32[1920,128]{1,0:T(8,128)S(1)}, f32[1920,128]{1,0:T(8,128)}, f32[1920,128]{1,0:T(8,128)}) custom-call(f32[7200,128]{1,0:T(8,128)} %bitcast.37, f32[8,136,128]{2,1,0:T(8,128)S(1)} %pad.21.refs_3_.refs_1_, f32[8,136,128]{2,1,0:T(8,128)S(1)} %pad.22.refs_4_.refs_2_, f32[8,136,128]{2,1,0:T(8,128)S(1)} %pad.23.refs_5_.refs_3_, ...), custom_call_target="tpu_custom_call" | custom-call | tf_op jit(solution)/shard_map/gathered/pallas_call | solution.py:330
  101.3 3.6 %collective-permute-start.9 = (f32[1920,128]{1,0:T(8,128)}, f32[1920,128]{1,0:T(8,128)}, u32[]{:S(2)}, u32[]{:S(2)}) collective-permute-start(f32[1920,128]{1,0:T(8,128)} %get-tuple-element.20), channel_id=1, source_target_pairs={{0,1},{1,2},{2,3},{3,4},{4,5},{5,6},{6,7},{7,8},{8,9},{9,10},{10,1... | collective-permute-start | bytes 2949128 | tf_op jit(solution)/shard_map/ppermute | solution.py:348
  105.0 1.9 %collective-permute-start.10 = (f32[1920,128]{1,0:T(8,128)}, f32[1920,128]{1,0:T(8,128)}, u32[]{:S(2)}, u32[]{:S(2)}) collective-permute-start(f32[1920,128]{1,0:T(8,128)} %get-tuple-element.21), channel_id=1, source_target_pairs={{1,0},{2,1},{3,2},{4,3},{5,4},{6,5},{7,6},{8,7},{9,8},{10,9},{11,1... | collective-permute-start | bytes 2949128 | tf_op jit(solution)/shard_map/ppermute | solution.py:348
  106.9 30.7 %gathered.3 = (f32[1920,128]{1,0:T(8,128)S(1)}, f32[1920,128]{1,0:T(8,128)}, f32[1920,128]{1,0:T(8,128)}) custom-call(f32[7200,128]{1,0:T(8,128)} %bitcast.38, f32[8,136,128]{2,1,0:T(8,128)S(1)} %pad.21.refs_3_.refs_1_, f32[8,136,128]{2,1,0:T(8,128)S(1)} %pad.22.refs_4_.refs_2_, f32[8,136,128]{2,1,0:T(8,128)S(1)} %pad.23.refs_5_.refs_3_, ...), custom_call_target="tpu_custom_call" | custom-call | tf_op jit(solution)/shard_map/gathered/pallas_call | solution.py:330
  138.6 3.6 %collective-permute-start.12 = (f32[1920,128]{1,0:T(8,128)}, f32[1920,128]{1,0:T(8,128)}, u32[]{:S(2)}, u32[]{:S(2)}) collective-permute-start(f32[1920,128]{1,0:T(8,128)} %get-tuple-element.23), channel_id=1, source_target_pairs={{0,1},{1,2},{2,3},{3,4},{4,5},{5,6},{6,7},{7,8},{8,9},{9,10},{10,1... | collective-permute-start | bytes 2949128 | tf_op jit(solution)/shard_map/ppermute | solution.py:348
  142.3 1.9 %collective-permute-start.13 = (f32[1920,128]{1,0:T(8,128)}, f32[1920,128]{1,0:T(8,128)}, u32[]{:S(2)}, u32[]{:S(2)}) collective-permute-start(f32[1920,128]{1,0:T(8,128)} %get-tuple-element.24), channel_id=1, source_target_pairs={{1,0},{2,1},{3,2},{4,3},{5,4},{6,5},{7,6},{8,7},{9,8},{10,9},{11,1... | collective-permute-start | bytes 2949128 | tf_op jit(solution)/shard_map/ppermute | solution.py:348
  144.2 9.4 %partial.3 = (f32[1440,128]{1,0:T(8,128)S(1)}, f32[1440,128]{1,0:T(8,128)S(1)}) custom-call(f32[7200,128]{1,0:T(8,128)} %bitcast.39, f32[1440,128]{1,0:T(8,128)} %bitcast.11.refs_1_, f32[1440,128]{1,0:T(8,128)} %bitcast.12.refs_2_, f32[8,136,128]{2,1,0:T(8,128)S(1)} %pad.21.refs_3_.refs_1_, f32[8,136,128]{2,1,0:T(8,128)S(1)} %pad.22.refs_4_.refs_2_, ...), custom_call_target="tpu_custom_call" | custom-call | tf_op jit(solution)/shard_map/partial/pallas_call | solution.py:308
  154.5 1.2 collective-permute-start.7
  155.7 3.6 %shard_map.46.refs_0_ = f32[60,120,128]{2,1,0:T(8,128)} custom-call(f32[60,32,128]{2,1,0:T(8,128)} %bitcast.29, f32[60,32,128]{2,1,0:T(8,128)} %bitcast.10.refs_1_), custom_call_target="tpu_custom_call" | custom-call | tf_op jit(solution)/shard_map/pallas_call | solution.py:231
  159.3 13.5 %collective-permute-done.7 = f32[1440,128]{1,0:T(8,128)S(1)} collective-permute-done((f32[1440,128]{1,0:T(8,128)S(1)}, f32[1440,128]{1,0:T(8,128)S(1)}, u32[]{:S(2)}, u32[]{:S(2)}) %collective-permute-start.7) | collective-permute-done | bytes 737312 | tf_op jit(solution)/shard_map/ppermute | solution.py:255
  173.7 3.1 %shard_map.47.refs_0_ = f32[60,120,128]{2,1,0:T(8,128)} custom-call(f32[60,120,128]{2,1,0:T(8,128)} %shard_map.46.refs_0_, f32[60,24,128]{2,1,0:T(8,128)} %bitcast.32, f32[60,24,128]{2,1,0:T(8,128)} %bitcast.44), custom_call_target="tpu_custom_call", output_to_operand_aliasing={{}: (0, {})} | custom-call | tf_op jit(solution)/shard_map/pallas_call | solution.py:231
  176.8 3.8 %shard_map.48.refs_0_ = f32[60,120,128]{2,1,0:T(8,128)} custom-call(f32[60,120,128]{2,1,0:T(8,128)} %shard_map.47.refs_0_, f32[60,32,128]{2,1,0:T(8,128)} %bitcast.30, f32[60,32,128]{2,1,0:T(8,128)} %bitcast.18.refs_2_, f32[60,32,128]{2,1,0:T(8,128)} %bitcast.19.refs_3_), custom_call_target="tpu_custom_call", output_to_operand_aliasing={{}: (0, {})} | custom-call | tf_op jit(solution)/shard_map/pallas_call | solution.py:231
  180.7 3.8 %shard_map.49 = f32[60,120,128]{2,1,0:T(8,128)} custom-call(f32[60,120,128]{2,1,0:T(8,128)} %shard_map.48.refs_0_, f32[60,32,128]{2,1,0:T(8,128)} %bitcast.31, f32[60,32,128]{2,1,0:T(8,128)} %bitcast.22.refs_2_, f32[60,32,128]{2,1,0:T(8,128)} %bitcast.23.refs_3_), custom_call_target="tpu_custom_call", output_to_operand_aliasing={{}: (0, {})} | custom-call | tf_op jit(solution)/shard_map/pallas_call | solution.py:231
  (51 shorter events, 14.3 us)
Async XLA Ops:
  0.0 9.0 %copy-start.8 = (f32[7,1,120,128]{3,2,1,0:T(8,128)S(1)}, f32[7,1,120,128]{3,2,1,0:T(8,128)}, u32[]{:S(2)}) copy-start(f32[7,1,120,128]{3,2,1,0:T(8,128)} %param.6) | copy-start | bytes 1290244
  0.0 9.0 %copy-start.9 = (f32[1,120,128]{2,1,0:T(8,128)S(1)}, f32[1,120,128]{2,1,0:T(8,128)}, u32[]{:S(2)}) copy-start(f32[1,120,128]{2,1,0:T(8,128)} %param.5) | copy-start | bytes 184324
  3.3 37.5 %copy-start.5 = (f32[7,120,120]{2,1,0:T(8,128)S(1)}, f32[7,120,120]{2,1,0:T(8,128)}, u32[]{:S(2)}) copy-start(f32[7,120,120]{2,1,0:T(8,128)} %param.7) | copy-start | bytes 1209604
  3.3 42.3 %collective-permute-start.1 = (f32[60,32,128]{2,1,0:T(8,128)}, f32[60,32,128]{2,1,0:T(8,128)}, u32[]{:S(2)}, u32[]{:S(2)}) collective-permute-start(f32[60,32,128]{2,1,0:T(8,128)} %get-tuple-element.26), channel_id=1, source_target_pairs={{0,1},{1,2},{2,3},{3,4},{4,5},{5,6},{6,7},{7,8},{8,9},{9,10},{10,1... | collective-permute-start | bytes 2949128 | tf_op jit(solution)/shard_map/ppermute | solution.py:291
  7.1 38.5 %collective-permute-start = (f32[60,32,128]{2,1,0:T(8,128)}, f32[60,32,128]{2,1,0:T(8,128)}, u32[]{:S(2)}, u32[]{:S(2)}) collective-permute-start(f32[60,32,128]{2,1,0:T(8,128)} %get-tuple-element.26), channel_id=1, source_target_pairs={{1,0},{2,1},{3,2},{4,3},{5,4},{6,5},{7,6},{8,7},{9,8},{10,9},{11,1... | collective-permute-start | bytes 2949128 | tf_op jit(solution)/shard_map/ppermute | solution.py:291
  9.9 29.6 %collective-permute-start.3 = (f32[8,120,128]{2,1,0:T(8,128)}, f32[8,120,128]{2,1,0:T(8,128)S(1)}, u32[]{:S(2)}, u32[]{:S(2)}) collective-permute-start(f32[8,120,128]{2,1,0:T(8,128)} %maximum_bitcast_fusion), channel_id=1, source_target_pairs={{0,1},{1,2},{2,3},{3,4},{4,5},{5,6},{6,7},{7,8},{8,9},{9,10},{10,1... | collective-permute-start | bytes 1474568 | tf_op jit(solution)/shard_map/ppermute | solution.py:277
  13.5 31.0 %collective-permute-start.2 = (f32[8,120,128]{2,1,0:T(8,128)}, f32[8,120,128]{2,1,0:T(8,128)}, u32[]{:S(2)}, u32[]{:S(2)}) collective-permute-start(f32[8,120,128]{2,1,0:T(8,128)} %maximum_bitcast_fusion), channel_id=1, source_target_pairs={{1,0},{2,1},{3,2},{4,3},{5,4},{6,5},{7,6},{8,7},{9,8},{10,9},{11,1... | collective-permute-start | bytes 1474568 | tf_op jit(solution)/shard_map/ppermute | solution.py:278
  17.9 53.8 %collective-permute-start.8 = (f32[1980,128]{1,0:T(8,128)}, f32[1980,128]{1,0:T(8,128)S(1)}, u32[]{:S(2)}, u32[]{:S(2)}) collective-permute-start(f32[1980,128]{1,0:T(8,128)} %reshape.81), channel_id=1, source_target_pairs={{0,16},{16,0},{1,17},{17,1},{2,18},{18,2},{3,19},{19,3},{4,20},{20... | collective-permute-start | bytes 3041288 | tf_op jit(solution)/shard_map/ppermute | solution.py:255
  39.5 3.2 %copy-start.7 = (f32[8,120,128]{2,1,0:T(8,128)}, f32[8,120,128]{2,1,0:T(8,128)S(1)}, u32[]{:S(2)}) copy-start(f32[8,120,128]{2,1,0:T(8,128)S(1)} %collective-permute-done.3) | copy-start | bytes 1474564
  39.5 65.5 %collective-permute-start.11 = (f32[1920,128]{1,0:T(8,128)}, f32[1920,128]{1,0:T(8,128)}, u32[]{:S(2)}, u32[]{:S(2)}) collective-permute-start(f32[1920,128]{1,0:T(8,128)} %bitcast.40), channel_id=1, source_target_pairs={{0,16},{16,0},{1,17},{17,1},{2,18},{18,2},{3,19},{19,3},{4,20},{20... | collective-permute-start | bytes 2949128 | tf_op jit(solution)/shard_map/ppermute | solution.py:255
  60.4 0.9 copy-start.1
  61.3 93.2 %collective-permute-start.4 = (f32[1920,128]{1,0:T(8,128)}, f32[1920,128]{1,0:T(8,128)}, u32[]{:S(2)}, u32[]{:S(2)}) collective-permute-start(f32[1920,128]{1,0:T(8,128)} %get-tuple-element.16), channel_id=1, source_target_pairs={{0,16},{16,0},{1,17},{17,1},{2,18},{18,2},{3,19},{19,3},{4,20},{20... | collective-permute-start | bytes 2949128 | tf_op jit(solution)/shard_map/ppermute | solution.py:255
  63.6 75.0 %collective-permute-start.6 = (f32[60,24,128]{2,1,0:T(8,128)}, f32[60,24,128]{2,1,0:T(8,128)}, u32[]{:S(2)}, u32[]{:S(2)}) collective-permute-start(f32[60,24,128]{2,1,0:T(8,128)} %slice.17), channel_id=1, source_target_pairs={{0,1},{1,2},{2,3},{3,4},{4,5},{5,6},{6,7},{7,8},{8,9},{9,10},{10,1... | collective-permute-start | bytes 2211848 | tf_op jit(solution)/shard_map/ppermute | solution.py:291
  68.4 73.8 %collective-permute-start.5 = (f32[60,24,128]{2,1,0:T(8,128)}, f32[60,24,128]{2,1,0:T(8,128)}, u32[]{:S(2)}, u32[]{:S(2)}) collective-permute-start(f32[60,24,128]{2,1,0:T(8,128)} %slice.17), channel_id=1, source_target_pairs={{1,0},{2,1},{3,2},{4,3},{5,4},{6,5},{7,6},{8,7},{9,8},{10,9},{11,1... | collective-permute-start | bytes 2211848 | tf_op jit(solution)/shard_map/ppermute | solution.py:291
  71.7 35.3 %copy-start = (f32[1980,128]{1,0:T(8,128)}, f32[1980,128]{1,0:T(8,128)S(1)}, u32[]{:S(2)}) copy-start(f32[1980,128]{1,0:T(8,128)S(1)} %collective-permute-done.8.refs_5_) | copy-start | bytes 3041284
  101.3 36.3 %copy-start.2 = (f32[1920,128]{1,0:T(8,128)}, f32[1920,128]{1,0:T(8,128)S(1)}, u32[]{:S(2)}) copy-start(f32[1920,128]{1,0:T(8,128)S(1)} %get-tuple-element.19) | copy-start | bytes 2949124
  101.3 75.5 %collective-permute-start.9 = (f32[1920,128]{1,0:T(8,128)}, f32[1920,128]{1,0:T(8,128)}, u32[]{:S(2)}, u32[]{:S(2)}) collective-permute-start(f32[1920,128]{1,0:T(8,128)} %get-tuple-element.20), channel_id=1, source_target_pairs={{0,1},{1,2},{2,3},{3,4},{4,5},{5,6},{6,7},{7,8},{8,9},{9,10},{10,1... | collective-permute-start | bytes 2949128 | tf_op jit(solution)/shard_map/ppermute | solution.py:348
  105.0 71.8 %collective-permute-start.10 = (f32[1920,128]{1,0:T(8,128)}, f32[1920,128]{1,0:T(8,128)}, u32[]{:S(2)}, u32[]{:S(2)}) collective-permute-start(f32[1920,128]{1,0:T(8,128)} %get-tuple-element.21), channel_id=1, source_target_pairs={{1,0},{2,1},{3,2},{4,3},{5,4},{6,5},{7,6},{8,7},{9,8},{10,9},{11,1... | collective-permute-start | bytes 2949128 | tf_op jit(solution)/shard_map/ppermute | solution.py:348
  137.7 1.0 copy-start.3
  138.6 42.0 %collective-permute-start.12 = (f32[1920,128]{1,0:T(8,128)}, f32[1920,128]{1,0:T(8,128)}, u32[]{:S(2)}, u32[]{:S(2)}) collective-permute-start(f32[1920,128]{1,0:T(8,128)} %get-tuple-element.23), channel_id=1, source_target_pairs={{0,1},{1,2},{2,3},{3,4},{4,5},{5,6},{6,7},{7,8},{8,9},{9,10},{10,1... | collective-permute-start | bytes 2949128 | tf_op jit(solution)/shard_map/ppermute | solution.py:348
  142.3 38.4 %collective-permute-start.13 = (f32[1920,128]{1,0:T(8,128)}, f32[1920,128]{1,0:T(8,128)}, u32[]{:S(2)}, u32[]{:S(2)}) collective-permute-start(f32[1920,128]{1,0:T(8,128)} %get-tuple-element.24), channel_id=1, source_target_pairs={{1,0},{2,1},{3,2},{4,3},{5,4},{6,5},{7,6},{8,7},{9,8},{10,9},{11,1... | collective-permute-start | bytes 2949128 | tf_op jit(solution)/shard_map/ppermute | solution.py:348
  153.6 0.9 copy-start.4
  154.5 18.4 %collective-permute-start.7 = (f32[1440,128]{1,0:T(8,128)S(1)}, f32[1440,128]{1,0:T(8,128)S(1)}, u32[]{:S(2)}, u32[]{:S(2)}) collective-permute-start(f32[1440,128]{1,0:T(8,128)S(1)} %get-tuple-element.18), channel_id=1, source_target_pairs={{0,16},{16,0},{1,17},{17,1},{2,18},{18,2},{3,19},{19,3},{4,20},{20... | collective-permute-start | bytes 2211848 | tf_op jit(solution)/shard_map/ppermute | solution.py:255
  172.8 0.9 copy-start.6

commit v2 on v1

v2 whole, which is shorter than its diff:
```python
import functools
import math

import jax
import jax.numpy as jnp
from jax import lax
from jax.experimental import pallas as pl
from jax.experimental.pallas import tpu as pltpu
from jax.sharding import PartitionSpec as P

SUB = 8
PACK = 16
FACES = 6
LIMIT = 48 * 2**20
VMEM = pl.BlockSpec(memory_space=pltpu.VMEM)
ANY = pl.BlockSpec(memory_space=pl.ANY)


def halves(value):
    high = value.astype(jnp.bfloat16)
    low = (value - high.astype(jnp.float32)).astype(jnp.bfloat16)
    return high, low


def window_of(low_row, last, rows):
    base = low_row // SUB * SUB - SUB
    return base, (last // SUB + 2) * SUB - base


def fetch(copies, semaphores):
    started = []
    for index, (source, target) in enumerate(copies):
        started.append(pltpu.make_async_copy(source, target, semaphores.at[index]))
    for copy in started:
        copy.start()
    for copy in started:
        copy.wait()


def fetch_rows(own, perms, fields, near, base, size, rows, semaphores, more=()):
    begin, end = max(base, 0), min(base + size, rows)
    inside, there = pl.ds(begin, end - begin), pl.ds(begin - base, end - begin)
    terms = fields.shape[1]
    for edge, cells in ((0, begin - base), (end - base, base + size - end)):
        if cells:
            fields[0, :, pl.ds(edge, cells), :] = jnp.zeros((terms, cells, fields.shape[3]), fields.dtype)
    copies = [(own.at[:, inside, :], near.at[:, there, :])]
    for n, ref in enumerate(perms):
        copies.append((ref.at[:, inside, :], fields.at[n, :, there, :]))
    fetch(copies + list(more), semaphores)


def face_coefs(coef, fields, begin, count):
    terms, nz = fields.shape[1], fields.shape[3]
    span = coef.shape[0] // (FACES * terms)
    lane = lax.broadcasted_iota(jnp.int32, (count, nz), 1)
    for k in range(terms):
        here = fields[0, k, pl.ds(begin, count), :]
        others = (
            fields[1, k, pl.ds(begin, count), :],
            fields[2, k, pl.ds(begin, count), :],
            fields[0, k, pl.ds(begin + 1, count), :],
            fields[0, k, pl.ds(begin - 1, count), :],
            jnp.where(lane < nz - 1, pltpu.roll(here, nz - 1, 1), 0.0),
            jnp.where(lane > 0, pltpu.roll(here, 1, 1), 0.0),
        )
        for f, other in enumerate(others):
            coef[pl.ds((f * terms + k) * span, count), :] = 0.5 * (here + other)


def strided_rows(ref, start, count, stride):
    return ref[pl.ds(start, count, stride=stride), :]


def mode_block(ref, block, row, modes, stride):
    size = min(PACK, modes - block * PACK)
    value = strided_rows(ref, block * PACK * stride + row, size, stride)
    if size == PACK:
        return value
    return jnp.concatenate([value, jnp.zeros((PACK - size, value.shape[1]), value.dtype)], 0)


def factor_of(coef, at, terms, span):
    def factor(f, k):
        value = coef[pl.ds((f * terms + k) * span + at, SUB, stride=0), :]
        return jnp.concatenate([value] * (PACK // SUB), 0)

    return factor


def gathered_kernel(first, count, rows, mode_dev, pad, groups, sources, *refs):
    own_all, perm, perm_up, perm_down, weights = refs[:5]
    pieces = refs[5 : 5 + len(sources) * (groups - 1)]
    out, to_up, to_down = refs[5 + len(pieces) : 8 + len(pieces)]
    (
        near, fields, semaphores, coef, stack_even, stack_odd, mixed_even, mixed_odd, pending, above, beyond
    ) = refs[8 + len(pieces) :]
    terms, nz = fields.shape[1], fields.shape[3]
    low_row, last = max(first - 1, 0), min(first + count, rows - 1)
    span = coef.shape[0] // (FACES * terms)
    base, size = window_of(low_row, last, rows)
    perms = (perm, perm_up, perm_down)
    fetch_rows(own_all, perms, fields, near, base, size, rows, semaphores)
    own = near.reshape(mode_dev * size, nz)
    face_coefs(coef, fields, low_row - base, last - low_row + 1)
    lane = lax.broadcasted_iota(jnp.int32, (PACK, nz), 1)
    wide = groups * pad
    blocks = [(block, min(PACK, mode_dev - block * PACK)) for block in range(pad // PACK)]

    def fill(stack, slot, row, source):
        lanes = pl.ds(slot * nz, nz)
        start, length, index = source
        for s in range(groups):
            piece, at, stride = (own, row - base, size) if s == 0 else (pieces[index * (groups - 1) + s - 1], row - start, length)
            for block in range(pad // PACK):
                high, low = halves(mode_block(piece, block, at, mode_dev, stride))
                place = s * pad + block * PACK
                stack[place : place + PACK, lanes] = high
                stack[wide + place : wide + place + PACK, lanes] = low
                stack[2 * wide + place : 2 * wide + place + PACK, lanes] = high

    def mix(stack, mixed):
        mixed[...] = jnp.dot(weights[...], stack[...], preferred_element_type=jnp.float32)

    def sums(mixed, slot, row, block, faces):
        factor = factor_of(coef, row - low_row, terms, span)
        totals = [None] * len(faces)
        for k in range(terms):
            if k == terms - 1:
                value = mode_block(own, block, row - base, mode_dev, size)
            else:
                value = mixed[pl.ds(k * pad + block * PACK, PACK), pl.ds(slot * nz, nz)]
            for n, f in enumerate(faces):
                part = factor(f, k) * value
                totals[n] = part if totals[n] is None else totals[n] + part
        return totals

    def spread(mixed, row):
        for block, modes in blocks:
            here = pl.ds(block * PACK, PACK)
            here_out = block * PACK * count + row - first
            for slot in range(2):
                up, down, north, south, east, west = sums(mixed, slot, row + slot, block, range(FACES))
                place = pl.ds(here_out + slot, modes, stride=count)
                to_up[place, :] = -up[:modes]
                to_down[place, :] = -down[:modes]
                moved_east = jnp.where(lane > 0, pltpu.roll(east, 1, 1), 0.0)
                moved_west = jnp.where(lane < nz - 1, pltpu.roll(west, nz - 1, 1), 0.0)
                total = ((up + down) + (north + south)) + ((east - moved_east) + (west - moved_west))
                if slot == 0:
                    before = pending[here, :] - south
                    back = pl.ds(block * PACK * count + jnp.maximum(row - 1 - first, 0), modes, stride=count)
                    out[back, :] = before[:modes]
                    carried = total - above[here, :], north
                else:
                    out[pl.ds(here_out, modes, stride=count), :] = (carried[0] - south)[:modes]
                    pending[here, :] = total - carried[1]
                    above[here, :] = north

    def source_of(row):
        for index, (start, length) in reversed(list(enumerate(sources))):
            if row >= start:
                return start, length, index

    fill(stack_odd, 0, low_row, source_of(low_row))
    fill(stack_odd, 1, last, source_of(last))
    mix(stack_odd, mixed_odd)
    main = source_of(first)
    if main[2] != len(sources) - 1:
        late = source_of(last)
        fill(stack_even, 0, first, main)
        fill(stack_even, 1, first + 1, late)
        main = late
    else:
        fill(stack_even, 0, first, main)
        fill(stack_even, 1, first + 1, main)
    mix(stack_even, mixed_even)
    for block, modes in blocks:
        here = pl.ds(block * PACK, PACK)
        zero = jnp.zeros((PACK, nz), jnp.float32)
        above[here, :] = sums(mixed_odd, 0, low_row, block, [2])[0] if low_row < first else zero
        beyond[here, :] = sums(mixed_odd, 1, last, block, [3])[0] if last >= first + count else zero
        pending[here, :] = zero

    def body(step, carry):
        row = first + 4 * step
        fill(stack_odd, 0, row + 2, main)
        fill(stack_odd, 1, row + 3, main)
        mix(stack_odd, mixed_odd)
        spread(mixed_even, row)
        later = jnp.minimum(row + 4, first + count - 2)
        fill(stack_even, 0, later, main)
        fill(stack_even, 1, later + 1, main)
        mix(stack_even, mixed_even)
        spread(mixed_odd, row + 2)
        return carry

    lax.fori_loop(0, count // 4, body, 0)
    for block, modes in blocks:
        here = pl.ds(block * PACK, PACK)
        value = pending[here, :] - beyond[here, :]
        out[pl.ds(block * PACK * count + count - 1, modes, stride=count), :] = value[:modes]


def partial_kernel(first, count, rows, mode_dev, pad, groups, halo_first, *refs):
    own_all, up_all, down_all, perm, perm_up, perm_down, weights, out = refs[:8]
    sends = refs[8 : 8 + groups - 1]
    near, halo, fields, semaphores, coef, high_even, low_even, mean_even, high_odd, low_odd, mean_odd = refs[
        8 + groups - 1 :
    ]
    even, odd = (high_even, low_even, mean_even), (high_odd, low_odd, mean_odd)
    terms, nz = fields.shape[1], fields.shape[3]
    base, size = window_of(first, first + count - 1, rows)
    perms = (perm, perm_up, perm_down)
    here = pl.ds(first - halo_first, count)
    halos = [(up_all.at[:, here, :], halo.at[0]), (down_all.at[:, here, :], halo.at[1])]
    fetch_rows(own_all, perms, fields, near, base, size, rows, semaphores, halos)
    own = near.reshape(mode_dev * size, nz)
    up, down = halo.at[0].reshape(mode_dev * count, nz), halo.at[1].reshape(mode_dev * count, nz)
    face_coefs(coef, fields, first - base, count)
    lane = lax.broadcasted_iota(jnp.int32, (PACK, nz), 1)
    wide = groups * pad

    def build(store, row):
        high, low, mean = store
        for slot in range(2):
            lanes = pl.ds(slot * nz, nz)
            at = row + slot
            factor = factor_of(coef, at - first, terms, count)
            north_in, south_in = at + 1 < rows, at > 0
            for block in range(pad // PACK):
                centre = mode_block(own, block, at - base, mode_dev, size)
                north = mode_block(own, block, jnp.minimum(at + 1, rows - 1) - base, mode_dev, size)
                south = mode_block(own, block, jnp.maximum(at - 1, 0) - base, mode_dev, size)
                others = (
                    mode_block(up, block, at - first, mode_dev, count),
                    mode_block(down, block, at - first, mode_dev, count),
                    jnp.where(north_in, north, 0.0) if first + count == rows else north,
                    jnp.where(south_in, south, 0.0) if first == 0 else south,
                    jnp.where(lane < nz - 1, pltpu.roll(centre, nz - 1, 1), 0.0),
                    jnp.where(lane > 0, pltpu.roll(centre, 1, 1), 0.0),
                )
                steps = [centre - other for other in others]
                for k in range(terms):
                    total = factor(0, k) * steps[0]
                    for f in range(1, FACES):
                        total = total + factor(f, k) * steps[f]
                    if k == terms - 1:
                        mean[slot, pl.ds(block * PACK, PACK), :] = total
                    else:
                        place = pl.ds(k * pad + block * PACK, PACK)
                        high[place, lanes], low[place, lanes] = halves(total)

    def multiply(store, row):
        high, low, mean = store
        both = jnp.dot(weights[...], high[...], preferred_element_type=jnp.float32)
        rest = jnp.dot(weights[0:wide, :], low[...], preferred_element_type=jnp.float32)
        result = both[0:wide] + both[wide : 2 * wide] + rest
        for slot in range(2):
            lanes = slice(slot * nz, (slot + 1) * nz)
            for s in range(groups):
                target = out if s == 0 else sends[s - 1]
                value = result[s * pad : (s + 1) * pad, lanes]
                if s == 0:
                    value = value + mean[slot]
                target[pl.ds(row + slot - first, mode_dev, stride=count), :] = value[:mode_dev]

    build(even, first)

    def body(step, carry):
        row = first + 4 * step
        multiply(even, row)
        build(odd, row + 2)
        multiply(odd, row + 2)
        build(even, jnp.minimum(row + 4, first + count - 2))
        return carry

    lax.fori_loop(0, count // 4, body, 0)


def place_sum(result, parts, first, shape):
    modes, count, nz = parts[0].shape
    kept = [] if result is None else [result]
    steps = next(n for n in (2, 3, 1) if modes % n == 0)

    def kernel(*refs):
        *sources, out = refs[len(kept) :]
        total = sources[0][...]
        for source in sources[1:]:
            total = total + source[...]
        out[...] = total

    size = math.gcd(first, count)
    if size < count:
        steps = 1
    return pl.pallas_call(
        kernel,
        grid=(steps, count // size),
        in_specs=[pl.BlockSpec(memory_space=pl.ANY)] * len(kept)
        + [pl.BlockSpec((modes // steps, size, nz), lambda i, j: (i, j, 0))] * len(parts),
        out_specs=pl.BlockSpec((modes // steps, size, nz), lambda i, j: (i, j + first // size, 0)),
        out_shape=jax.ShapeDtypeStruct(shape, jnp.float32),
        input_output_aliases={0: 0} if kept else {},
        name="place",
    )(*kept, *parts)


def local(mode_coeffs, mean_perm, kl_fields, couplings):
    mode_dev, _, rows, nz = mode_coeffs.shape
    terms = kl_fields.shape[0] + 1
    groups = lax.axis_size("modes")
    planes = lax.axis_size("space")
    pad = pl.cdiv(mode_dev, PACK) * PACK
    group = lax.axis_index("modes")
    forward = [(i, i + 1) for i in range(planes - 1)]
    backward = [(target, source) for source, target in forward]
    own3 = mode_coeffs.reshape(mode_dev, rows, nz)

    def rotated(value, step):
        return lax.ppermute(value, "modes", [(i, (i + step) % groups) for i in range(groups)])

    def block(row_group, column_group):
        piece = lax.dynamic_slice(
            couplings,
            (0, (row_group % groups) * mode_dev, (column_group % groups) * mode_dev),
            (terms - 1, mode_dev, mode_dev),
        )
        return jnp.pad(piece, ((0, 0), (0, pad - mode_dev), (0, pad - mode_dev)))

    def split(value):
        high = lax.reduce_precision(value, 8, 7)
        return high.astype(jnp.bfloat16), (value - high).astype(jnp.bfloat16)

    gathered = [(0, 32), (32, 40)]
    partial = [(72, 24), (96, 24)]

    perm = jnp.concatenate([kl_fields, mean_perm[None]], 0).reshape(terms, rows, nz)
    perm_up, perm_down = lax.ppermute(perm, "space", backward), lax.ppermute(perm, "space", forward)
    received, bounds, low_row = [], [], 0
    for index, (first, count) in enumerate(gathered):
        high_row = min(first + count + 1, rows)
        piece = own3[:, low_row:high_row].reshape(mode_dev * (high_row - low_row), nz)
        if index:
            piece, perm_up, perm_down = lax.optimization_barrier((piece, perm_up, perm_down))
        received.append([rotated(piece, s) for s in range(1, groups)])
        bounds.append((low_row, high_row - low_row))
        low_row = high_row
    halo_first = partial[0][0]
    edge = own3[:, halo_first:]
    halos = lax.ppermute(edge, "space", backward), lax.ppermute(edge, "space", forward)

    high, low = split(jnp.concatenate([block(group, group - s) for s in range(groups)], 2))
    gathered_weights = jnp.concatenate([high, high, low], 2).reshape((terms - 1) * pad, 3 * groups * pad)
    high, low = split(jnp.concatenate([block(group + s, group) for s in range(groups)], 1))
    partial_weights = (
        jnp.concatenate([high, low], 1).transpose(1, 0, 2).reshape(2 * groups * pad, (terms - 1) * pad)
    )

    params = pltpu.CompilerParams(vmem_limit_bytes=LIMIT)
    f32 = jnp.float32
    result = None
    shape = (mode_dev, rows, nz)

    shares = []

    def window_scratch(first, count, around):
        _, size = window_of(max(first - around, 0), min(first + count - 1 + around, rows - 1), rows)
        return [
            pltpu.VMEM((mode_dev, size, nz), f32),
            pltpu.VMEM((3, terms, size, nz), f32),
            pltpu.SemaphoreType.DMA((6,)),
            pltpu.VMEM((FACES * terms * (count + around * SUB), nz), f32),
        ]

    def cost(count):
        products = 3 * 2 * (terms - 1) * mode_dev * mode_dev * groups * count * nz
        return pl.CostEstimate(flops=16 * products, bytes_accessed=2**20 * count, transcendentals=0)

    def partial_shares(index):
        first, count = partial[index]
        flat = jax.ShapeDtypeStruct((mode_dev * count, nz), f32)
        near, *rest = window_scratch(first, count, 0)
        outs = pl.pallas_call(
            functools.partial(partial_kernel, first, count, rows, mode_dev, pad, groups, halo_first),
            in_specs=[ANY] * 6 + [VMEM],
            out_specs=[VMEM] * groups,
            out_shape=[flat] * groups,
            scratch_shapes=[near, pltpu.VMEM((2, mode_dev, count, nz), f32), *rest]
            + [
                pltpu.VMEM(((terms - 1) * pad, 2 * nz), jnp.bfloat16),
                pltpu.VMEM(((terms - 1) * pad, 2 * nz), jnp.bfloat16),
                pltpu.VMEM((2, pad, nz), f32),
            ]
            * 2,
            compiler_params=params,
            cost_estimate=cost(count),
            name="partial",
        )(own3, *halos, perm, perm_up, perm_down, partial_weights)
        parts = [outs[0]] + [rotated(value, s) for s, value in enumerate(outs[1:], 1)]
        return first, [part.reshape(mode_dev, count, nz) for part in parts]

    def gathered_shares(index):
        first, count = gathered[index]
        begin = max(index - 1, 0)
        sources = bounds[begin : index + 1]
        pieces = [piece for group_pieces in received[begin : index + 1] for piece in group_pieces]
        flat = jax.ShapeDtypeStruct((mode_dev * count, nz), f32)
        centre, to_up, to_down = pl.pallas_call(
            functools.partial(
                gathered_kernel, first, count, rows, mode_dev, pad, groups, sources
            ),
            in_specs=[ANY] * 4 + [VMEM] * (1 + len(pieces)),
            out_specs=[VMEM] * 3,
            out_shape=[flat] * 3,
            scratch_shapes=window_scratch(first, count, 1)
            + [
                pltpu.VMEM((3 * groups * pad, 2 * nz), jnp.bfloat16),
                pltpu.VMEM((3 * groups * pad, 2 * nz), jnp.bfloat16),
                pltpu.VMEM(((terms - 1) * pad, 2 * nz), f32),
                pltpu.VMEM(((terms - 1) * pad, 2 * nz), f32),
                pltpu.VMEM((pad, nz), f32),
                pltpu.VMEM((pad, nz), f32),
                pltpu.VMEM((pad, nz), f32),
            ],
            compiler_params=params,
            cost_estimate=cost(count),
            name="gathered",
        )(own3, perm, perm_up, perm_down, gathered_weights, *pieces)
        parts = [centre, lax.ppermute(to_up, "space", forward), lax.ppermute(to_down, "space", backward)]
        return first, [part.reshape(mode_dev, count, nz) for part in parts]

    shares = [gathered_shares(0), partial_shares(0), partial_shares(1), gathered_shares(1)]
    for first, parts in shares:
        result = place_sum(result, parts, first, shape)
    return result.reshape(mode_coeffs.shape)


def solution(mesh):
    in_specs = (
        P("modes", "space", None, None),
        P("space", None, None),
        P(None, "space", None, None),
        P(),
    )
    out_specs = P("modes", "space", None, None)
    return jax.shard_map(local, mesh=mesh, in_specs=in_specs, out_specs=out_specs, check_vma=False)
```

time: 186 us -> 127 us (0.68)
  Pallas kernels: 99 us -> 50.8 us
  starting transfers between devices: 33 us -> 23.2 us
  waiting for transfers between devices: 34 us -> 29.1 us
  local copies, waits for them, and re-layouts: 17.1 us -> 20 us
    pallas_call x8, Pallas kernels: 99 us -> 50.8 us  [the longest x2 23.4 us: gathered_shares(): pl.pallas_call(functools.partial(gathered_kernel, first, count, rows, mod...]
    ppermute x10 -> x8, starting transfers between devices: 29.1 us -> 20.2 us  [the longest x2 4.84 us: gathered_shares(): lax.ppermute(to_down, 'space', backward)]
    unnamed x22 -> x26, local copies, waits for them, and re-layouts: 4.01 us -> 7.71 us
    pad x3 -> x0, local copies, waits for them, and re-layouts: 3.21 us -> none  [widened(): return jnp.pad(value, ((0, 0), (SUB, SUB), (0, 0)))]
    ppermute x10 -> x8, waiting for transfers between devices: 20.4 us -> 17.8 us  [the longest x1 9.86 us: local(): lax.ppermute(edge, 'space', backward)]
    ppermute x4, waiting for transfers between devices: 13.5 us -> 11.3 us  [rotated(): lax.ppermute(value, 'modes', [(i, (i + step) % groups) for i in range(gro...]
    convert_element_type x2, other arithmetic: 0.27 us -> 2.25 us  [split(): return (high.astype(jnp.bfloat16), (value - high).astype(jnp.bfloat16))]
  transfers between devices with their start and end apart: 14 -> 12, of which waited for: 2 -> 3; matrix products, arithmetic and copies ran while one was open for 6% -> 11% of each run, Pallas kernels for 52% -> 37%
where the time goes in v2:
time: 127 us; the launch traced here: 126 us
  Pallas kernels  50.8 us (40%)
  waiting for transfers between devices  29.1 us (23%)
  starting transfers between devices  23.2 us (18%)
  local copies, waits for them, and re-layouts  20 us (16%)
  other arithmetic  2.35 us (2%)
    pallas_call x2, Pallas kernels, gathered_shares(): pl.pallas_call(functools.partial(gathered_kernel, first, count, rows, mod...  23.4 us
    pallas_call x2, Pallas kernels, partial_shares(): pl.pallas_call(functools.partial(partial_kernel, first, count, rows, mode...  16 us
    pallas_call x4, Pallas kernels, place_sum(): pl.pallas_call(kernel, grid=(steps, count // size), in_specs=[pl.BlockSpe...  11.4 us
    ppermute x4, waiting for transfers between devices, rotated(): lax.ppermute(value, 'modes', [(i, (i + step) % groups) for i in range(gro...  11.3 us
    ppermute x1, waiting for transfers between devices, local(): lax.ppermute(edge, 'space', backward)  9.86 us
    ppermute x1, waiting for transfers between devices, local(): lax.ppermute(perm, 'space', backward)  7.9 us
    unnamed x26, local copies, waits for them, and re-layouts  7.71 us
    ppermute x2, starting transfers between devices, gathered_shares(): lax.ppermute(to_down, 'space', backward)  4.84 us
  transfers between devices with their start and end apart: 12, of which 3 were waited for; matrix products, arithmetic and copies ran while one was open for 11% of the time, Pallas kernels for 37%

profile of v2, /device:TPU:17, one launch (start us, length us, event | category | flops | bytes accessed | tf_op | source)
XLA Modules:
  0.0 125.6 jit_solution(11499445850741650064)
XLA Ops:
  0.0 1.4 %slice.13 = f32[60,33,128]{2,1,0:T(8,128)S(1)} slice(f32[60,120,128]{2,1,0:T(8,128)} %bitcast.28), slice={[0:60], [0:33], [0:128]} | slice | bytes 2027520 | tf_op jit(solution)/shard_map/slice | solution.py:342
  3.7 4.0 %collective-permute-start.1 = (f32[8,120,128]{2,1,0:T(8,128)S(1)}, f32[8,120,128]{2,1,0:T(8,128)}, u32[]{:S(2)}, u32[]{:S(2)}) collective-permute-start(f32[8,120,128]{2,1,0:T(8,128)S(1)} %maximum_bitcast_fusion.refs_1_.refs_3_), channel_id=1, source_target_pairs={{0,1},{1,2},{2,3},{3,4},{4,5},{5,6},{6,7},{7,8},{8,9},{9,10},{10,1... | collective-permute-start | bytes 1474568 | tf_op jit(solution)/shard_map/ppermute | solution.py:338
  7.7 1.9 %collective-permute-start = (f32[8,120,128]{2,1,0:T(8,128)S(1)}, f32[8,120,128]{2,1,0:T(8,128)}, u32[]{:S(2)}, u32[]{:S(2)}) collective-permute-start(f32[8,120,128]{2,1,0:T(8,128)S(1)} %maximum_bitcast_fusion.refs_1_.refs_3_), channel_id=1, source_target_pairs={{1,0},{2,1},{3,2},{4,3},{5,4},{6,5},{7,6},{8,7},{9,8},{10,9},{11,1... | collective-permute-start | bytes 1474568 | tf_op jit(solution)/shard_map/ppermute | solution.py:338
  9.6 2.6 %slice.14 = f32[60,48,128]{2,1,0:T(8,128)} slice(f32[60,120,128]{2,1,0:T(8,128)} %bitcast.29), slice={[0:60], [72:120], [0:128]} | slice | bytes 2949120 | tf_op jit(solution)/shard_map/slice | solution.py:349
  12.2 3.6 %collective-permute-start.6 = (f32[60,48,128]{2,1,0:T(8,128)}, f32[60,48,128]{2,1,0:T(8,128)S(1)}, u32[]{:S(2)}, u32[]{:S(2)}) collective-permute-start(f32[60,48,128]{2,1,0:T(8,128)} %slice.14), channel_id=1, source_target_pairs={{0,1},{1,2},{2,3},{3,4},{4,5},{5,6},{6,7},{7,8},{8,9},{9,10},{10,1... | collective-permute-start | bytes 4423688 | tf_op jit(solution)/shard_map/ppermute | solution.py:350
  15.9 1.9 %collective-permute-start.5 = (f32[60,48,128]{2,1,0:T(8,128)}, f32[60,48,128]{2,1,0:T(8,128)}, u32[]{:S(2)}, u32[]{:S(2)}) collective-permute-start(f32[60,48,128]{2,1,0:T(8,128)} %slice.14), channel_id=1, source_target_pairs={{1,0},{2,1},{3,2},{4,3},{5,4},{6,5},{7,6},{8,7},{9,8},{10,9},{11,1... | collective-permute-start | bytes 4423688 | tf_op jit(solution)/shard_map/ppermute | solution.py:350
  17.8 2.1 %constant_dynamic-slice_fusion = (f32[7,60,60]{2,1,0:T(8,128)S(1)}, f32[7,60,60]{2,1,0:T(8,128)S(1)}, f32[7,60,60]{2,1,0:T(8,128)}) fusion(f32[7,120,120]{2,1,0:T(8,128)} %param.7, s32[]{:T(128)S(6)} %select_n.44, s32[]{:T(128)S(6)} %select_n.40, s32[]{:T(128)S(6)} %select_n.42), kind=kLoop, calls=%fused_computation.12 | loop fusion | bytes 604812 | tf_op jit(solution)/shard_map/dynamic_slice | solution.py:323
  19.9 2.5 %slice.12 = f32[60,40,128]{2,1,0:T(8,128)} slice(f32[60,120,128]{2,1,0:T(8,128)} %bitcast.30), slice={[0:60], [33:73], [0:128]} | slice | bytes 2457600 | tf_op jit(solution)/shard_map/slice | solution.py:342
  23.5 1.6 %pad.12 = f32[7,64,64]{2,1,0:T(8,128)} pad(f32[7,60,60]{2,1,0:T(8,128)} %get-tuple-element.37, f32[]{:T(128)} %constant.45.clone.1), padding=0_0x0_4x0_4 | pad | bytes 215492 | tf_op jit(solution)/shard_map/jit(_pad)/pad | solution.py:328
  28.5 7.9 %collective-permute-done.refs_2_.refs_4_ = f32[8,120,128]{2,1,0:T(8,128)} collective-permute-done((f32[8,120,128]{2,1,0:T(8,128)S(1)}, f32[8,120,128]{2,1,0:T(8,128)}, u32[]{:S(2)}, u32[]{:S(2)}) %collective-permute-start) | collective-permute-done | bytes 491552 | tf_op jit(solution)/shard_map/ppermute | solution.py:338
  36.6 10.6 %gathered.2 = (f32[1920,128]{1,0:T(8,128)S(1)}, f32[1920,128]{1,0:T(8,128)S(1)}, f32[1920,128]{1,0:T(8,128)S(1)}) custom-call(f32[60,120,128]{2,1,0:T(8,128)} %bitcast.31, f32[8,120,128]{2,1,0:T(8,128)S(1)} %maximum_bitcast_fusion.refs_1_.refs_3_, f32[8,120,128]{2,1,0:T(8,128)} %collective-permute-done.refs_2_.refs_4_, ...), custom_call_target="tpu_custom_call" | custom-call | flops 19818086400 | bytes 33554432 | tf_op jit(solution)/shard_map/gathered/pallas_call | solution.py:408
  48.2 1.9 %collective-permute-start.3 = (f32[1920,128]{1,0:T(8,128)S(1)}, f32[1920,128]{1,0:T(8,128)S(1)}, u32[]{:S(2)}, u32[]{:S(2)}) collective-permute-start(f32[1920,128]{1,0:T(8,128)S(1)} %get-tuple-element.21), channel_id=1, source_target_pairs={{0,1},{1,2},{2,3},{3,4},{4,5},{5,6},{6,7},{7,8},{8,9},{9,10},{10,1... | collective-permute-start | bytes 2949128 | tf_op jit(solution)/shard_map/ppermute | solution.py:429
  50.1 2.5 %collective-permute-start.4 = (f32[1920,128]{1,0:T(8,128)S(1)}, f32[1920,128]{1,0:T(8,128)S(1)}, u32[]{:S(2)}, u32[]{:S(2)}) collective-permute-start(f32[1920,128]{1,0:T(8,128)S(1)} %get-tuple-element.22), channel_id=1, source_target_pairs={{1,0},{2,1},{3,2},{4,3},{5,4},{6,5},{7,6},{8,7},{9,8},{10,9},{11,1... | collective-permute-start | bytes 2949128 | tf_op jit(solution)/shard_map/ppermute | solution.py:429
  52.7 9.9 %collective-permute-done.5.refs_1_ = f32[60,48,128]{2,1,0:T(8,128)} collective-permute-done((f32[60,48,128]{2,1,0:T(8,128)}, f32[60,48,128]{2,1,0:T(8,128)}, u32[]{:S(2)}, u32[]{:S(2)}) %collective-permute-start.5) | collective-permute-done | bytes 1474592 | tf_op jit(solution)/shard_map/ppermute | solution.py:350
  62.5 8.0 %partial.2 = (f32[1440,128]{1,0:T(8,128)S(1)}, f32[1440,128]{1,0:T(8,128)}) custom-call(f32[60,120,128]{2,1,0:T(8,128)} %bitcast.32, f32[60,48,128]{2,1,0:T(8,128)} %collective-permute-done.5.refs_1_, f32[60,48,128]{2,1,0:T(8,128)S(1)} %collective-permute-done.6.refs_2_, f32[8,120,128]{2,1,0:T(8,128)S(1)} %maximum_bitcast_fusion.refs_1_.refs_3_, ...), custom_call_target="tpu_custom_call" | custom-call | flops 14863564800 | bytes 25165824 | tf_op jit(solution)/shard_map/partial/pallas_call | solution.py:383
  72.7 12.8 %gathered.3 = (f32[2400,128]{1,0:T(8,128)S(1)}, f32[2400,128]{1,0:T(8,128)S(1)}, f32[2400,128]{1,0:T(8,128)}) custom-call(f32[60,120,128]{2,1,0:T(8,128)} %bitcast.33, f32[8,120,128]{2,1,0:T(8,128)S(1)} %maximum_bitcast_fusion.refs_1_.refs_3_, f32[8,120,128]{2,1,0:T(8,128)} %collective-permute-done.refs_2_.refs_4_, ...), custom_call_target="tpu_custom_call" | custom-call | flops 24772608000 | bytes 41943040 | tf_op jit(solution)/shard_map/gathered/pallas_call | solution.py:408
  86.5 2.0 %collective-permute-start.10 = (f32[2400,128]{1,0:T(8,128)S(1)}, f32[2400,128]{1,0:T(8,128)}, u32[]{:S(2)}, u32[]{:S(2)}) collective-permute-start(f32[2400,128]{1,0:T(8,128)S(1)} %get-tuple-element.29), channel_id=1, source_target_pairs={{0,1},{1,2},{2,3},{3,4},{4,5},{5,6},{6,7},{7,8},{8,9},{9,10},{10,1... | collective-permute-start | bytes 3686408 | tf_op jit(solution)/shard_map/ppermute | solution.py:429
  88.6 2.3 %collective-permute-start.11 = (f32[2400,128]{1,0:T(8,128)}, f32[2400,128]{1,0:T(8,128)}, u32[]{:S(2)}, u32[]{:S(2)}) collective-permute-start(f32[2400,128]{1,0:T(8,128)} %get-tuple-element.30), channel_id=1, source_target_pairs={{1,0},{2,1},{3,2},{4,3},{5,4},{6,5},{7,6},{8,7},{9,8},{10,9},{11,1... | collective-permute-start | bytes 3686408 | tf_op jit(solution)/shard_map/ppermute | solution.py:429
  90.9 7.9 %partial.3 = (f32[1440,128]{1,0:T(8,128)S(1)}, f32[1440,128]{1,0:T(8,128)}) custom-call(f32[60,120,128]{2,1,0:T(8,128)} %bitcast.34, f32[60,48,128]{2,1,0:T(8,128)} %collective-permute-done.5.refs_1_, f32[60,48,128]{2,1,0:T(8,128)S(1)} %collective-permute-done.6.refs_2_, f32[8,120,128]{2,1,0:T(8,128)S(1)} %maximum_bitcast_fusion.refs_1_.refs_3_, ...), custom_call_target="tpu_custom_call" | custom-call | flops 14863564800 | bytes 25165824 | tf_op jit(solution)/shard_map/partial/pallas_call | solution.py:383
  102.0 2.6 %place.4.refs_0_ = f32[60,120,128]{2,1,0:T(8,128)} custom-call(f32[60,32,128]{2,1,0:T(8,128)} %bitcast.25, f32[60,32,128]{2,1,0:T(8,128)} %bitcast.36, f32[60,32,128]{2,1,0:T(8,128)} %bitcast.37), custom_call_target="tpu_custom_call" | custom-call | tf_op jit(solution)/shard_map/place/pallas_call | solution.py:296
  104.6 2.1 %place.5.refs_0_ = f32[60,120,128]{2,1,0:T(8,128)} custom-call(f32[60,120,128]{2,1,0:T(8,128)} %place.4.refs_0_, f32[60,24,128]{2,1,0:T(8,128)} %bitcast.26, f32[60,24,128]{2,1,0:T(8,128)} %bitcast.13.refs_2_), custom_call_target="tpu_custom_call", output_to_operand_aliasing={{}: (0, {})} | custom-call | tf_op jit(solution)/shard_map/place/pallas_call | solution.py:296
  106.7 11.3 %collective-permute-done.8 = f32[1440,128]{1,0:T(8,128)S(1)} collective-permute-done((f32[1440,128]{1,0:T(8,128)}, f32[1440,128]{1,0:T(8,128)S(1)}, u32[]{:S(2)}, u32[]{:S(2)}) %collective-permute-start.8) | collective-permute-done | bytes 737312 | tf_op jit(solution)/shard_map/ppermute | solution.py:320
  118.9 2.1 %place.6.refs_0_ = f32[60,120,128]{2,1,0:T(8,128)} custom-call(f32[60,120,128]{2,1,0:T(8,128)} %place.5.refs_0_, f32[60,24,128]{2,1,0:T(8,128)} %bitcast.27, f32[60,24,128]{2,1,0:T(8,128)} %bitcast.41), custom_call_target="tpu_custom_call", output_to_operand_aliasing={{}: (0, {})} | custom-call | tf_op jit(solution)/shard_map/place/pallas_call | solution.py:296
  121.0 4.6 %place.7 = f32[60,120,128]{2,1,0:T(8,128)} custom-call(f32[60,120,128]{2,1,0:T(8,128)} %place.6.refs_0_, f32[60,40,128]{2,1,0:T(8,128)} %bitcast.24, f32[60,40,128]{2,1,0:T(8,128)} %bitcast.17.refs_2_, f32[60,40,128]{2,1,0:T(8,128)} %bitcast.18.refs_3_), custom_call_target="tpu_custom_call", output_to_operand_aliasing={{}: (0, {})} | custom-call | tf_op jit(solution)/shard_map/place/pallas_call | solution.py:296
  (48 shorter events, 15.0 us)
Async XLA Ops:
  1.4 2.3 %copy-start.9 = (f32[7,1,120,128]{3,2,1,0:T(8,128)S(1)}, f32[7,1,120,128]{3,2,1,0:T(8,128)}, u32[]{:S(2)}) copy-start(f32[7,1,120,128]{3,2,1,0:T(8,128)} %param.6) | copy-start | bytes 1290244
  1.4 2.3 %copy-start.10 = (f32[1,120,128]{2,1,0:T(8,128)S(1)}, f32[1,120,128]{2,1,0:T(8,128)}, u32[]{:S(2)}) copy-start(f32[1,120,128]{2,1,0:T(8,128)} %param.5) | copy-start | bytes 184324
  2.4 34.2 %collective-permute-start.2 = (f32[1980,128]{1,0:T(8,128)}, f32[1980,128]{1,0:T(8,128)S(1)}, u32[]{:S(2)}, u32[]{:S(2)}) collective-permute-start(f32[1980,128]{1,0:T(8,128)} %reshape.61), channel_id=1, source_target_pairs={{0,16},{16,0},{1,17},{17,1},{2,18},{18,2},{3,19},{19,3},{4,20},{20... | collective-permute-start | bytes 3041288 | tf_op jit(solution)/shard_map/ppermute | solution.py:320
  3.7 24.8 %collective-permute-start.1 = (f32[8,120,128]{2,1,0:T(8,128)S(1)}, f32[8,120,128]{2,1,0:T(8,128)}, u32[]{:S(2)}, u32[]{:S(2)}) collective-permute-start(f32[8,120,128]{2,1,0:T(8,128)S(1)} %maximum_bitcast_fusion.refs_1_.refs_3_), channel_id=1, source_target_pairs={{0,1},{1,2},{2,3},{3,4},{4,5},{5,6},{6,7},{7,8},{8,9},{9,10},{10,1... | collective-permute-start | bytes 1474568 | tf_op jit(solution)/shard_map/ppermute | solution.py:338
  7.7 28.7 %collective-permute-start = (f32[8,120,128]{2,1,0:T(8,128)S(1)}, f32[8,120,128]{2,1,0:T(8,128)}, u32[]{:S(2)}, u32[]{:S(2)}) collective-permute-start(f32[8,120,128]{2,1,0:T(8,128)S(1)} %maximum_bitcast_fusion.refs_1_.refs_3_), channel_id=1, source_target_pairs={{1,0},{2,1},{3,2},{4,3},{5,4},{6,5},{7,6},{8,7},{9,8},{10,9},{11,1... | collective-permute-start | bytes 1474568 | tf_op jit(solution)/shard_map/ppermute | solution.py:338
  12.2 40.4 %collective-permute-start.6 = (f32[60,48,128]{2,1,0:T(8,128)}, f32[60,48,128]{2,1,0:T(8,128)S(1)}, u32[]{:S(2)}, u32[]{:S(2)}) collective-permute-start(f32[60,48,128]{2,1,0:T(8,128)} %slice.14), channel_id=1, source_target_pairs={{0,1},{1,2},{2,3},{3,4},{4,5},{5,6},{6,7},{7,8},{8,9},{9,10},{10,1... | collective-permute-start | bytes 4423688 | tf_op jit(solution)/shard_map/ppermute | solution.py:350
  15.9 46.7 %collective-permute-start.5 = (f32[60,48,128]{2,1,0:T(8,128)}, f32[60,48,128]{2,1,0:T(8,128)}, u32[]{:S(2)}, u32[]{:S(2)}) collective-permute-start(f32[60,48,128]{2,1,0:T(8,128)} %slice.14), channel_id=1, source_target_pairs={{1,0},{2,1},{3,2},{4,3},{5,4},{6,5},{7,6},{8,7},{9,8},{10,9},{11,1... | collective-permute-start | bytes 4423688 | tf_op jit(solution)/shard_map/ppermute | solution.py:350
  36.4 35.3 %collective-permute-start.9 = (f32[2400,128]{1,0:T(8,128)}, f32[2400,128]{1,0:T(8,128)S(1)}, u32[]{:S(2)}, u32[]{:S(2)}) collective-permute-start(f32[2400,128]{1,0:T(8,128)} %bitcast.35), channel_id=1, source_target_pairs={{0,16},{16,0},{1,17},{17,1},{2,18},{18,2},{3,19},{19,3},{4,20},{20... | collective-permute-start | bytes 3686408 | tf_op jit(solution)/shard_map/ppermute | solution.py:320
  36.6 10.6 %copy-start.4 = (f32[1980,128]{1,0:T(8,128)}, f32[1980,128]{1,0:T(8,128)S(1)}, u32[]{:S(2)}) copy-start(f32[1980,128]{1,0:T(8,128)S(1)} %collective-permute-done.2.refs_5_) | copy-start | bytes 3041284
  47.2 0.9 copy-start.1
  48.2 51.5 %collective-permute-start.3 = (f32[1920,128]{1,0:T(8,128)S(1)}, f32[1920,128]{1,0:T(8,128)S(1)}, u32[]{:S(2)}, u32[]{:S(2)}) collective-permute-start(f32[1920,128]{1,0:T(8,128)S(1)} %get-tuple-element.21), channel_id=1, source_target_pairs={{0,1},{1,2},{2,3},{3,4},{4,5},{5,6},{6,7},{7,8},{8,9},{9,10},{10,1... | collective-permute-start | bytes 2949128 | tf_op jit(solution)/shard_map/ppermute | solution.py:429
  50.1 22.6 %copy-start.5 = (f32[1980,128]{1,0:T(8,128)S(1)}, f32[1980,128]{1,0:T(8,128)}, u32[]{:S(2)}) copy-start(f32[1980,128]{1,0:T(8,128)} %copy-done.4) | copy-start | bytes 3041284
  50.1 50.8 %collective-permute-start.4 = (f32[1920,128]{1,0:T(8,128)S(1)}, f32[1920,128]{1,0:T(8,128)S(1)}, u32[]{:S(2)}, u32[]{:S(2)}) collective-permute-start(f32[1920,128]{1,0:T(8,128)S(1)} %get-tuple-element.22), channel_id=1, source_target_pairs={{1,0},{2,1},{3,2},{4,3},{5,4},{6,5},{7,6},{8,7},{9,8},{10,9},{11,1... | collective-permute-start | bytes 2949128 | tf_op jit(solution)/shard_map/ppermute | solution.py:429
  70.5 0.9 copy-start.2
  71.4 33.2 %collective-permute-start.7 = (f32[1440,128]{1,0:T(8,128)}, f32[1440,128]{1,0:T(8,128)}, u32[]{:S(2)}, u32[]{:S(2)}) collective-permute-start(f32[1440,128]{1,0:T(8,128)} %get-tuple-element.24), channel_id=1, source_target_pairs={{0,16},{16,0},{1,17},{17,1},{2,18},{18,2},{3,19},{19,3},{4,20},{20... | collective-permute-start | bytes 2211848 | tf_op jit(solution)/shard_map/ppermute | solution.py:320
  71.7 1.0 copy-start.11
  85.5 1.0 copy-start
  86.5 34.5 %collective-permute-start.10 = (f32[2400,128]{1,0:T(8,128)S(1)}, f32[2400,128]{1,0:T(8,128)}, u32[]{:S(2)}, u32[]{:S(2)}) collective-permute-start(f32[2400,128]{1,0:T(8,128)S(1)} %get-tuple-element.29), channel_id=1, source_target_pairs={{0,1},{1,2},{2,3},{3,4},{4,5},{5,6},{6,7},{7,8},{8,9},{9,10},{10,1... | collective-permute-start | bytes 3686408 | tf_op jit(solution)/shard_map/ppermute | solution.py:429
  88.6 32.4 %collective-permute-start.11 = (f32[2400,128]{1,0:T(8,128)}, f32[2400,128]{1,0:T(8,128)}, u32[]{:S(2)}, u32[]{:S(2)}) collective-permute-start(f32[2400,128]{1,0:T(8,128)} %get-tuple-element.30), channel_id=1, source_target_pairs={{1,0},{2,1},{3,2},{4,3},{5,4},{6,5},{7,6},{8,7},{9,8},{10,9},{11,1... | collective-permute-start | bytes 3686408 | tf_op jit(solution)/shard_map/ppermute | solution.py:429
  98.8 0.9 copy-start.3
  99.7 1.2 copy-start.6
  99.7 18.3 %collective-permute-start.8 = (f32[1440,128]{1,0:T(8,128)}, f32[1440,128]{1,0:T(8,128)S(1)}, u32[]{:S(2)}, u32[]{:S(2)}) collective-permute-start(f32[1440,128]{1,0:T(8,128)} %get-tuple-element.26), channel_id=1, source_target_pairs={{0,16},{16,0},{1,17},{17,1},{2,18},{18,2},{3,19},{19,3},{4,20},{20... | collective-permute-start | bytes 2211848 | tf_op jit(solution)/shard_map/ppermute | solution.py:320
  100.9 1.1 copy-start.7
  118.0 0.9 copy-start.8

commit v3 on v2

v3 whole, which is shorter than its diff:
```python
import functools

import jax
import jax.numpy as jnp
from jax import lax
from jax.experimental import pallas as pl
from jax.experimental.pallas import tpu as pltpu
from jax.sharding import PartitionSpec as P

SUB = 8
PACK = 16
FACES = 6
LIMIT = 48 * 2**20
VMEM = pl.BlockSpec(memory_space=pltpu.VMEM)
ANY = pl.BlockSpec(memory_space=pl.ANY)
HBM = pl.BlockSpec(memory_space=pltpu.HBM)


def halves(value):
    high = value.astype(jnp.bfloat16)
    low = (value - high.astype(jnp.float32)).astype(jnp.bfloat16)
    return high, low


def spaced(count):
    return count + SUB if count // SUB % 2 == 0 else count


def tile_copy(source, row, target, at, semaphore):
    return pltpu.make_async_copy(
        source.at[:, pl.ds(pl.multiple_of(row, SUB), SUB), :],
        target.at[:, pl.ds(pl.multiple_of(at, SUB), SUB), :],
        semaphore,
    )


def window_fields(perms, fields, first, count, rows, semaphores):
    begin, end = max(first - SUB, 0), min(first + count + SUB, rows)
    there = pl.ds(begin - first + SUB, end - begin)
    copies = []
    for n, ref in enumerate(perms):
        copies.append(
            pltpu.make_async_copy(ref.at[:, pl.ds(begin, end - begin), :], fields.at[n, :, there, :], semaphores.at[n])
        )
    for copy in copies:
        copy.start()
    return copies


def clear_outside(first, count, rows, fields, windows):
    for outside, at in ((first == 0, 0), (first + count == rows, count + SUB)):
        if outside:
            tile = pl.ds(at, SUB)
            fields[0, :, tile, :] = jnp.zeros((fields.shape[1], SUB, fields.shape[3]), fields.dtype)
            for ref in windows:
                ref[:, tile, :] = jnp.zeros((ref.shape[0], SUB, ref.shape[2]), ref.dtype)


def face_coefs(coef, fields, begin, count):
    terms, nz = fields.shape[1], fields.shape[3]
    span = coef.shape[0] // (FACES * terms)
    lane = lax.broadcasted_iota(jnp.int32, (count, nz), 1)
    for k in range(terms):
        here = fields[0, k, pl.ds(begin, count), :]
        others = (
            fields[1, k, pl.ds(begin, count), :],
            fields[2, k, pl.ds(begin, count), :],
            fields[0, k, pl.ds(begin + 1, count), :],
            fields[0, k, pl.ds(begin - 1, count), :],
            jnp.where(lane < nz - 1, pltpu.roll(here, nz - 1, 1), 0.0),
            jnp.where(lane > 0, pltpu.roll(here, 1, 1), 0.0),
        )
        for f, other in enumerate(others):
            coef[pl.ds((f * terms + k) * span, count), :] = 0.5 * (here + other)


def strided_rows(ref, start, count, stride):
    return ref[pl.ds(start, count, stride=stride), :]


def mode_block(ref, block, row, modes, stride):
    size = min(PACK, modes - block * PACK)
    value = strided_rows(ref, block * PACK * stride + row, size, stride)
    if size == PACK:
        return value
    return jnp.concatenate([value, jnp.zeros((PACK - size, value.shape[1]), value.dtype)], 0)


def factor_of(coef, at, terms, span):
    def factor(f, k):
        value = coef[pl.ds((f * terms + k) * span + at, SUB, stride=0), :]
        return jnp.concatenate([value] * (PACK // SUB), 0)

    return factor


def gathered_kernel(first, count, rows, mode_dev, pad, groups, sources, *refs):
    own_all, perm, perm_odd, perm_even, weights = refs[:5]
    pieces = refs[5 : 5 + len(sources) * (groups - 1)]
    results = refs[5 + len(pieces) : 8 + len(pieces)]
    near, far, fields, field_sems, in_sems, out_sems, coef = refs[8 + len(pieces) : 15 + len(pieces)]
    stack_even, mixed_even, stack_odd, mixed_odd, pending, above, *parts = refs[15 + len(pieces) :]
    terms, nz = fields.shape[1], fields.shape[3]
    span = coef.shape[0] // (FACES * terms)
    base, size = first - SUB, near.shape[1]
    tiles = count // SUB
    windows = [near] + [far.at[s] for s in range(groups - 1)]

    def tile_in(s, tile, index):
        row = base + tile * SUB
        if s == 0:
            return tile_copy(own_all, row, windows[0], tile * SUB, in_sems.at[0, tile])
        piece = pieces[index * (groups - 1) + s - 1]
        return tile_copy(piece, row - sources[index][0], windows[s], tile * SUB, in_sems.at[s, tile])

    def tile_out(n, tile):
        return tile_copy(parts[n], (tile + 1) * SUB, results[n], tile * SUB, out_sems.at[n, tile])

    field_copies = window_fields((perm, perm_odd, perm_even), fields, first, count, rows, field_sems)
    present = [tile for tile in range(tiles + 2) if 0 <= base + tile * SUB < rows]
    latest = len(sources) - 1
    early = {tile: max(latest - 1, 0) if tile < 2 else latest for tile in present}
    for tile in present:
        for s in range(groups):
            tile_in(s, tile, early[tile]).start()
    clear_outside(first, count, rows, fields, windows)
    for copy in field_copies:
        copy.wait()
    own, *others = [ref.reshape(mode_dev * size, nz) for ref in windows]
    tall = parts[0].shape[1]
    out, to_odd, to_even = [part.reshape(mode_dev * tall, nz) for part in parts]
    face_coefs(coef, fields, SUB - 1, span)
    pending[...] = jnp.zeros_like(pending)
    above[...] = jnp.zeros_like(above)
    lane = lax.broadcasted_iota(jnp.int32, (PACK, nz), 1)
    wide = groups * pad
    blocks = [(block, min(PACK, mode_dev - block * PACK)) for block in range(pad // PACK)]

    def mix(stack, mixed, row):
        for slot in range(2):
            lanes = pl.ds(slot * nz, nz)
            for s, piece in enumerate([own, *others]):
                for block, _ in blocks:
                    high, low = halves(mode_block(piece, block, row + slot - base, mode_dev, size))
                    place = s * pad + block * PACK
                    stack[place : place + PACK, lanes] = high
                    stack[wide + place : wide + place + PACK, lanes] = low
                    stack[2 * wide + place : 2 * wide + place + PACK, lanes] = high
        mixed[...] = jnp.dot(weights[...], stack[...], preferred_element_type=jnp.float32)

    def spread(mixed, row):
        for block, modes in blocks:
            here = pl.ds(block * PACK, PACK)
            for slot in range(2):
                factor = factor_of(coef, row + slot - first + 1, terms, span)
                totals = [None] * FACES
                for k in range(terms):
                    if k == terms - 1:
                        value = mode_block(own, block, row + slot - base, mode_dev, size)
                    else:
                        value = mixed[pl.ds(k * pad + block * PACK, PACK), pl.ds(slot * nz, nz)]
                    for f in range(FACES):
                        part = factor(f, k) * value
                        totals[f] = part if totals[f] is None else totals[f] + part
                odd, even, north, south, east, west = totals
                at = block * PACK * tall + row + slot - first + SUB
                place = pl.ds(at, modes, stride=tall)
                to_odd[place, :] = -odd[:modes]
                to_even[place, :] = -even[:modes]
                moved_east = jnp.where(lane > 0, pltpu.roll(east, 1, 1), 0.0)
                moved_west = jnp.where(lane < nz - 1, pltpu.roll(west, nz - 1, 1), 0.0)
                total = ((odd + even) + (north + south)) + ((east - moved_east) + (west - moved_west))
                back = pl.ds(at - 1, modes, stride=tall)
                if slot == 0:
                    out[back, :] = (pending[here, :] - south)[:modes]
                    carried = total - above[here, :], north
                else:
                    out[back, :] = (carried[0] - south)[:modes]
                    pending[here, :] = total - carried[1]
                    above[here, :] = north

    def wait_in(tile, index):
        for s in range(groups):
            tile_in(s, tile, index).wait()

    for tile in (0, 1):
        if tile in present:
            wait_in(tile, early[tile])
    mix(stack_even, mixed_even, first - 1)

    def four_rows(step, carry):
        row = first - 1 + 4 * step
        mix(stack_odd, mixed_odd, row + 2)
        spread(mixed_even, row)
        mix(stack_even, mixed_even, row + 4)
        spread(mixed_odd, row + 2)
        return carry

    def tile_step(tile, carry):
        @pl.when(tile < (tiles if tiles + 1 in present else tiles - 1))
        def _():
            wait_in(tile + 2, latest)

        lax.fori_loop(2 * tile, 2 * tile + 2, four_rows, 0)

        @pl.when(tile > 0)
        def _():
            for n in range(3):
                tile_out(n, tile - 1).start()

        return carry

    lax.fori_loop(0, tiles, tile_step, 0)
    spread(mixed_even, first - 1 + count)
    for n in range(3):
        tile_out(n, tiles - 1).start()
    for tile in range(tiles):
        for n in range(3):
            tile_out(n, tile).wait()


def partial_kernel(first, count, rows, mode_dev, pad, groups, halo_first, *refs):
    own_all, odd_all, even_all, perm, perm_odd, perm_even, weights = refs[:7]
    results = refs[7 : 7 + groups]
    near, halo, fields, field_sems, in_sems, out_sems, coef, high_even, low_even, mean_even, high_odd, low_odd, mean_odd, shares = refs[7 + groups :]
    even, odd = (high_even, low_even, mean_even), (high_odd, low_odd, mean_odd)
    terms, nz = fields.shape[1], fields.shape[3]
    base, size = first - SUB, near.shape[1]
    tall = halo.shape[2]
    tiles = count // SUB

    def near_in(tile):
        return tile_copy(own_all, base + tile * SUB, near, tile * SUB, in_sems.at[0, tile])

    def halo_in(side, tile):
        ref = (odd_all, even_all)[side]
        return tile_copy(ref, first - halo_first + tile * SUB, halo.at[side], tile * SUB, in_sems.at[1 + side, tile])

    def tile_out(s, tile):
        return tile_copy(shares.at[s], tile * SUB, results[s], tile * SUB, out_sems.at[s, tile])

    field_copies = window_fields((perm, perm_odd, perm_even), fields, first, count, rows, field_sems)
    present = [tile for tile in range(tiles + 2) if 0 <= base + tile * SUB < rows]
    for tile in range(tiles + 2):
        if tile in present:
            near_in(tile).start()
        if tile < tiles:
            halo_in(0, tile).start()
            halo_in(1, tile).start()
    clear_outside(first, count, rows, fields, [near])
    for copy in field_copies:
        copy.wait()
    own = near.reshape(mode_dev * size, nz)
    side_odd, side_even = halo.at[0].reshape(mode_dev * tall, nz), halo.at[1].reshape(mode_dev * tall, nz)
    parts = [shares.at[s].reshape(mode_dev * tall, nz) for s in range(groups)]
    face_coefs(coef, fields, SUB, count)
    lane = lax.broadcasted_iota(jnp.int32, (PACK, nz), 1)
    wide = groups * pad

    def build(store, row):
        high, low, mean = store
        for slot in range(2):
            lanes = pl.ds(slot * nz, nz)
            at = row + slot
            factor = factor_of(coef, at - first, terms, count)
            for block in range(pad // PACK):
                centre = mode_block(own, block, at - base, mode_dev, size)
                others = (
                    mode_block(side_odd, block, at - first, mode_dev, tall),
                    mode_block(side_even, block, at - first, mode_dev, tall),
                    mode_block(own, block, at + 1 - base, mode_dev, size),
                    mode_block(own, block, at - 1 - base, mode_dev, size),
                    jnp.where(lane < nz - 1, pltpu.roll(centre, nz - 1, 1), 0.0),
                    jnp.where(lane > 0, pltpu.roll(centre, 1, 1), 0.0),
                )
                steps = [centre - other for other in others]
                for k in range(terms):
                    total = factor(0, k) * steps[0]
                    for f in range(1, FACES):
                        total = total + factor(f, k) * steps[f]
                    if k == terms - 1:
                        mean[slot, pl.ds(block * PACK, PACK), :] = total
                    else:
                        place = pl.ds(k * pad + block * PACK, PACK)
                        high[place, lanes], low[place, lanes] = halves(total)

    def multiply(store, row):
        high, low, mean = store
        both = jnp.dot(weights[...], high[...], preferred_element_type=jnp.float32)
        rest = jnp.dot(weights[0:wide, :], low[...], preferred_element_type=jnp.float32)
        result = both[0:wide] + both[wide : 2 * wide] + rest
        for slot in range(2):
            lanes = slice(slot * nz, (slot + 1) * nz)
            for s, part in enumerate(parts):
                value = result[s * pad : (s + 1) * pad, lanes]
                if s == 0:
                    value = value + mean[slot]
                part[pl.ds(row + slot - first, mode_dev, stride=tall), :] = value[:mode_dev]

    for tile in (0, 1):
        if tile in present:
            near_in(tile).wait()
    halo_in(0, 0).wait()
    halo_in(1, 0).wait()
    build(even, first)

    def four_rows(step, carry):
        row = first + 4 * step
        multiply(even, row)
        build(odd, row + 2)
        multiply(odd, row + 2)
        build(even, jnp.minimum(row + 4, first + count - 2))
        return carry

    def tile_step(tile, carry):
        @pl.when(tile < (tiles if tiles + 1 in present else tiles - 1))
        def _():
            near_in(tile + 2).wait()

        @pl.when(tile + 1 < tiles)
        def _():
            halo_in(0, tile + 1).wait()
            halo_in(1, tile + 1).wait()

        lax.fori_loop(2 * tile, 2 * tile + 2, four_rows, 0)
        for s in range(groups):
            tile_out(s, tile).start()
        return carry

    lax.fori_loop(0, tiles, tile_step, 0)
    for tile in range(tiles):
        for s in range(groups):
            tile_out(s, tile).wait()


def place_sum(result, parts, first, shape):
    modes, count, nz = parts[0].shape
    kept = [] if result is None else [result]
    steps = next(n for n in (4, 3, 1) if modes % n == 0)
    some = modes // steps

    def kernel(*refs):
        sources = refs[len(kept) : len(kept) + len(parts)]
        out, near, total, in_sems, out_sems = refs[len(kept) + len(parts) :]
        copies_in = [
            [
                pltpu.make_async_copy(
                    source.at[pl.ds(step * some, some)], near.at[n, pl.ds(step * some, some)], in_sems.at[n, step]
                )
                for n, source in enumerate(sources)
            ]
            for step in range(steps)
        ]
        for copies in copies_in:
            for copy in copies:
                copy.start()
        copies_out = []
        for step, copies in enumerate(copies_in):
            here = pl.ds(step * some, some)
            for copy in copies:
                copy.wait()
            value = near[0, here]
            for n in range(1, len(parts)):
                value = value + near[n, here]
            total[here] = value
            copies_out.append(
                pltpu.make_async_copy(total.at[here], out.at[here, pl.ds(first, count), :], out_sems.at[step])
            )
            copies_out[-1].start()
        for copy in copies_out:
            copy.wait()

    return pl.pallas_call(
        kernel,
        in_specs=[ANY] * (len(kept) + len(parts)),
        out_specs=ANY,
        out_shape=jax.ShapeDtypeStruct(shape, jnp.float32),
        scratch_shapes=[
            pltpu.VMEM((len(parts), modes, count, nz), jnp.float32),
            pltpu.VMEM((modes, count, nz), jnp.float32),
            pltpu.SemaphoreType.DMA((len(parts), steps)),
            pltpu.SemaphoreType.DMA((steps,)),
        ],
        compiler_params=pltpu.CompilerParams(vmem_limit_bytes=LIMIT),
        input_output_aliases={0: 0} if kept else {},
        name="place",
    )(*kept, *parts)


def local(mode_coeffs, mean_perm, kl_fields, couplings):
    mode_dev, _, rows, nz = mode_coeffs.shape
    terms = kl_fields.shape[0] + 1
    groups = lax.axis_size("modes")
    planes = lax.axis_size("space")
    pad = pl.cdiv(mode_dev, PACK) * PACK
    group = lax.axis_index("modes")
    pairs = [
        [pair for i in range(start, planes - 1, 2) for pair in ((i, i + 1), (i + 1, i))] for start in (1, 0)
    ]
    own3 = mode_coeffs.reshape(mode_dev, rows, nz)

    def swapped(value, side):
        return lax.ppermute(value, "space", pairs[side])

    def rotated(value, step):
        return lax.ppermute(value, "modes", [(i, (i + step) % groups) for i in range(groups)])

    def block(row_group, column_group):
        piece = lax.dynamic_slice(
            couplings,
            (0, (row_group % groups) * mode_dev, (column_group % groups) * mode_dev),
            (terms - 1, mode_dev, mode_dev),
        )
        return jnp.pad(piece, ((0, 0), (0, pad - mode_dev), (0, pad - mode_dev)))

    def split(value):
        high = lax.reduce_precision(value, 8, 7)
        return high.astype(jnp.bfloat16), (value - high).astype(jnp.bfloat16)

    quarter = pl.cdiv(pl.cdiv(rows, 4), SUB) * SUB
    gathered = [(0, quarter), (quarter, quarter + SUB)]
    begin = 2 * quarter + SUB
    half = (rows - begin) // 2 // SUB * SUB
    partial = [(begin, half), (begin + half, rows - begin - half)]

    high, low = split(jnp.concatenate([block(group, group - s) for s in range(groups)], 2))
    gathered_weights = jnp.concatenate([high, high, low], 2).reshape((terms - 1) * pad, 3 * groups * pad)
    high, low = split(jnp.concatenate([block(group + s, group) for s in range(groups)], 1))
    partial_weights = (
        jnp.concatenate([high, low], 1).transpose(1, 0, 2).reshape(2 * groups * pad, (terms - 1) * pad)
    )

    perm = jnp.concatenate([kl_fields, mean_perm[None]], 0).reshape(terms, rows, nz)
    perm, ready = lax.optimization_barrier((perm, own3))
    bounds = [(0, gathered[1][0] + SUB), (gathered[1][0] + SUB, gathered[1][1])]
    piece, later_piece = [ready[:, start : start + length] for start, length in bounds]
    edge = ready[:, begin:]
    perm_odd, perm_even = swapped(perm, 0), swapped(perm, 1)
    arrived = [rotated(piece, s) for s in range(1, groups)]
    edge, perm_odd, perm_even, gathered_weights, partial_weights = lax.optimization_barrier(
        (edge, perm_odd, perm_even, gathered_weights, partial_weights)
    )
    halos = [swapped(edge, 0), swapped(edge, 1)]
    later_piece, arrived = lax.optimization_barrier((later_piece, arrived))
    received = [arrived, [rotated(later_piece, s) for s in range(1, groups)]]

    params = pltpu.CompilerParams(vmem_limit_bytes=LIMIT)
    f32 = jnp.float32
    result = None
    shape = (mode_dev, rows, nz)

    shares = []

    def window_scratch(count, around, inputs, outputs):
        size = count + 2 * SUB
        tiles = size // SUB
        return [
            pltpu.VMEM((3, terms, size, nz), f32),
            pltpu.SemaphoreType.DMA((3,)),
            pltpu.SemaphoreType.DMA((inputs, tiles)),
            pltpu.SemaphoreType.DMA((outputs, tiles)),
            pltpu.VMEM((FACES * terms * (count + around * SUB), nz), f32),
        ]

    def window_modes(count):
        return mode_dev, spaced(count + 2 * SUB), nz

    def cost(count):
        products = 3 * 2 * (terms - 1) * mode_dev * mode_dev * groups * count * nz
        return pl.CostEstimate(flops=products // 1024, bytes_accessed=2**10 * count, transcendentals=0)

    def partial_shares(index, source):
        first, count = partial[index]
        flat = jax.ShapeDtypeStruct((mode_dev, count, nz), f32)
        outs = pl.pallas_call(
            functools.partial(partial_kernel, first, count, rows, mode_dev, pad, groups, partial[0][0]),
            in_specs=[HBM] * 6 + [VMEM],
            out_specs=[HBM] * groups,
            out_shape=[flat] * groups,
            scratch_shapes=[pltpu.VMEM(window_modes(count), f32), pltpu.VMEM((2, mode_dev, spaced(count), nz), f32)]
            + window_scratch(count, 0, 3, groups)
            + [
                pltpu.VMEM(((terms - 1) * pad, 2 * nz), jnp.bfloat16),
                pltpu.VMEM(((terms - 1) * pad, 2 * nz), jnp.bfloat16),
                pltpu.VMEM((2, pad, nz), f32),
            ]
            * 2
            + [pltpu.VMEM((groups, mode_dev, spaced(count), nz), f32)],
            compiler_params=params,
            cost_estimate=cost(count),
            name="partial",
        )(source, *halos, perm, perm_odd, perm_even, partial_weights)
        parts = [outs[0]] + [rotated(value, s) for s, value in enumerate(outs[1:], 1)]
        return first, parts

    def gathered_shares(index, source):
        first, count = gathered[index]
        sources = bounds[: index + 1]
        pieces = [piece for group_pieces in received[: index + 1] for piece in group_pieces]
        flat = jax.ShapeDtypeStruct((mode_dev, count, nz), f32)
        centre, to_odd, to_even = pl.pallas_call(
            functools.partial(
                gathered_kernel, first, count, rows, mode_dev, pad, groups, sources
            ),
            in_specs=[HBM] * 4 + [VMEM] + [HBM] * len(pieces),
            out_specs=[HBM] * 3,
            out_shape=[flat] * 3,
            scratch_shapes=[pltpu.VMEM(window_modes(count), f32), pltpu.VMEM((groups - 1, *window_modes(count)), f32)]
            + window_scratch(count, 1, groups, 3)
            + [
                pltpu.VMEM((3 * groups * pad, 2 * nz), jnp.bfloat16),
                pltpu.VMEM(((terms - 1) * pad, 2 * nz), f32),
            ]
            * 2
            + [pltpu.VMEM((pad, nz), f32)] * 2
            + [pltpu.VMEM(window_modes(count), f32)] * 3,
            compiler_params=params,
            cost_estimate=cost(count),
            name="gathered",
        )(source, perm, perm_odd, perm_even, gathered_weights, *pieces)
        if index == 0:
            to_odd, to_even, *halos[:] = lax.optimization_barrier((to_odd, to_even, *halos))
        parts = [centre, swapped(to_odd, 0), swapped(to_even, 1)]
        return first, parts

    shares, source = [], own3
    for compute, index in ((gathered_shares, 0), (partial_shares, 0), (gathered_shares, 1), (partial_shares, 1)):
        if len(shares) == 3:
            source, shares[0][1][1:], shares[1][1][1:] = lax.optimization_barrier(
                (source, shares[0][1][1:], shares[1][1][1:])
            )
        share = compute(index, source)
        source, share[1][0] = lax.optimization_barrier((source, share[1][0]))
        shares.append(share)
    shares.append(shares.pop(2))
    for first, parts in shares:
        result = place_sum(result, parts, first, shape)
    return result.reshape(mode_coeffs.shape)


def solution(mesh):
    in_specs = (
        P("modes", "space", None, None),
        P("space", None, None),
        P(None, "space", None, None),
        P(),
    )
    out_specs = P("modes", "space", None, None)
    return jax.shard_map(local, mesh=mesh, in_specs=in_specs, out_specs=out_specs, check_vma=False)
```

time: 127 us -> 117 us (0.921)
  the two profiles are of different devices: /device:TPU:17 before, /device:TPU:0 now
where the time goes in v3:
time: 117 us
  Pallas kernels  46.9 us (40%)
  waiting for transfers between devices  28.6 us (24%)
  starting transfers between devices  27.2 us (23%)
  local copies, waits for them, and re-layouts  11.5 us (10%)
  other arithmetic  2.13 us (2%)
    ppermute x4, waiting for transfers between devices, rotated(): lax.ppermute(value, 'modes', [(i, (i + step) % groups) for i in range(gro...  28.6 us
    pallas_call x2, Pallas kernels, gathered_shares(): pl.pallas_call(functools.partial(gathered_kernel, first, count, rows, mod...  22.3 us
    ppermute x8, starting transfers between devices, swapped(): return lax.ppermute(value, 'space', pairs[side])  18.9 us
    pallas_call x2, Pallas kernels, partial_shares(): pl.pallas_call(functools.partial(partial_kernel, first, count, rows, mode...  13.5 us
    pallas_call x4, Pallas kernels, place_sum(): pl.pallas_call(kernel, in_specs=[ANY] * (len(kept) + len(parts)), out_spe...  11.1 us
    ppermute x4, starting transfers between devices, rotated(): lax.ppermute(value, 'modes', [(i, (i + step) % groups) for i in range(gro...  8.23 us
    unnamed x14, local copies, waits for them, and re-layouts  4.14 us
    slice x1, local copies, waits for them, and re-layouts, local(): ready[:, start:start + length]  3.25 us
  transfers between devices with their start and end apart: 12, of which 3 were waited for; matrix products, arithmetic and copies ran while one was open for 7% of the time, Pallas kernels for 38%

profile of v3, /device:TPU:0, one launch (start us, length us, event | category | flops | bytes accessed | tf_op | source)
XLA Modules:
  0.0 116.5 jit_solution(17760798143716240141)
XLA Ops:
  0.0 1.1 maximum_bitcast_fusion.refs_1_.refs_3_
  2.3 3.2 %fusion.2 = (f32[60,40,128]{2,1,0:T(8,128)}, f32[60,40,128]{2,1,0:T(8,128)}) fusion(f32[60,120,128]{2,1,0:T(8,128)} %bitcast.13), kind=kLoop, calls=%fused_computation.15 | loop fusion | bytes 4915200 | tf_op jit(solution)/shard_map/slice | solution.py:436
  5.5 2.6 %collective-permute-start.2 = (f32[60,40,128]{2,1,0:T(8,128)}, f32[60,40,128]{2,1,0:T(8,128)}, u32[]{:S(2)}, u32[]{:S(2)}) collective-permute-start(f32[60,40,128]{2,1,0:T(8,128)} %get-tuple-element.73), channel_id=1, source_target_pairs={{0,16},{16,0},{1,17},{17,1},{2,18},{18,2},{3,19},{19,3},{4,20},{20... | collective-permute-start | bytes 3686408 | tf_op jit(solution)/shard_map/ppermute | solution.py:406
  8.4 2.6 %slice.9 = f32[60,48,128]{2,1,0:T(8,128)} slice(f32[60,120,128]{2,1,0:T(8,128)} %bitcast.14), slice={[0:60], [72:120], [0:128]} | slice | bytes 2949120 | tf_op jit(solution)/shard_map/slice | solution.py:437
  13.0 4.3 %collective-permute-start.4 = (f32[60,48,128]{2,1,0:T(8,128)S(1)}, f32[60,48,128]{2,1,0:T(8,128)S(1)}, u32[]{:S(2)}, u32[]{:S(2)}) collective-permute-start(f32[60,48,128]{2,1,0:T(8,128)S(1)} %copy-done.4), channel_id=1, source_target_pairs={{0,1},{1,0},{2,3},{3,2},{4,5},{5,4},{6,7},{7,6},{8,9},{9,8},{10,11... | collective-permute-start | bytes 4423688 | tf_op jit(solution)/shard_map/ppermute | solution.py:403
  18.1 15.9 %collective-permute-done.2.refs_5_ = f32[60,40,128]{2,1,0:T(8,128)} collective-permute-done((f32[60,40,128]{2,1,0:T(8,128)}, f32[60,40,128]{2,1,0:T(8,128)}, u32[]{:S(2)}, u32[]{:S(2)}) %collective-permute-start.2) | collective-permute-done | bytes 1228832 | tf_op jit(solution)/shard_map/ppermute | solution.py:406
  34.0 2.5 %collective-permute-start.5 = (f32[60,40,128]{2,1,0:T(8,128)}, f32[60,40,128]{2,1,0:T(8,128)}, u32[]{:S(2)}, u32[]{:S(2)}) collective-permute-start(f32[60,40,128]{2,1,0:T(8,128)} %get-tuple-element.56), channel_id=1, source_target_pairs={{0,16},{16,0},{1,17},{17,1},{2,18},{18,2},{3,19},{19,3},{4,20},{20... | collective-permute-start | bytes 3686408 | tf_op jit(solution)/shard_map/ppermute | solution.py:406
  36.5 10.1 %gathered.2 = (f32[60,32,128]{2,1,0:T(8,128)S(1)}, f32[60,32,128]{2,1,0:T(8,128)}, f32[60,32,128]{2,1,0:T(8,128)}) custom-call(f32[60,120,128]{2,1,0:T(8,128)} %bitcast.15, f32[8,120,128]{2,1,0:T(8,128)S(1)} %maximum_bitcast_fusion.refs_1_.refs_3_, f32[8,120,128]{2,1,0:T(8,128)S(1)} %collective-permute-done.refs_2_.refs_4_, ...), custom_call_target="tpu_custom_call" | custom-call | flops 1209600 | bytes 32768 | tf_op jit(solution)/shard_map/gathered/pallas_call | solution.py:501
  47.6 1.1 copy-done
  48.7 1.6 %collective-permute-start.6 = (f32[60,32,128]{2,1,0:T(8,128)}, f32[60,32,128]{2,1,0:T(8,128)}, u32[]{:S(2)}, u32[]{:S(2)}) collective-permute-start(f32[60,32,128]{2,1,0:T(8,128)} %get-tuple-element.59), channel_id=1, source_target_pairs={{1,2},{2,1},{3,4},{4,3},{5,6},{6,5},{7,8},{8,7},{9,10},{10,9},{11,... | collective-permute-start | bytes 2949128 | tf_op jit(solution)/shard_map/ppermute | solution.py:403
  50.3 9.1 %collective-permute-start.7 = (f32[60,32,128]{2,1,0:T(8,128)}, f32[60,32,128]{2,1,0:T(8,128)}, u32[]{:S(2)}, u32[]{:S(2)}) collective-permute-start(f32[60,32,128]{2,1,0:T(8,128)} %get-tuple-element.60), channel_id=1, source_target_pairs={{0,1},{1,0},{2,3},{3,2},{4,5},{5,4},{6,7},{7,6},{8,9},{9,8},{10,11... | collective-permute-start | bytes 2949128 | tf_op jit(solution)/shard_map/ppermute | solution.py:403
  60.5 1.4 %copy-done.1 = f32[60,48,128]{2,1,0:T(8,128)S(1)} copy-done((f32[60,48,128]{2,1,0:T(8,128)S(1)}, f32[60,48,128]{2,1,0:T(8,128)}, u32[]{:S(2)}) %copy-start.1) | copy-done | bytes 1474584
  61.8 6.8 %partial.2 = (f32[60,24,128]{2,1,0:T(8,128)S(1)}, f32[60,24,128]{2,1,0:T(8,128)S(1)}) custom-call(f32[60,120,128]{2,1,0:T(8,128)} %bitcast.16, f32[60,48,128]{2,1,0:T(8,128)S(1)} %copy-done.1, f32[60,48,128]{2,1,0:T(8,128)S(1)} %collective-permute-done.4.refs_2_, f32[8,120,128]{2,1,0:T(8,128)S(1)} %maximum_bitcast_fusion.refs_1_.refs_3_, ...), custom_call_target="tpu_custom_call" | custom-call | flops 907200 | bytes 24576 | tf_op jit(solution)/shard_map/partial/pallas_call | solution.py:475
  68.6 1.6 %collective-permute-start.8 = (f32[60,24,128]{2,1,0:T(8,128)S(1)}, f32[60,24,128]{2,1,0:T(8,128)S(1)}, u32[]{:S(2)}, u32[]{:S(2)}) collective-permute-start(f32[60,24,128]{2,1,0:T(8,128)S(1)} %get-tuple-element.61), channel_id=1, source_target_pairs={{0,16},{16,0},{1,17},{17,1},{2,18},{18,2},{3,19},{19,3},{4,20},{20... | collective-permute-start | bytes 2211848 | tf_op jit(solution)/shard_map/ppermute | solution.py:406
  70.2 12.1 %gathered.3 = (f32[60,40,128]{2,1,0:T(8,128)S(1)}, f32[60,40,128]{2,1,0:T(8,128)}, f32[60,40,128]{2,1,0:T(8,128)S(1)}) custom-call(f32[60,120,128]{2,1,0:T(8,128)} %bitcast.17, f32[8,120,128]{2,1,0:T(8,128)S(1)} %maximum_bitcast_fusion.refs_1_.refs_3_, f32[8,120,128]{2,1,0:T(8,128)S(1)} %collective-permute-done.refs_2_.refs_4_, ...), custom_call_target="tpu_custom_call" | custom-call | flops 1512000 | bytes 40960 | tf_op jit(solution)/shard_map/gathered/pallas_call | solution.py:501
  83.0 1.3 %collective-permute-start.11 = (f32[60,40,128]{2,1,0:T(8,128)S(1)}, f32[60,40,128]{2,1,0:T(8,128)S(1)}, u32[]{:S(2)}, u32[]{:S(2)}) collective-permute-start(f32[60,40,128]{2,1,0:T(8,128)S(1)} %get-tuple-element.72), channel_id=1, source_target_pairs={{0,1},{1,0},{2,3},{3,2},{4,5},{5,4},{6,7},{7,6},{8,9},{9,8},{10,11... | collective-permute-start | bytes 3686408 | tf_op jit(solution)/shard_map/ppermute | solution.py:403
  84.3 2.8 %collective-permute-done.8.refs_2_ = f32[60,24,128]{2,1,0:T(8,128)S(1)} collective-permute-done((f32[60,24,128]{2,1,0:T(8,128)S(1)}, f32[60,24,128]{2,1,0:T(8,128)S(1)}, u32[]{:S(2)}, u32[]{:S(2)}) %collective-permute-start.8) | collective-permute-done | bytes 737312 | tf_op jit(solution)/shard_map/ppermute | solution.py:406
  87.1 6.8 %partial.3 = (f32[60,24,128]{2,1,0:T(8,128)S(1)}, f32[60,24,128]{2,1,0:T(8,128)S(1)}) custom-call(f32[60,120,128]{2,1,0:T(8,128)} %bitcast.18, f32[60,48,128]{2,1,0:T(8,128)S(1)} %copy-done.1, f32[60,48,128]{2,1,0:T(8,128)S(1)} %collective-permute-done.4.refs_2_, f32[8,120,128]{2,1,0:T(8,128)S(1)} %maximum_bitcast_fusion.refs_1_.refs_3_, ...), custom_call_target="tpu_custom_call" | custom-call | flops 907200 | bytes 24576 | tf_op jit(solution)/shard_map/partial/pallas_call | solution.py:475
  93.9 1.5 %collective-permute-start.9 = (f32[60,24,128]{2,1,0:T(8,128)S(1)}, f32[60,24,128]{2,1,0:T(8,128)S(1)}, u32[]{:S(2)}, u32[]{:S(2)}) collective-permute-start(f32[60,24,128]{2,1,0:T(8,128)S(1)} %get-tuple-element.69), channel_id=1, source_target_pairs={{0,16},{16,0},{1,17},{17,1},{2,18},{18,2},{3,19},{19,3},{4,20},{20... | collective-permute-start | bytes 2211848 | tf_op jit(solution)/shard_map/ppermute | solution.py:406
  95.4 3.2 %place.4.refs_0_ = f32[60,120,128]{2,1,0:T(8,128)} custom-call(f32[60,32,128]{2,1,0:T(8,128)S(1)} %copy-done.3, f32[60,32,128]{2,1,0:T(8,128)} %collective-permute-done.6.refs_1_, f32[60,32,128]{2,1,0:T(8,128)} %collective-permute-done.7.refs_2_), custom_call_target="tpu_custom_call" | custom-call | tf_op jit(solution)/shard_map/place/pallas_call | solution.py:373
  98.7 2.9 %place.5.refs_0_ = f32[60,120,128]{2,1,0:T(8,128)} custom-call(f32[60,120,128]{2,1,0:T(8,128)} %place.4.refs_0_, f32[60,24,128]{2,1,0:T(8,128)S(1)} %get-tuple-element.64.refs_1_, f32[60,24,128]{2,1,0:T(8,128)S(1)} %collective-permute-done.8.refs_2_), custom_call_target="tpu_custom_call", output_to_operand_aliasing={{}: (0, {})} | custom-call | tf_op jit(solution)/shard_map/place/pallas_call | solution.py:373
  101.6 9.9 %collective-permute-done.9.refs_2_ = f32[60,24,128]{2,1,0:T(8,128)S(1)} collective-permute-done((f32[60,24,128]{2,1,0:T(8,128)S(1)}, f32[60,24,128]{2,1,0:T(8,128)S(1)}, u32[]{:S(2)}, u32[]{:S(2)}) %collective-permute-start.9) | collective-permute-done | bytes 737312 | tf_op jit(solution)/shard_map/ppermute | solution.py:406
  111.5 2.9 %place.6.refs_0_ = f32[60,120,128]{2,1,0:T(8,128)} custom-call(f32[60,120,128]{2,1,0:T(8,128)} %place.5.refs_0_, f32[60,24,128]{2,1,0:T(8,128)S(1)} %get-tuple-element.68.refs_1_, f32[60,24,128]{2,1,0:T(8,128)S(1)} %collective-permute-done.9.refs_2_), custom_call_target="tpu_custom_call", output_to_operand_aliasing={{}: (0, {})} | custom-call | tf_op jit(solution)/shard_map/place/pallas_call | solution.py:373
  114.4 2.1 %place.7 = f32[60,120,128]{2,1,0:T(8,128)} custom-call(f32[60,120,128]{2,1,0:T(8,128)} %place.6.refs_0_, f32[60,40,128]{2,1,0:T(8,128)S(1)} %get-tuple-element.70.refs_1_, f32[60,40,128]{2,1,0:T(8,128)S(1)} %collective-permute-done.10.refs_2_, f32[60,40,128]{2,1,0:T(8,128)S(1)} %collective-permute-done.11.refs_3_), custom_call_target="tpu_custom_call", output_to_operand_aliasing={{}: (0, {})} | custom-call | tf_op jit(solution)/shard_map/place/pallas_call | solution.py:373
  (34 shorter events, 6.9 us)
Async XLA Ops:
  1.1 7.1 %copy-start.5 = (f32[7,120,120]{2,1,0:T(8,128)S(1)}, f32[7,120,120]{2,1,0:T(8,128)}, u32[]{:S(2)}) copy-start(f32[7,120,120]{2,1,0:T(8,128)} %param.7) | copy-start | bytes 1209604
  1.1 11.6 %collective-permute-start.1 = (f32[8,120,128]{2,1,0:T(8,128)S(1)}, f32[8,120,128]{2,1,0:T(8,128)S(1)}, u32[]{:S(2)}, u32[]{:S(2)}) collective-permute-start(f32[8,120,128]{2,1,0:T(8,128)S(1)} %maximum_bitcast_fusion.refs_1_.refs_3_), channel_id=1, source_target_pairs={{0,1},{1,0},{2,3},{3,2},{4,5},{5,4},{6,7},{7,6},{8,9},{9,8},{10,11... | collective-permute-start | bytes 1474568 | tf_op jit(solution)/shard_map/ppermute | solution.py:403
  1.6 11.0 %collective-permute-start = (f32[8,120,128]{2,1,0:T(8,128)S(1)}, f32[8,120,128]{2,1,0:T(8,128)S(1)}, u32[]{:S(2)}, u32[]{:S(2)}) collective-permute-start(f32[8,120,128]{2,1,0:T(8,128)S(1)} %maximum_bitcast_fusion.refs_1_.refs_3_), channel_id=1, source_target_pairs={{1,2},{2,1},{3,4},{4,3},{5,6},{6,5},{7,8},{8,7},{9,10},{10,9},{11,... | collective-permute-start | bytes 1474568 | tf_op jit(solution)/shard_map/ppermute | solution.py:403
  5.5 28.4 %collective-permute-start.2 = (f32[60,40,128]{2,1,0:T(8,128)}, f32[60,40,128]{2,1,0:T(8,128)}, u32[]{:S(2)}, u32[]{:S(2)}) collective-permute-start(f32[60,40,128]{2,1,0:T(8,128)} %get-tuple-element.73), channel_id=1, source_target_pairs={{0,16},{16,0},{1,17},{17,1},{2,18},{18,2},{3,19},{19,3},{4,20},{20... | collective-permute-start | bytes 3686408 | tf_op jit(solution)/shard_map/ppermute | solution.py:406
  11.6 1.5 %copy-start.4 = (f32[60,48,128]{2,1,0:T(8,128)S(1)}, f32[60,48,128]{2,1,0:T(8,128)}, u32[]{:S(2)}) copy-start(f32[60,48,128]{2,1,0:T(8,128)} %slice.9) | copy-start | bytes 4423684
  13.0 34.5 %collective-permute-start.4 = (f32[60,48,128]{2,1,0:T(8,128)S(1)}, f32[60,48,128]{2,1,0:T(8,128)S(1)}, u32[]{:S(2)}, u32[]{:S(2)}) collective-permute-start(f32[60,48,128]{2,1,0:T(8,128)S(1)} %copy-done.4), channel_id=1, source_target_pairs={{0,1},{1,0},{2,3},{3,2},{4,5},{5,4},{6,7},{7,6},{8,9},{9,8},{10,11... | collective-permute-start | bytes 4423688 | tf_op jit(solution)/shard_map/ppermute | solution.py:403
  17.3 30.2 %collective-permute-start.3 = (f32[60,48,128]{2,1,0:T(8,128)S(1)}, f32[60,48,128]{2,1,0:T(8,128)S(1)}, u32[]{:S(2)}, u32[]{:S(2)}) collective-permute-start(f32[60,48,128]{2,1,0:T(8,128)S(1)} %copy-done.4), channel_id=1, source_target_pairs={{1,2},{2,1},{3,4},{4,3},{5,6},{6,5},{7,8},{8,7},{9,10},{10,9},{11,... | collective-permute-start | bytes 4423688 | tf_op jit(solution)/shard_map/ppermute | solution.py:403
  34.0 36.2 %collective-permute-start.5 = (f32[60,40,128]{2,1,0:T(8,128)}, f32[60,40,128]{2,1,0:T(8,128)}, u32[]{:S(2)}, u32[]{:S(2)}) collective-permute-start(f32[60,40,128]{2,1,0:T(8,128)} %get-tuple-element.56), channel_id=1, source_target_pairs={{0,16},{16,0},{1,17},{17,1},{2,18},{18,2},{3,19},{19,3},{4,20},{20... | collective-permute-start | bytes 3686408 | tf_op jit(solution)/shard_map/ppermute | solution.py:406
  46.6 1.0 copy-start.2
  47.6 1.1 copy-start
  48.7 38.4 %collective-permute-start.6 = (f32[60,32,128]{2,1,0:T(8,128)}, f32[60,32,128]{2,1,0:T(8,128)}, u32[]{:S(2)}, u32[]{:S(2)}) collective-permute-start(f32[60,32,128]{2,1,0:T(8,128)} %get-tuple-element.59), channel_id=1, source_target_pairs={{1,2},{2,1},{3,4},{4,3},{5,6},{6,5},{7,8},{8,7},{9,10},{10,9},{11,... | collective-permute-start | bytes 2949128 | tf_op jit(solution)/shard_map/ppermute | solution.py:403
  50.3 36.8 %collective-permute-start.7 = (f32[60,32,128]{2,1,0:T(8,128)}, f32[60,32,128]{2,1,0:T(8,128)}, u32[]{:S(2)}, u32[]{:S(2)}) collective-permute-start(f32[60,32,128]{2,1,0:T(8,128)} %get-tuple-element.60), channel_id=1, source_target_pairs={{0,1},{1,0},{2,3},{3,2},{4,5},{5,4},{6,7},{7,6},{8,9},{9,8},{10,11... | collective-permute-start | bytes 2949128 | tf_op jit(solution)/shard_map/ppermute | solution.py:403
  60.4 1.4 %copy-start.1 = (f32[60,48,128]{2,1,0:T(8,128)S(1)}, f32[60,48,128]{2,1,0:T(8,128)}, u32[]{:S(2)}) copy-start(f32[60,48,128]{2,1,0:T(8,128)} %copy-done) | copy-start | bytes 4423684
  68.6 18.5 %collective-permute-start.8 = (f32[60,24,128]{2,1,0:T(8,128)S(1)}, f32[60,24,128]{2,1,0:T(8,128)S(1)}, u32[]{:S(2)}, u32[]{:S(2)}) collective-permute-start(f32[60,24,128]{2,1,0:T(8,128)S(1)} %get-tuple-element.61), channel_id=1, source_target_pairs={{0,16},{16,0},{1,17},{17,1},{2,18},{18,2},{3,19},{19,3},{4,20},{20... | collective-permute-start | bytes 2211848 | tf_op jit(solution)/shard_map/ppermute | solution.py:406
  82.3 32.1 %collective-permute-start.10 = (f32[60,40,128]{2,1,0:T(8,128)}, f32[60,40,128]{2,1,0:T(8,128)S(1)}, u32[]{:S(2)}, u32[]{:S(2)}) collective-permute-start(f32[60,40,128]{2,1,0:T(8,128)} %get-tuple-element.71), channel_id=1, source_target_pairs={{1,2},{2,1},{3,4},{4,3},{5,6},{6,5},{7,8},{8,7},{9,10},{10,9},{11,... | collective-permute-start | bytes 3686408 | tf_op jit(solution)/shard_map/ppermute | solution.py:403
  83.0 31.3 %collective-permute-start.11 = (f32[60,40,128]{2,1,0:T(8,128)S(1)}, f32[60,40,128]{2,1,0:T(8,128)S(1)}, u32[]{:S(2)}, u32[]{:S(2)}) collective-permute-start(f32[60,40,128]{2,1,0:T(8,128)S(1)} %get-tuple-element.72), channel_id=1, source_target_pairs={{0,1},{1,0},{2,3},{3,2},{4,5},{5,4},{6,7},{7,6},{8,9},{9,8},{10,11... | collective-permute-start | bytes 3686408 | tf_op jit(solution)/shard_map/ppermute | solution.py:403
  84.3 11.1 %copy-start.3 = (f32[60,32,128]{2,1,0:T(8,128)S(1)}, f32[60,32,128]{2,1,0:T(8,128)}, u32[]{:S(2)}) copy-start(f32[60,32,128]{2,1,0:T(8,128)} %copy-done.2) | copy-start | bytes 2949124
  93.9 17.6 %collective-permute-start.9 = (f32[60,24,128]{2,1,0:T(8,128)S(1)}, f32[60,24,128]{2,1,0:T(8,128)S(1)}, u32[]{:S(2)}, u32[]{:S(2)}) collective-permute-start(f32[60,24,128]{2,1,0:T(8,128)S(1)} %get-tuple-element.69), channel_id=1, source_target_pairs={{0,16},{16,0},{1,17},{17,1},{2,18},{18,2},{3,19},{19,3},{4,20},{20... | collective-permute-start | bytes 2211848 | tf_op jit(solution)/shard_map/ppermute | solution.py:406

commit v4 on v3

--- a/solution.py
+++ b/solution.py
@@ -8,6 +8,7 @@
 from jax.sharding import PartitionSpec as P
 
 SUB = 8
+AHEAD = 3
 PACK = 16
 FACES = 6
 LIMIT = 48 * 2**20
@@ -120,9 +121,13 @@
     present = [tile for tile in range(tiles + 2) if 0 <= base + tile * SUB < rows]
     latest = len(sources) - 1
     early = {tile: max(latest - 1, 0) if tile < 2 else latest for tile in present}
+    def start_in(tile, index):
+        for s in range(groups):
+            tile_in(s, tile, index).start()
+
     for tile in present:
-        for s in range(groups):
-            tile_in(s, tile, early[tile]).start()
+        if tile < AHEAD:
+            start_in(tile, early[tile])
     clear_outside(first, count, rows, fields, windows)
     for copy in field_copies:
         copy.wait()
@@ -197,7 +202,11 @@
         return carry
 
     def tile_step(tile, carry):
-        @pl.when(tile < (tiles if tiles + 1 in present else tiles - 1))
+        @pl.when(tile + AHEAD <= present[-1])
+        def _():
+            start_in(tile + AHEAD, latest)
+
+        @pl.when(tile + 2 <= present[-1])
         def _():
             wait_in(tile + 2, latest)
 
@@ -222,7 +231,7 @@
 def partial_kernel(first, count, rows, mode_dev, pad, groups, halo_first, *refs):
     own_all, odd_all, even_all, perm, perm_odd, perm_even, weights = refs[:7]
     results = refs[7 : 7 + groups]
-    near, halo, fields, field_sems, in_sems, out_sems, coef, high_even, low_even, mean_even, high_odd, low_odd, mean_odd, shares = refs[7 + groups :]
+    near, halo, fields, field_sems, in_sems, out_sems, coef, high_even, low_even, mean_even, high_odd, low_odd, mean_odd, shares, table = refs[7 + groups :]
     even, odd = (high_even, low_even, mean_even), (high_odd, low_odd, mean_odd)
     terms, nz = fields.shape[1], fields.shape[3]
     base, size = first - SUB, near.shape[1]
@@ -241,13 +250,18 @@
 
     field_copies = window_fields((perm, perm_odd, perm_even), fields, first, count, rows, field_sems)
     present = [tile for tile in range(tiles + 2) if 0 <= base + tile * SUB < rows]
-    for tile in range(tiles + 2):
+    def start_halos(tile):
+        halo_in(0, tile).start()
+        halo_in(1, tile).start()
+
+    for tile in range(AHEAD):
         if tile in present:
             near_in(tile).start()
-        if tile < tiles:
-            halo_in(0, tile).start()
-            halo_in(1, tile).start()
+        if tile < min(AHEAD - 1, tiles):
+            start_halos(tile)
     clear_outside(first, count, rows, fields, [near])
+    for k in range(weights.shape[0]):
+        table[:, k * pad : (k + 1) * pad] = weights[k]
     for copy in field_copies:
         copy.wait()
     own = near.reshape(mode_dev * size, nz)
@@ -286,8 +300,8 @@
 
     def multiply(store, row):
         high, low, mean = store
-        both = jnp.dot(weights[...], high[...], preferred_element_type=jnp.float32)
-        rest = jnp.dot(weights[0:wide, :], low[...], preferred_element_type=jnp.float32)
+        both = jnp.dot(table[...], high[...], preferred_element_type=jnp.float32)
+        rest = jnp.dot(table[0:wide, :], low[...], preferred_element_type=jnp.float32)
         result = both[0:wide] + both[wide : 2 * wide] + rest
         for slot in range(2):
             lanes = slice(slot * nz, (slot + 1) * nz)
@@ -313,7 +327,15 @@
         return carry
 
     def tile_step(tile, carry):
-        @pl.when(tile < (tiles if tiles + 1 in present else tiles - 1))
+        @pl.when(tile + AHEAD <= present[-1])
+        def _():
+            near_in(tile + AHEAD).start()
+
+        @pl.when(tile + AHEAD - 1 < tiles)
+        def _():
+            start_halos(tile + AHEAD - 1)
+
+        @pl.when(tile + 2 <= present[-1])
         def _():
             near_in(tile + 2).wait()
 
@@ -333,38 +355,39 @@
             tile_out(s, tile).wait()
 
 
-def place_sum(result, parts, first, shape):
-    modes, count, nz = parts[0].shape
+def place_sums(result, shares, shape):
+    modes, _, nz = shape
     kept = [] if result is None else [result]
     steps = next(n for n in (4, 3, 1) if modes % n == 0)
     some = modes // steps
+    flat = [part for _, parts in shares for part in parts]
 
     def kernel(*refs):
-        sources = refs[len(kept) : len(kept) + len(parts)]
-        out, near, total, in_sems, out_sems = refs[len(kept) + len(parts) :]
-        copies_in = [
-            [
-                pltpu.make_async_copy(
-                    source.at[pl.ds(step * some, some)], near.at[n, pl.ds(step * some, some)], in_sems.at[n, step]
-                )
-                for n, source in enumerate(sources)
-            ]
-            for step in range(steps)
-        ]
-        for copies in copies_in:
-            for copy in copies:
-                copy.start()
-        copies_out = []
-        for step, copies in enumerate(copies_in):
+        sources = refs[len(kept) : len(kept) + len(flat)]
+        out, *scratch = refs[len(kept) + len(flat) :]
+        in_sems, out_sems = scratch[-2:]
+        jobs, copies_out = [], []
+        for step in range(steps):
             here = pl.ds(step * some, some)
+            n = 0
+            for (first, parts), total in zip(shares, scratch[len(flat) :]):
+                copies = [
+                    pltpu.make_async_copy(sources[m].at[here], scratch[m].at[here], in_sems.at[m, step])
+                    for m in range(n, n + len(parts))
+                ]
+                for copy in copies:
+                    copy.start()
+                jobs.append((step, here, first, parts[0].shape[1], n, copies, total))
+                n += len(parts)
+        for number, (step, here, first, count, n, copies, total) in enumerate(jobs):
             for copy in copies:
                 copy.wait()
-            value = near[0, here]
-            for n in range(1, len(parts)):
-                value = value + near[n, here]
+            value = scratch[n][here]
+            for m in range(n + 1, n + len(copies)):
+                value = value + scratch[m][here]
             total[here] = value
             copies_out.append(
-                pltpu.make_async_copy(total.at[here], out.at[here, pl.ds(first, count), :], out_sems.at[step])
+                pltpu.make_async_copy(total.at[here], out.at[here, pl.ds(first, count), :], out_sems.at[number])
             )
             copies_out[-1].start()
         for copy in copies_out:
@@ -372,19 +395,16 @@
 
     return pl.pallas_call(
         kernel,
-        in_specs=[ANY] * (len(kept) + len(parts)),
+        in_specs=[ANY] * (len(kept) + len(flat)),
         out_specs=ANY,
         out_shape=jax.ShapeDtypeStruct(shape, jnp.float32),
-        scratch_shapes=[
-            pltpu.VMEM((len(parts), modes, count, nz), jnp.float32),
-            pltpu.VMEM((modes, count, nz), jnp.float32),
-            pltpu.SemaphoreType.DMA((len(parts), steps)),
-            pltpu.SemaphoreType.DMA((steps,)),
-        ],
+        scratch_shapes=[pltpu.VMEM(part.shape, jnp.float32) for part in flat]
+        + [pltpu.VMEM(parts[0].shape, jnp.float32) for _, parts in shares]
+        + [pltpu.SemaphoreType.DMA((len(flat), steps)), pltpu.SemaphoreType.DMA((steps * len(shares),))],
         compiler_params=pltpu.CompilerParams(vmem_limit_bytes=LIMIT),
         input_output_aliases={0: 0} if kept else {},
         name="place",
-    )(*kept, *parts)
+    )(*kept, *flat)
 
 
 def local(mode_coeffs, mean_perm, kl_fields, couplings):
@@ -426,9 +446,7 @@
     high, low = split(jnp.concatenate([block(group, group - s) for s in range(groups)], 2))
     gathered_weights = jnp.concatenate([high, high, low], 2).reshape((terms - 1) * pad, 3 * groups * pad)
     high, low = split(jnp.concatenate([block(group + s, group) for s in range(groups)], 1))
-    partial_weights = (
-        jnp.concatenate([high, low], 1).transpose(1, 0, 2).reshape(2 * groups * pad, (terms - 1) * pad)
-    )
+    partial_weights = jnp.concatenate([high, low], 1)
 
     perm = jnp.concatenate([kl_fields, mean_perm[None]], 0).reshape(terms, rows, nz)
     perm, ready = lax.optimization_barrier((perm, own3))
@@ -446,7 +464,6 @@
 
     params = pltpu.CompilerParams(vmem_limit_bytes=LIMIT)
     f32 = jnp.float32
-    result = None
     shape = (mode_dev, rows, nz)
 
     shares = []
@@ -485,7 +502,10 @@
                 pltpu.VMEM((2, pad, nz), f32),
             ]
             * 2
-            + [pltpu.VMEM((groups, mode_dev, spaced(count), nz), f32)],
+            + [
+                pltpu.VMEM((groups, mode_dev, spaced(count), nz), f32),
+                pltpu.VMEM((2 * groups * pad, (terms - 1) * pad), jnp.bfloat16),
+            ],
             compiler_params=params,
             cost_estimate=cost(count),
             name="partial",
@@ -532,9 +552,8 @@
         share = compute(index, source)
         source, share[1][0] = lax.optimization_barrier((source, share[1][0]))
         shares.append(share)
-    shares.append(shares.pop(2))
-    for first, parts in shares:
-        result = place_sum(result, parts, first, shape)
+    result = place_sums(None, shares[:2], shape)
+    result = place_sums(result, shares[2:], shape)
     return result.reshape(mode_coeffs.shape)
 
 

time: 117 us -> 115 us (0.983)
  the two profiles are of different devices: /device:TPU:0 before, /device:TPU:17 now
where the time goes in v4:
time: 115 us
  Pallas kernels  48.4 us (42%)
  waiting for transfers between devices  40.5 us (35%)
  starting transfers between devices  18.4 us (16%)
  local copies, waits for them, and re-layouts  6.1 us (5%)
  other arithmetic  1.44 us (1%)
    ppermute x8, waiting for transfers between devices, swapped(): return lax.ppermute(value, 'space', pairs[side])  24 us
    pallas_call x2, Pallas kernels, gathered_shares(): pl.pallas_call(functools.partial(gathered_kernel, first, count, rows, mod...  22.3 us
    ppermute x4, waiting for transfers between devices, rotated(): lax.ppermute(value, 'modes', [(i, (i + step) % groups) for i in range(gro...  16.5 us
    pallas_call x2, Pallas kernels, partial_shares(): pl.pallas_call(functools.partial(partial_kernel, first, count, rows, mode...  14.6 us
    ppermute x8, starting transfers between devices, swapped(): return lax.ppermute(value, 'space', pairs[side])  13.4 us
    pallas_call x2, Pallas kernels, place_sums(): pl.pallas_call(kernel, in_specs=[ANY] * (len(kept) + len(flat)), out_spec...  11.5 us
    ppermute x4, starting transfers between devices, rotated(): lax.ppermute(value, 'modes', [(i, (i + step) % groups) for i in range(gro...  4.98 us
    slice x1, local copies, waits for them, and re-layouts, local(): ready[:, start:start + length]  3.27 us
  transfers between devices with their start and end apart: 12, of which 4 were waited for; matrix products, arithmetic and copies ran while one was open for 5% of the time, Pallas kernels for 38%

profile of v4, /device:TPU:17, one launch (start us, length us, event | category | flops | bytes accessed | tf_op | source)
XLA Modules:
  0.0 115.0 jit_solution(13439639836816497225)
XLA Ops:
  0.0 1.1 maximum_bitcast_fusion.refs_1_.refs_3_
  1.1 0.7 collective-permute-start.1
  1.8 3.2 %collective-permute-start = (f32[8,120,128]{2,1,0:T(8,128)S(1)}, f32[8,120,128]{2,1,0:T(8,128)S(1)}, u32[]{:S(2)}, u32[]{:S(2)}) collective-permute-start(f32[8,120,128]{2,1,0:T(8,128)S(1)} %maximum_bitcast_fusion.refs_1_.refs_3_), channel_id=1, source_target_pairs={{1,2},{2,1},{3,4},{4,3},{5,6},{6,5},{7,8},{8,7},{9,10},{10,9},{11,... | collective-permute-start | bytes 1474568 | tf_op jit(solution)/shard_map/ppermute | solution.py:423
  5.0 3.3 %fusion.2 = (f32[60,40,128]{2,1,0:T(8,128)}, f32[60,40,128]{2,1,0:T(8,128)}) fusion(f32[60,120,128]{2,1,0:T(8,128)} %bitcast.10), kind=kLoop, calls=%fused_computation.15 | loop fusion | bytes 4915200 | tf_op jit(solution)/shard_map/slice | solution.py:454
  8.3 1.2 %collective-permute-start.2 = (f32[60,40,128]{2,1,0:T(8,128)}, f32[60,40,128]{2,1,0:T(8,128)S(1)}, u32[]{:S(2)}, u32[]{:S(2)}) collective-permute-start(f32[60,40,128]{2,1,0:T(8,128)} %get-tuple-element.73), channel_id=1, source_target_pairs={{0,16},{16,0},{1,17},{17,1},{2,18},{18,2},{3,19},{19,3},{4,20},{20... | collective-permute-start | bytes 3686408 | tf_op jit(solution)/shard_map/ppermute | solution.py:426
  9.5 0.2 constant_dynamic-slice_fusion
  9.8 1.5 %slice.9 = f32[60,48,128]{2,1,0:T(8,128)S(1)} slice(f32[60,120,128]{2,1,0:T(8,128)} %bitcast.11), slice={[0:60], [72:120], [0:128]} | slice | bytes 2949120 | tf_op jit(solution)/shard_map/slice | solution.py:455
  11.7 5.8 %collective-permute-done.refs_2_.refs_4_ = f32[8,120,128]{2,1,0:T(8,128)S(1)} collective-permute-done((f32[8,120,128]{2,1,0:T(8,128)S(1)}, f32[8,120,128]{2,1,0:T(8,128)S(1)}, u32[]{:S(2)}, u32[]{:S(2)}) %collective-permute-start) | collective-permute-done | bytes 491552 | tf_op jit(solution)/shard_map/ppermute | solution.py:423
  17.5 2.9 %collective-permute-start.3 = (f32[60,48,128]{2,1,0:T(8,128)S(1)}, f32[60,48,128]{2,1,0:T(8,128)S(1)}, u32[]{:S(2)}, u32[]{:S(2)}) collective-permute-start(f32[60,48,128]{2,1,0:T(8,128)S(1)} %slice.9), channel_id=1, source_target_pairs={{1,2},{2,1},{3,4},{4,3},{5,6},{6,5},{7,8},{8,7},{9,10},{10,9},{11,... | collective-permute-start | bytes 4423688 | tf_op jit(solution)/shard_map/ppermute | solution.py:423
  20.4 16.5 %collective-permute-done.2.refs_5_ = f32[60,40,128]{2,1,0:T(8,128)S(1)} collective-permute-done((f32[60,40,128]{2,1,0:T(8,128)}, f32[60,40,128]{2,1,0:T(8,128)S(1)}, u32[]{:S(2)}, u32[]{:S(2)}) %collective-permute-start.2) | collective-permute-done | bytes 1228832 | tf_op jit(solution)/shard_map/ppermute | solution.py:426
  36.9 1.2 %collective-permute-start.5 = (f32[60,40,128]{2,1,0:T(8,128)S(1)}, f32[60,40,128]{2,1,0:T(8,128)S(1)}, u32[]{:S(2)}, u32[]{:S(2)}) collective-permute-start(f32[60,40,128]{2,1,0:T(8,128)S(1)} %copy-done.2), channel_id=1, source_target_pairs={{0,16},{16,0},{1,17},{17,1},{2,18},{18,2},{3,19},{19,3},{4,20},{20... | collective-permute-start | bytes 3686408 | tf_op jit(solution)/shard_map/ppermute | solution.py:426
  38.1 10.1 %gathered.2 = (f32[60,32,128]{2,1,0:T(8,128)S(1)}, f32[60,32,128]{2,1,0:T(8,128)}, f32[60,32,128]{2,1,0:T(8,128)}) custom-call(f32[60,120,128]{2,1,0:T(8,128)} %bitcast.12, f32[8,120,128]{2,1,0:T(8,128)S(1)} %maximum_bitcast_fusion.refs_1_.refs_3_, f32[8,120,128]{2,1,0:T(8,128)S(1)} %collective-permute-done.refs_2_.refs_4_, ...), custom_call_target="tpu_custom_call" | custom-call | flops 1209600 | bytes 32768 | tf_op jit(solution)/shard_map/gathered/pallas_call | solution.py:521
  48.2 6.1 %collective-permute-done.3.refs_1_ = f32[60,48,128]{2,1,0:T(8,128)S(1)} collective-permute-done((f32[60,48,128]{2,1,0:T(8,128)S(1)}, f32[60,48,128]{2,1,0:T(8,128)S(1)}, u32[]{:S(2)}, u32[]{:S(2)}) %collective-permute-start.3) | collective-permute-done | bytes 1474592 | tf_op jit(solution)/shard_map/ppermute | solution.py:423
  54.3 2.6 %collective-permute-start.6 = (f32[60,32,128]{2,1,0:T(8,128)}, f32[60,32,128]{2,1,0:T(8,128)S(1)}, u32[]{:S(2)}, u32[]{:S(2)}) collective-permute-start(f32[60,32,128]{2,1,0:T(8,128)} %get-tuple-element.59), channel_id=1, source_target_pairs={{1,2},{2,1},{3,4},{4,3},{5,6},{6,5},{7,8},{8,7},{9,10},{10,9},{11,... | collective-permute-start | bytes 2949128 | tf_op jit(solution)/shard_map/ppermute | solution.py:423
  57.0 7.7 %partial.2 = (f32[60,24,128]{2,1,0:T(8,128)S(1)}, f32[60,24,128]{2,1,0:T(8,128)}) custom-call(f32[60,120,128]{2,1,0:T(8,128)} %bitcast.13, f32[60,48,128]{2,1,0:T(8,128)S(1)} %collective-permute-done.3.refs_1_, f32[60,48,128]{2,1,0:T(8,128)} %copy-done.1, f32[8,120,128]{2,1,0:T(8,128)S(1)} %maximum_bitcast_fusion.refs_1_.refs_3_, ...), custom_call_target="tpu_custom_call" | custom-call | flops 907200 | bytes 24576 | tf_op jit(solution)/shard_map/partial/pallas_call | solution.py:492
  64.7 1.3 %collective-permute-start.8 = (f32[60,24,128]{2,1,0:T(8,128)}, f32[60,24,128]{2,1,0:T(8,128)S(1)}, u32[]{:S(2)}, u32[]{:S(2)}) collective-permute-start(f32[60,24,128]{2,1,0:T(8,128)} %get-tuple-element.61), channel_id=1, source_target_pairs={{0,16},{16,0},{1,17},{17,1},{2,18},{18,2},{3,19},{19,3},{4,20},{20... | collective-permute-start | bytes 2211848 | tf_op jit(solution)/shard_map/ppermute | solution.py:426
  65.9 1.0 copy-done.3
  67.0 12.2 %gathered.3 = (f32[60,40,128]{2,1,0:T(8,128)S(1)}, f32[60,40,128]{2,1,0:T(8,128)S(1)}, f32[60,40,128]{2,1,0:T(8,128)}) custom-call(f32[60,120,128]{2,1,0:T(8,128)} %bitcast.14, f32[8,120,128]{2,1,0:T(8,128)S(1)} %maximum_bitcast_fusion.refs_1_.refs_3_, f32[8,120,128]{2,1,0:T(8,128)S(1)} %collective-permute-done.refs_2_.refs_4_, ...), custom_call_target="tpu_custom_call" | custom-call | flops 1512000 | bytes 40960 | tf_op jit(solution)/shard_map/gathered/pallas_call | solution.py:521
  79.2 3.9 %collective-permute-start.9 = (f32[60,40,128]{2,1,0:T(8,128)S(1)}, f32[60,40,128]{2,1,0:T(8,128)S(1)}, u32[]{:S(2)}, u32[]{:S(2)}) collective-permute-start(f32[60,40,128]{2,1,0:T(8,128)S(1)} %get-tuple-element.67), channel_id=1, source_target_pairs={{1,2},{2,1},{3,4},{4,3},{5,6},{6,5},{7,8},{8,7},{9,10},{10,9},{11,... | collective-permute-start | bytes 3686408 | tf_op jit(solution)/shard_map/ppermute | solution.py:423
  83.2 7.0 %partial.3 = (f32[60,24,128]{2,1,0:T(8,128)S(1)}, f32[60,24,128]{2,1,0:T(8,128)S(1)}) custom-call(f32[60,120,128]{2,1,0:T(8,128)} %bitcast.15, f32[60,48,128]{2,1,0:T(8,128)S(1)} %collective-permute-done.3.refs_1_, f32[60,48,128]{2,1,0:T(8,128)} %copy-done.1, f32[8,120,128]{2,1,0:T(8,128)S(1)} %maximum_bitcast_fusion.refs_1_.refs_3_, ...), custom_call_target="tpu_custom_call" | custom-call | flops 907200 | bytes 24576 | tf_op jit(solution)/shard_map/partial/pallas_call | solution.py:492
  90.1 1.3 %collective-permute-start.11 = (f32[60,24,128]{2,1,0:T(8,128)S(1)}, f32[60,24,128]{2,1,0:T(8,128)S(1)}, u32[]{:S(2)}, u32[]{:S(2)}) collective-permute-start(f32[60,24,128]{2,1,0:T(8,128)S(1)} %get-tuple-element.72), channel_id=1, source_target_pairs={{0,16},{16,0},{1,17},{17,1},{2,18},{18,2},{3,19},{19,3},{4,20},{20... | collective-permute-start | bytes 2211848 | tf_op jit(solution)/shard_map/ppermute | solution.py:426
  91.4 7.1 %place.2.refs_0_ = f32[60,120,128]{2,1,0:T(8,128)} custom-call(f32[60,32,128]{2,1,0:T(8,128)S(1)} %get-tuple-element.46.refs_0_, f32[60,32,128]{2,1,0:T(8,128)S(1)} %collective-permute-done.6.refs_1_, f32[60,32,128]{2,1,0:T(8,128)S(1)} %collective-permute-done.7.refs_2_, f32[60,24,128]{2,1,0:T(8,128)S(1)} %get-tuple-element.64.refs_3_, ...), custom_call_target="tpu_custom_call" | custom-call | tf_op jit(solution)/shard_map/place/pallas_call | solution.py:396
  98.6 12.1 %collective-permute-done.9.refs_2_ = f32[60,40,128]{2,1,0:T(8,128)S(1)} collective-permute-done((f32[60,40,128]{2,1,0:T(8,128)S(1)}, f32[60,40,128]{2,1,0:T(8,128)S(1)}, u32[]{:S(2)}, u32[]{:S(2)}) %collective-permute-start.9) | collective-permute-done | bytes 1228832 | tf_op jit(solution)/shard_map/ppermute | solution.py:423
  110.6 4.4 %place.3 = f32[60,120,128]{2,1,0:T(8,128)} custom-call(f32[60,120,128]{2,1,0:T(8,128)} %place.2.refs_0_, f32[60,40,128]{2,1,0:T(8,128)S(1)} %get-tuple-element.66.refs_1_, f32[60,40,128]{2,1,0:T(8,128)S(1)} %collective-permute-done.9.refs_2_, f32[60,40,128]{2,1,0:T(8,128)S(1)} %collective-permute-done.10.refs_3_, ...), custom_call_target="tpu_custom_call", output_to_operand_aliasing={{}: (0, {})} | custom-call | tf_op jit(solution)/shard_map/place/pallas_call | solution.py:396
  (26 shorter events, 0.6 us)
Async XLA Ops:
  1.1 8.4 %copy-start.4 = (f32[7,120,120]{2,1,0:T(8,128)S(1)}, f32[7,120,120]{2,1,0:T(8,128)}, u32[]{:S(2)}) copy-start(f32[7,120,120]{2,1,0:T(8,128)} %param.7) | copy-start | bytes 1209604
  1.1 10.6 %collective-permute-start.1 = (f32[8,120,128]{2,1,0:T(8,128)S(1)}, f32[8,120,128]{2,1,0:T(8,128)S(1)}, u32[]{:S(2)}, u32[]{:S(2)}) collective-permute-start(f32[8,120,128]{2,1,0:T(8,128)S(1)} %maximum_bitcast_fusion.refs_1_.refs_3_), channel_id=1, source_target_pairs={{0,1},{1,0},{2,3},{3,2},{4,5},{5,4},{6,7},{7,6},{8,9},{9,8},{10,11... | collective-permute-start | bytes 1474568 | tf_op jit(solution)/shard_map/ppermute | solution.py:423
  1.8 15.7 %collective-permute-start = (f32[8,120,128]{2,1,0:T(8,128)S(1)}, f32[8,120,128]{2,1,0:T(8,128)S(1)}, u32[]{:S(2)}, u32[]{:S(2)}) collective-permute-start(f32[8,120,128]{2,1,0:T(8,128)S(1)} %maximum_bitcast_fusion.refs_1_.refs_3_), channel_id=1, source_target_pairs={{1,2},{2,1},{3,4},{4,3},{5,6},{6,5},{7,8},{8,7},{9,10},{10,9},{11,... | collective-permute-start | bytes 1474568 | tf_op jit(solution)/shard_map/ppermute | solution.py:423
  8.3 28.6 %collective-permute-start.2 = (f32[60,40,128]{2,1,0:T(8,128)}, f32[60,40,128]{2,1,0:T(8,128)S(1)}, u32[]{:S(2)}, u32[]{:S(2)}) collective-permute-start(f32[60,40,128]{2,1,0:T(8,128)} %get-tuple-element.73), channel_id=1, source_target_pairs={{0,16},{16,0},{1,17},{17,1},{2,18},{18,2},{3,19},{19,3},{4,20},{20... | collective-permute-start | bytes 3686408 | tf_op jit(solution)/shard_map/ppermute | solution.py:426
  11.4 25.4 %copy-start.2 = (f32[60,40,128]{2,1,0:T(8,128)S(1)}, f32[60,40,128]{2,1,0:T(8,128)}, u32[]{:S(2)}) copy-start(f32[60,40,128]{2,1,0:T(8,128)} %get-tuple-element.56) | copy-start | bytes 3686404
  17.5 30.7 %collective-permute-start.4 = (f32[60,48,128]{2,1,0:T(8,128)S(1)}, f32[60,48,128]{2,1,0:T(8,128)S(1)}, u32[]{:S(2)}, u32[]{:S(2)}) collective-permute-start(f32[60,48,128]{2,1,0:T(8,128)S(1)} %slice.9), channel_id=1, source_target_pairs={{0,1},{1,0},{2,3},{3,2},{4,5},{5,4},{6,7},{7,6},{8,9},{9,8},{10,11... | collective-permute-start | bytes 4423688 | tf_op jit(solution)/shard_map/ppermute | solution.py:423
  17.5 36.8 %collective-permute-start.3 = (f32[60,48,128]{2,1,0:T(8,128)S(1)}, f32[60,48,128]{2,1,0:T(8,128)S(1)}, u32[]{:S(2)}, u32[]{:S(2)}) collective-permute-start(f32[60,48,128]{2,1,0:T(8,128)S(1)} %slice.9), channel_id=1, source_target_pairs={{1,2},{2,1},{3,4},{4,3},{5,6},{6,5},{7,8},{8,7},{9,10},{10,9},{11,... | collective-permute-start | bytes 4423688 | tf_op jit(solution)/shard_map/ppermute | solution.py:423
  36.9 11.3 %copy-start = (f32[60,40,128]{2,1,0:T(8,128)}, f32[60,40,128]{2,1,0:T(8,128)S(1)}, u32[]{:S(2)}) copy-start(f32[60,40,128]{2,1,0:T(8,128)S(1)} %collective-permute-done.2.refs_5_) | copy-start | bytes 3686404
  36.9 29.0 %collective-permute-start.5 = (f32[60,40,128]{2,1,0:T(8,128)S(1)}, f32[60,40,128]{2,1,0:T(8,128)S(1)}, u32[]{:S(2)}, u32[]{:S(2)}) collective-permute-start(f32[60,40,128]{2,1,0:T(8,128)S(1)} %copy-done.2), channel_id=1, source_target_pairs={{0,16},{16,0},{1,17},{17,1},{2,18},{18,2},{3,19},{19,3},{4,20},{20... | collective-permute-start | bytes 3686408 | tf_op jit(solution)/shard_map/ppermute | solution.py:426
  48.2 8.8 %copy-start.1 = (f32[60,48,128]{2,1,0:T(8,128)}, f32[60,48,128]{2,1,0:T(8,128)S(1)}, u32[]{:S(2)}) copy-start(f32[60,48,128]{2,1,0:T(8,128)S(1)} %collective-permute-done.4.refs_2_) | copy-start | bytes 4423684
  54.3 28.9 %collective-permute-start.6 = (f32[60,32,128]{2,1,0:T(8,128)}, f32[60,32,128]{2,1,0:T(8,128)S(1)}, u32[]{:S(2)}, u32[]{:S(2)}) collective-permute-start(f32[60,32,128]{2,1,0:T(8,128)} %get-tuple-element.59), channel_id=1, source_target_pairs={{1,2},{2,1},{3,4},{4,3},{5,6},{6,5},{7,8},{8,7},{9,10},{10,9},{11,... | collective-permute-start | bytes 2949128 | tf_op jit(solution)/shard_map/ppermute | solution.py:423
  56.9 26.3 %collective-permute-start.7 = (f32[60,32,128]{2,1,0:T(8,128)}, f32[60,32,128]{2,1,0:T(8,128)S(1)}, u32[]{:S(2)}, u32[]{:S(2)}) collective-permute-start(f32[60,32,128]{2,1,0:T(8,128)} %get-tuple-element.60), channel_id=1, source_target_pairs={{0,1},{1,0},{2,3},{3,2},{4,5},{5,4},{6,7},{7,6},{8,9},{9,8},{10,11... | collective-permute-start | bytes 2949128 | tf_op jit(solution)/shard_map/ppermute | solution.py:423
  64.7 18.5 %collective-permute-start.8 = (f32[60,24,128]{2,1,0:T(8,128)}, f32[60,24,128]{2,1,0:T(8,128)S(1)}, u32[]{:S(2)}, u32[]{:S(2)}) collective-permute-start(f32[60,24,128]{2,1,0:T(8,128)} %get-tuple-element.61), channel_id=1, source_target_pairs={{0,16},{16,0},{1,17},{17,1},{2,18},{18,2},{3,19},{19,3},{4,20},{20... | collective-permute-start | bytes 2211848 | tf_op jit(solution)/shard_map/ppermute | solution.py:426
  65.9 1.0 copy-start.3
  79.2 31.5 %collective-permute-start.9 = (f32[60,40,128]{2,1,0:T(8,128)S(1)}, f32[60,40,128]{2,1,0:T(8,128)S(1)}, u32[]{:S(2)}, u32[]{:S(2)}) collective-permute-start(f32[60,40,128]{2,1,0:T(8,128)S(1)} %get-tuple-element.67), channel_id=1, source_target_pairs={{1,2},{2,1},{3,4},{4,3},{5,6},{6,5},{7,8},{8,7},{9,10},{10,9},{11,... | collective-permute-start | bytes 3686408 | tf_op jit(solution)/shard_map/ppermute | solution.py:423
  83.1 27.6 %collective-permute-start.10 = (f32[60,40,128]{2,1,0:T(8,128)}, f32[60,40,128]{2,1,0:T(8,128)S(1)}, u32[]{:S(2)}, u32[]{:S(2)}) collective-permute-start(f32[60,40,128]{2,1,0:T(8,128)} %get-tuple-element.68), channel_id=1, source_target_pairs={{0,1},{1,0},{2,3},{3,2},{4,5},{5,4},{6,7},{7,6},{8,9},{9,8},{10,11... | collective-permute-start | bytes 3686408 | tf_op jit(solution)/shard_map/ppermute | solution.py:423
  90.1 20.5 %collective-permute-start.11 = (f32[60,24,128]{2,1,0:T(8,128)S(1)}, f32[60,24,128]{2,1,0:T(8,128)S(1)}, u32[]{:S(2)}, u32[]{:S(2)}) collective-permute-start(f32[60,24,128]{2,1,0:T(8,128)S(1)} %get-tuple-element.72), channel_id=1, source_target_pairs={{0,16},{16,0},{1,17},{17,1},{2,18},{18,2},{3,19},{19,3},{4,20},{20... | collective-permute-start | bytes 2211848 | tf_op jit(solution)/shard_map/ppermute | solution.py:426

commit v5 on v4

--- a/solution.py
+++ b/solution.py
@@ -358,7 +358,7 @@
 def place_sums(result, shares, shape):
     modes, _, nz = shape
     kept = [] if result is None else [result]
-    steps = next(n for n in (4, 3, 1) if modes % n == 0)
+    steps = next(n for n in (2, 3, 1) if modes % n == 0)
     some = modes // steps
     flat = [part for _, parts in shares for part in parts]
 

time: 115 us -> 114 us (level)
  Pallas kernels: 48.4 us -> 43.8 us
  waiting for transfers between devices: 40.5 us -> 43.7 us
    pallas_call x2, Pallas kernels: 11.5 us -> 6.88 us  [place_sums(): pl.pallas_call(kernel, in_specs=[ANY] * (len(kept) + len(flat)), out_spec...]
    ppermute x8, waiting for transfers between devices: 24 us -> 27.2 us  [swapped(): return lax.ppermute(value, 'space', pairs[side])]
  transfers between devices with their start and end apart: 12 -> 12, of which waited for: 4 -> 4; matrix products, arithmetic and copies ran while one was open for 5% -> 5% of each run, Pallas kernels for 38% -> 36%
where the time goes in v5:
time: 114 us
  Pallas kernels  43.8 us (38%)
  waiting for transfers between devices  43.7 us (38%)
  starting transfers between devices  18.4 us (16%)
  local copies, waits for them, and re-layouts  6.1 us (5%)
  other arithmetic  1.44 us (1%)
    ppermute x8, waiting for transfers between devices, swapped(): return lax.ppermute(value, 'space', pairs[side])  27.2 us
    pallas_call x2, Pallas kernels, gathered_shares(): pl.pallas_call(functools.partial(gathered_kernel, first, count, rows, mod...  22.3 us
    ppermute x4, waiting for transfers between devices, rotated(): lax.ppermute(value, 'modes', [(i, (i + step) % groups) for i in range(gro...  16.5 us
    pallas_call x2, Pallas kernels, partial_shares(): pl.pallas_call(functools.partial(partial_kernel, first, count, rows, mode...  14.6 us
    ppermute x8, starting transfers between devices, swapped(): return lax.ppermute(value, 'space', pairs[side])  13.4 us
    pallas_call x2, Pallas kernels, place_sums(): pl.pallas_call(kernel, in_specs=[ANY] * (len(kept) + len(flat)), out_spec...  6.88 us
    ppermute x4, starting transfers between devices, rotated(): lax.ppermute(value, 'modes', [(i, (i + step) % groups) for i in range(gro...  4.98 us
    slice x1, local copies, waits for them, and re-layouts, local(): ready[:, start:start + length]  3.27 us
  transfers between devices with their start and end apart: 12, of which 4 were waited for; matrix products, arithmetic and copies ran while one was open for 5% of the time, Pallas kernels for 36%

profile of v5, /device:TPU:17, one launch (start us, length us, event | category | flops | bytes accessed | tf_op | source)
XLA Modules:
  0.0 113.6 jit_solution(13062304439169079081)
XLA Ops:
  0.0 1.1 maximum_bitcast_fusion.refs_1_.refs_3_
  1.1 0.7 collective-permute-start.1
  1.8 3.2 %collective-permute-start = (f32[8,120,128]{2,1,0:T(8,128)S(1)}, f32[8,120,128]{2,1,0:T(8,128)S(1)}, u32[]{:S(2)}, u32[]{:S(2)}) collective-permute-start(f32[8,120,128]{2,1,0:T(8,128)S(1)} %maximum_bitcast_fusion.refs_1_.refs_3_), channel_id=1, source_target_pairs={{1,2},{2,1},{3,4},{4,3},{5,6},{6,5},{7,8},{8,7},{9,10},{10,9},{11,... | collective-permute-start | bytes 1474568 | tf_op jit(solution)/shard_map/ppermute | solution.py:423
  5.0 3.3 %fusion.2 = (f32[60,40,128]{2,1,0:T(8,128)}, f32[60,40,128]{2,1,0:T(8,128)}) fusion(f32[60,120,128]{2,1,0:T(8,128)} %bitcast.10), kind=kLoop, calls=%fused_computation.15 | loop fusion | bytes 4915200 | tf_op jit(solution)/shard_map/slice | solution.py:454
  8.3 1.2 %collective-permute-start.2 = (f32[60,40,128]{2,1,0:T(8,128)}, f32[60,40,128]{2,1,0:T(8,128)S(1)}, u32[]{:S(2)}, u32[]{:S(2)}) collective-permute-start(f32[60,40,128]{2,1,0:T(8,128)} %get-tuple-element.73), channel_id=1, source_target_pairs={{0,16},{16,0},{1,17},{17,1},{2,18},{18,2},{3,19},{19,3},{4,20},{20... | collective-permute-start | bytes 3686408 | tf_op jit(solution)/shard_map/ppermute | solution.py:426
  9.5 0.2 constant_dynamic-slice_fusion
  9.8 1.5 %slice.9 = f32[60,48,128]{2,1,0:T(8,128)S(1)} slice(f32[60,120,128]{2,1,0:T(8,128)} %bitcast.11), slice={[0:60], [72:120], [0:128]} | slice | bytes 2949120 | tf_op jit(solution)/shard_map/slice | solution.py:455
  11.7 5.8 %collective-permute-done.refs_2_.refs_4_ = f32[8,120,128]{2,1,0:T(8,128)S(1)} collective-permute-done((f32[8,120,128]{2,1,0:T(8,128)S(1)}, f32[8,120,128]{2,1,0:T(8,128)S(1)}, u32[]{:S(2)}, u32[]{:S(2)}) %collective-permute-start) | collective-permute-done | bytes 491552 | tf_op jit(solution)/shard_map/ppermute | solution.py:423
  17.5 2.9 %collective-permute-start.3 = (f32[60,48,128]{2,1,0:T(8,128)S(1)}, f32[60,48,128]{2,1,0:T(8,128)S(1)}, u32[]{:S(2)}, u32[]{:S(2)}) collective-permute-start(f32[60,48,128]{2,1,0:T(8,128)S(1)} %slice.9), channel_id=1, source_target_pairs={{1,2},{2,1},{3,4},{4,3},{5,6},{6,5},{7,8},{8,7},{9,10},{10,9},{11,... | collective-permute-start | bytes 4423688 | tf_op jit(solution)/shard_map/ppermute | solution.py:423
  20.4 16.5 %collective-permute-done.2.refs_5_ = f32[60,40,128]{2,1,0:T(8,128)S(1)} collective-permute-done((f32[60,40,128]{2,1,0:T(8,128)}, f32[60,40,128]{2,1,0:T(8,128)S(1)}, u32[]{:S(2)}, u32[]{:S(2)}) %collective-permute-start.2) | collective-permute-done | bytes 1228832 | tf_op jit(solution)/shard_map/ppermute | solution.py:426
  36.9 1.2 %collective-permute-start.5 = (f32[60,40,128]{2,1,0:T(8,128)S(1)}, f32[60,40,128]{2,1,0:T(8,128)S(1)}, u32[]{:S(2)}, u32[]{:S(2)}) collective-permute-start(f32[60,40,128]{2,1,0:T(8,128)S(1)} %copy-done.2), channel_id=1, source_target_pairs={{0,16},{16,0},{1,17},{17,1},{2,18},{18,2},{3,19},{19,3},{4,20},{20... | collective-permute-start | bytes 3686408 | tf_op jit(solution)/shard_map/ppermute | solution.py:426
  38.1 10.1 %gathered.2 = (f32[60,32,128]{2,1,0:T(8,128)S(1)}, f32[60,32,128]{2,1,0:T(8,128)}, f32[60,32,128]{2,1,0:T(8,128)}) custom-call(f32[60,120,128]{2,1,0:T(8,128)} %bitcast.12, f32[8,120,128]{2,1,0:T(8,128)S(1)} %maximum_bitcast_fusion.refs_1_.refs_3_, f32[8,120,128]{2,1,0:T(8,128)S(1)} %collective-permute-done.refs_2_.refs_4_, ...), custom_call_target="tpu_custom_call" | custom-call | flops 1209600 | bytes 32768 | tf_op jit(solution)/shard_map/gathered/pallas_call | solution.py:521
  48.2 6.1 %collective-permute-done.3.refs_1_ = f32[60,48,128]{2,1,0:T(8,128)S(1)} collective-permute-done((f32[60,48,128]{2,1,0:T(8,128)S(1)}, f32[60,48,128]{2,1,0:T(8,128)S(1)}, u32[]{:S(2)}, u32[]{:S(2)}) %collective-permute-start.3) | collective-permute-done | bytes 1474592 | tf_op jit(solution)/shard_map/ppermute | solution.py:423
  54.3 2.6 %collective-permute-start.6 = (f32[60,32,128]{2,1,0:T(8,128)}, f32[60,32,128]{2,1,0:T(8,128)S(1)}, u32[]{:S(2)}, u32[]{:S(2)}) collective-permute-start(f32[60,32,128]{2,1,0:T(8,128)} %get-tuple-element.59), channel_id=1, source_target_pairs={{1,2},{2,1},{3,4},{4,3},{5,6},{6,5},{7,8},{8,7},{9,10},{10,9},{11,... | collective-permute-start | bytes 2949128 | tf_op jit(solution)/shard_map/ppermute | solution.py:423
  57.0 7.7 %partial.2 = (f32[60,24,128]{2,1,0:T(8,128)S(1)}, f32[60,24,128]{2,1,0:T(8,128)}) custom-call(f32[60,120,128]{2,1,0:T(8,128)} %bitcast.13, f32[60,48,128]{2,1,0:T(8,128)S(1)} %collective-permute-done.3.refs_1_, f32[60,48,128]{2,1,0:T(8,128)} %copy-done.1, f32[8,120,128]{2,1,0:T(8,128)S(1)} %maximum_bitcast_fusion.refs_1_.refs_3_, ...), custom_call_target="tpu_custom_call" | custom-call | flops 907200 | bytes 24576 | tf_op jit(solution)/shard_map/partial/pallas_call | solution.py:492
  64.7 1.3 %collective-permute-start.8 = (f32[60,24,128]{2,1,0:T(8,128)}, f32[60,24,128]{2,1,0:T(8,128)S(1)}, u32[]{:S(2)}, u32[]{:S(2)}) collective-permute-start(f32[60,24,128]{2,1,0:T(8,128)} %get-tuple-element.61), channel_id=1, source_target_pairs={{0,16},{16,0},{1,17},{17,1},{2,18},{18,2},{3,19},{19,3},{4,20},{20... | collective-permute-start | bytes 2211848 | tf_op jit(solution)/shard_map/ppermute | solution.py:426
  65.9 1.0 copy-done.3
  67.0 12.2 %gathered.3 = (f32[60,40,128]{2,1,0:T(8,128)S(1)}, f32[60,40,128]{2,1,0:T(8,128)S(1)}, f32[60,40,128]{2,1,0:T(8,128)}) custom-call(f32[60,120,128]{2,1,0:T(8,128)} %bitcast.14, f32[8,120,128]{2,1,0:T(8,128)S(1)} %maximum_bitcast_fusion.refs_1_.refs_3_, f32[8,120,128]{2,1,0:T(8,128)S(1)} %collective-permute-done.refs_2_.refs_4_, ...), custom_call_target="tpu_custom_call" | custom-call | flops 1512000 | bytes 40960 | tf_op jit(solution)/shard_map/gathered/pallas_call | solution.py:521
  79.2 3.9 %collective-permute-start.9 = (f32[60,40,128]{2,1,0:T(8,128)S(1)}, f32[60,40,128]{2,1,0:T(8,128)S(1)}, u32[]{:S(2)}, u32[]{:S(2)}) collective-permute-start(f32[60,40,128]{2,1,0:T(8,128)S(1)} %get-tuple-element.67), channel_id=1, source_target_pairs={{1,2},{2,1},{3,4},{4,3},{5,6},{6,5},{7,8},{8,7},{9,10},{10,9},{11,... | collective-permute-start | bytes 3686408 | tf_op jit(solution)/shard_map/ppermute | solution.py:423
  83.2 7.0 %partial.3 = (f32[60,24,128]{2,1,0:T(8,128)S(1)}, f32[60,24,128]{2,1,0:T(8,128)S(1)}) custom-call(f32[60,120,128]{2,1,0:T(8,128)} %bitcast.15, f32[60,48,128]{2,1,0:T(8,128)S(1)} %collective-permute-done.3.refs_1_, f32[60,48,128]{2,1,0:T(8,128)} %copy-done.1, f32[8,120,128]{2,1,0:T(8,128)S(1)} %maximum_bitcast_fusion.refs_1_.refs_3_, ...), custom_call_target="tpu_custom_call" | custom-call | flops 907200 | bytes 24576 | tf_op jit(solution)/shard_map/partial/pallas_call | solution.py:492
  90.1 1.3 %collective-permute-start.11 = (f32[60,24,128]{2,1,0:T(8,128)S(1)}, f32[60,24,128]{2,1,0:T(8,128)S(1)}, u32[]{:S(2)}, u32[]{:S(2)}) collective-permute-start(f32[60,24,128]{2,1,0:T(8,128)S(1)} %get-tuple-element.72), channel_id=1, source_target_pairs={{0,16},{16,0},{1,17},{17,1},{2,18},{18,2},{3,19},{19,3},{4,20},{20... | collective-permute-start | bytes 2211848 | tf_op jit(solution)/shard_map/ppermute | solution.py:426
  91.4 3.9 %place.2.refs_0_ = f32[60,120,128]{2,1,0:T(8,128)} custom-call(f32[60,32,128]{2,1,0:T(8,128)S(1)} %get-tuple-element.46.refs_0_, f32[60,32,128]{2,1,0:T(8,128)S(1)} %collective-permute-done.6.refs_1_, f32[60,32,128]{2,1,0:T(8,128)S(1)} %collective-permute-done.7.refs_2_, f32[60,24,128]{2,1,0:T(8,128)S(1)} %get-tuple-element.64.refs_3_, ...), custom_call_target="tpu_custom_call" | custom-call | tf_op jit(solution)/shard_map/place/pallas_call | solution.py:396
  95.3 15.3 %collective-permute-done.9.refs_2_ = f32[60,40,128]{2,1,0:T(8,128)S(1)} collective-permute-done((f32[60,40,128]{2,1,0:T(8,128)S(1)}, f32[60,40,128]{2,1,0:T(8,128)S(1)}, u32[]{:S(2)}, u32[]{:S(2)}) %collective-permute-start.9) | collective-permute-done | bytes 1228832 | tf_op jit(solution)/shard_map/ppermute | solution.py:423
  110.6 3.0 %place.3 = f32[60,120,128]{2,1,0:T(8,128)} custom-call(f32[60,120,128]{2,1,0:T(8,128)} %place.2.refs_0_, f32[60,40,128]{2,1,0:T(8,128)S(1)} %get-tuple-element.66.refs_1_, f32[60,40,128]{2,1,0:T(8,128)S(1)} %collective-permute-done.9.refs_2_, f32[60,40,128]{2,1,0:T(8,128)S(1)} %collective-permute-done.10.refs_3_, ...), custom_call_target="tpu_custom_call", output_to_operand_aliasing={{}: (0, {})} | custom-call | tf_op jit(solution)/shard_map/place/pallas_call | solution.py:396
  (26 shorter events, 0.6 us)
Async XLA Ops:
  1.1 8.4 %copy-start.4 = (f32[7,120,120]{2,1,0:T(8,128)S(1)}, f32[7,120,120]{2,1,0:T(8,128)}, u32[]{:S(2)}) copy-start(f32[7,120,120]{2,1,0:T(8,128)} %param.7) | copy-start | bytes 1209604
  1.1 10.6 %collective-permute-start.1 = (f32[8,120,128]{2,1,0:T(8,128)S(1)}, f32[8,120,128]{2,1,0:T(8,128)S(1)}, u32[]{:S(2)}, u32[]{:S(2)}) collective-permute-start(f32[8,120,128]{2,1,0:T(8,128)S(1)} %maximum_bitcast_fusion.refs_1_.refs_3_), channel_id=1, source_target_pairs={{0,1},{1,0},{2,3},{3,2},{4,5},{5,4},{6,7},{7,6},{8,9},{9,8},{10,11... | collective-permute-start | bytes 1474568 | tf_op jit(solution)/shard_map/ppermute | solution.py:423
  1.8 15.7 %collective-permute-start = (f32[8,120,128]{2,1,0:T(8,128)S(1)}, f32[8,120,128]{2,1,0:T(8,128)S(1)}, u32[]{:S(2)}, u32[]{:S(2)}) collective-permute-start(f32[8,120,128]{2,1,0:T(8,128)S(1)} %maximum_bitcast_fusion.refs_1_.refs_3_), channel_id=1, source_target_pairs={{1,2},{2,1},{3,4},{4,3},{5,6},{6,5},{7,8},{8,7},{9,10},{10,9},{11,... | collective-permute-start | bytes 1474568 | tf_op jit(solution)/shard_map/ppermute | solution.py:423
  8.3 28.6 %collective-permute-start.2 = (f32[60,40,128]{2,1,0:T(8,128)}, f32[60,40,128]{2,1,0:T(8,128)S(1)}, u32[]{:S(2)}, u32[]{:S(2)}) collective-permute-start(f32[60,40,128]{2,1,0:T(8,128)} %get-tuple-element.73), channel_id=1, source_target_pairs={{0,16},{16,0},{1,17},{17,1},{2,18},{18,2},{3,19},{19,3},{4,20},{20... | collective-permute-start | bytes 3686408 | tf_op jit(solution)/shard_map/ppermute | solution.py:426
  11.4 25.4 %copy-start.2 = (f32[60,40,128]{2,1,0:T(8,128)S(1)}, f32[60,40,128]{2,1,0:T(8,128)}, u32[]{:S(2)}) copy-start(f32[60,40,128]{2,1,0:T(8,128)} %get-tuple-element.56) | copy-start | bytes 3686404
  17.5 30.7 %collective-permute-start.4 = (f32[60,48,128]{2,1,0:T(8,128)S(1)}, f32[60,48,128]{2,1,0:T(8,128)S(1)}, u32[]{:S(2)}, u32[]{:S(2)}) collective-permute-start(f32[60,48,128]{2,1,0:T(8,128)S(1)} %slice.9), channel_id=1, source_target_pairs={{0,1},{1,0},{2,3},{3,2},{4,5},{5,4},{6,7},{7,6},{8,9},{9,8},{10,11... | collective-permute-start | bytes 4423688 | tf_op jit(solution)/shard_map/ppermute | solution.py:423
  17.5 36.8 %collective-permute-start.3 = (f32[60,48,128]{2,1,0:T(8,128)S(1)}, f32[60,48,128]{2,1,0:T(8,128)S(1)}, u32[]{:S(2)}, u32[]{:S(2)}) collective-permute-start(f32[60,48,128]{2,1,0:T(8,128)S(1)} %slice.9), channel_id=1, source_target_pairs={{1,2},{2,1},{3,4},{4,3},{5,6},{6,5},{7,8},{8,7},{9,10},{10,9},{11,... | collective-permute-start | bytes 4423688 | tf_op jit(solution)/shard_map/ppermute | solution.py:423
  36.9 11.3 %copy-start = (f32[60,40,128]{2,1,0:T(8,128)}, f32[60,40,128]{2,1,0:T(8,128)S(1)}, u32[]{:S(2)}) copy-start(f32[60,40,128]{2,1,0:T(8,128)S(1)} %collective-permute-done.2.refs_5_) | copy-start | bytes 3686404
  36.9 29.0 %collective-permute-start.5 = (f32[60,40,128]{2,1,0:T(8,128)S(1)}, f32[60,40,128]{2,1,0:T(8,128)S(1)}, u32[]{:S(2)}, u32[]{:S(2)}) collective-permute-start(f32[60,40,128]{2,1,0:T(8,128)S(1)} %copy-done.2), channel_id=1, source_target_pairs={{0,16},{16,0},{1,17},{17,1},{2,18},{18,2},{3,19},{19,3},{4,20},{20... | collective-permute-start | bytes 3686408 | tf_op jit(solution)/shard_map/ppermute | solution.py:426
  48.2 8.8 %copy-start.1 = (f32[60,48,128]{2,1,0:T(8,128)}, f32[60,48,128]{2,1,0:T(8,128)S(1)}, u32[]{:S(2)}) copy-start(f32[60,48,128]{2,1,0:T(8,128)S(1)} %collective-permute-done.4.refs_2_) | copy-start | bytes 4423684
  54.3 28.9 %collective-permute-start.6 = (f32[60,32,128]{2,1,0:T(8,128)}, f32[60,32,128]{2,1,0:T(8,128)S(1)}, u32[]{:S(2)}, u32[]{:S(2)}) collective-permute-start(f32[60,32,128]{2,1,0:T(8,128)} %get-tuple-element.59), channel_id=1, source_target_pairs={{1,2},{2,1},{3,4},{4,3},{5,6},{6,5},{7,8},{8,7},{9,10},{10,9},{11,... | collective-permute-start | bytes 2949128 | tf_op jit(solution)/shard_map/ppermute | solution.py:423
  56.9 26.3 %collective-permute-start.7 = (f32[60,32,128]{2,1,0:T(8,128)}, f32[60,32,128]{2,1,0:T(8,128)S(1)}, u32[]{:S(2)}, u32[]{:S(2)}) collective-permute-start(f32[60,32,128]{2,1,0:T(8,128)} %get-tuple-element.60), channel_id=1, source_target_pairs={{0,1},{1,0},{2,3},{3,2},{4,5},{5,4},{6,7},{7,6},{8,9},{9,8},{10,11... | collective-permute-start | bytes 2949128 | tf_op jit(solution)/shard_map/ppermute | solution.py:423
  64.7 18.5 %collective-permute-start.8 = (f32[60,24,128]{2,1,0:T(8,128)}, f32[60,24,128]{2,1,0:T(8,128)S(1)}, u32[]{:S(2)}, u32[]{:S(2)}) collective-permute-start(f32[60,24,128]{2,1,0:T(8,128)} %get-tuple-element.61), channel_id=1, source_target_pairs={{0,16},{16,0},{1,17},{17,1},{2,18},{18,2},{3,19},{19,3},{4,20},{20... | collective-permute-start | bytes 2211848 | tf_op jit(solution)/shard_map/ppermute | solution.py:426
  65.9 1.0 copy-start.3
  79.2 31.5 %collective-permute-start.9 = (f32[60,40,128]{2,1,0:T(8,128)S(1)}, f32[60,40,128]{2,1,0:T(8,128)S(1)}, u32[]{:S(2)}, u32[]{:S(2)}) collective-permute-start(f32[60,40,128]{2,1,0:T(8,128)S(1)} %get-tuple-element.67), channel_id=1, source_target_pairs={{1,2},{2,1},{3,4},{4,3},{5,6},{6,5},{7,8},{8,7},{9,10},{10,9},{11,... | collective-permute-start | bytes 3686408 | tf_op jit(solution)/shard_map/ppermute | solution.py:423
  83.1 27.6 %collective-permute-start.10 = (f32[60,40,128]{2,1,0:T(8,128)}, f32[60,40,128]{2,1,0:T(8,128)S(1)}, u32[]{:S(2)}, u32[]{:S(2)}) collective-permute-start(f32[60,40,128]{2,1,0:T(8,128)} %get-tuple-element.68), channel_id=1, source_target_pairs={{0,1},{1,0},{2,3},{3,2},{4,5},{5,4},{6,7},{7,6},{8,9},{9,8},{10,11... | collective-permute-start | bytes 3686408 | tf_op jit(solution)/shard_map/ppermute | solution.py:423
  90.1 20.5 %collective-permute-start.11 = (f32[60,24,128]{2,1,0:T(8,128)S(1)}, f32[60,24,128]{2,1,0:T(8,128)S(1)}, u32[]{:S(2)}, u32[]{:S(2)}) collective-permute-start(f32[60,24,128]{2,1,0:T(8,128)S(1)} %get-tuple-element.72), channel_id=1, source_target_pairs={{0,16},{16,0},{1,17},{17,1},{2,18},{18,2},{3,19},{19,3},{4,20},{20... | collective-permute-start | bytes 2211848 | tf_op jit(solution)/shard_map/ppermute | solution.py:426

commit v6 on v5

--- a/solution.py
+++ b/solution.py
@@ -150,7 +150,6 @@
                     place = s * pad + block * PACK
                     stack[place : place + PACK, lanes] = high
                     stack[wide + place : wide + place + PACK, lanes] = low
-                    stack[2 * wide + place : 2 * wide + place + PACK, lanes] = high
         mixed[...] = jnp.dot(weights[...], stack[...], preferred_element_type=jnp.float32)
 
     def spread(mixed, row):
@@ -163,7 +162,8 @@
                     if k == terms - 1:
                         value = mode_block(own, block, row + slot - base, mode_dev, size)
                     else:
-                        value = mixed[pl.ds(k * pad + block * PACK, PACK), pl.ds(slot * nz, nz)]
+                        lanes, at = pl.ds(slot * nz, nz), k * pad + block * PACK
+                        value = mixed[pl.ds(at, PACK), lanes] + mixed[pl.ds(at + (terms - 1) * pad, PACK), lanes]
                     for f in range(FACES):
                         part = factor(f, k) * value
                         totals[f] = part if totals[f] is None else totals[f] + part
@@ -444,7 +444,13 @@
     partial = [(begin, half), (begin + half, rows - begin - half)]
 
     high, low = split(jnp.concatenate([block(group, group - s) for s in range(groups)], 2))
-    gathered_weights = jnp.concatenate([high, high, low], 2).reshape((terms - 1) * pad, 3 * groups * pad)
+    gathered_weights = jnp.concatenate(
+        [
+            jnp.concatenate(pair, 2).reshape((terms - 1) * pad, 2 * groups * pad)
+            for pair in ((high, high), (low, jnp.zeros_like(low)))
+        ],
+        0,
+    )
     high, low = split(jnp.concatenate([block(group + s, group) for s in range(groups)], 1))
     partial_weights = jnp.concatenate([high, low], 1)
 
@@ -528,8 +534,8 @@
             scratch_shapes=[pltpu.VMEM(window_modes(count), f32), pltpu.VMEM((groups - 1, *window_modes(count)), f32)]
             + window_scratch(count, 1, groups, 3)
             + [
-                pltpu.VMEM((3 * groups * pad, 2 * nz), jnp.bfloat16),
-                pltpu.VMEM(((terms - 1) * pad, 2 * nz), f32),
+                pltpu.VMEM((2 * groups * pad, 2 * nz), jnp.bfloat16),
+                pltpu.VMEM((2 * (terms - 1) * pad, 2 * nz), f32),
             ]
             * 2
             + [pltpu.VMEM((pad, nz), f32)] * 2

time: 114 us -> 123 us (1.079)
  starting transfers between devices: 18.4 us -> 28.3 us
    ppermute x4, starting transfers between devices: 4.98 us -> 14.9 us  [rotated(): lax.ppermute(value, 'modes', [(i, (i + step) % groups) for i in range(gro...]
  transfers between devices with their start and end apart: 12 -> 12, of which waited for: 4 -> 5; matrix products, arithmetic and copies ran while one was open for 5% -> 5% of each run, Pallas kernels for 36% -> 33%
where the time goes in v6:
time: 123 us; the launch traced here: 122 us
  waiting for transfers between devices  44 us (36%)
  Pallas kernels  43.1 us (35%)
  starting transfers between devices  28.3 us (23%)
  local copies, waits for them, and re-layouts  5.09 us (4%)
  other arithmetic  1.54 us (1%)
    ppermute x8, waiting for transfers between devices, swapped(): return lax.ppermute(value, 'space', pairs[side])  26.8 us
    pallas_call x2, Pallas kernels, gathered_shares(): pl.pallas_call(functools.partial(gathered_kernel, first, count, rows, mod...  21.6 us
    ppermute x4, waiting for transfers between devices, rotated(): lax.ppermute(value, 'modes', [(i, (i + step) % groups) for i in range(gro...  17.2 us
    ppermute x4, starting transfers between devices, rotated(): lax.ppermute(value, 'modes', [(i, (i + step) % groups) for i in range(gro...  14.9 us
    pallas_call x2, Pallas kernels, partial_shares(): pl.pallas_call(functools.partial(partial_kernel, first, count, rows, mode...  14.6 us
    ppermute x8, starting transfers between devices, swapped(): return lax.ppermute(value, 'space', pairs[side])  13.4 us
    pallas_call x2, Pallas kernels, place_sums(): pl.pallas_call(kernel, in_specs=[ANY] * (len(kept) + len(flat)), out_spec...  6.88 us
    slice x1, local copies, waits for them, and re-layouts, local(): ready[:, start:start + length]  3.28 us
  transfers between devices with their start and end apart: 12, of which 5 were waited for; matrix products, arithmetic and copies ran while one was open for 5% of the time, Pallas kernels for 33%

profile of v6, /device:TPU:17, one launch (start us, length us, event | category | flops | bytes accessed | tf_op | source)
XLA Modules:
  0.0 122.2 jit_solution(16218483489271380370)
XLA Ops:
  0.0 1.1 maximum_bitcast_fusion.refs_1_.refs_3_
  1.1 0.7 collective-permute-start.1
  1.8 3.2 %collective-permute-start = (f32[8,120,128]{2,1,0:T(8,128)S(1)}, f32[8,120,128]{2,1,0:T(8,128)S(1)}, u32[]{:S(2)}, u32[]{:S(2)}) collective-permute-start(f32[8,120,128]{2,1,0:T(8,128)S(1)} %maximum_bitcast_fusion.refs_1_.refs_3_), channel_id=1, source_target_pairs={{1,2},{2,1},{3,4},{4,3},{5,6},{6,5},{7,8},{8,7},{9,10},{10,9},{11,... | collective-permute-start | bytes 1474568 | tf_op jit(solution)/shard_map/ppermute | solution.py:423
  5.0 3.3 %fusion.3 = (f32[60,40,128]{2,1,0:T(8,128)}, f32[60,40,128]{2,1,0:T(8,128)}) fusion(f32[60,120,128]{2,1,0:T(8,128)} %bitcast.11), kind=kLoop, calls=%fused_computation.15 | loop fusion | bytes 4915200 | tf_op jit(solution)/shard_map/slice | solution.py:460
  8.3 1.2 collective-permute-start.2
  9.5 0.2 constant_dynamic-slice_fusion
  10.0 1.5 %slice.9 = f32[60,48,128]{2,1,0:T(8,128)S(1)} slice(f32[60,120,128]{2,1,0:T(8,128)} %bitcast.12), slice={[0:60], [72:120], [0:128]} | slice | bytes 2949120 | tf_op jit(solution)/shard_map/slice | solution.py:461
  11.9 5.7 %collective-permute-done.refs_2_.refs_4_ = f32[8,120,128]{2,1,0:T(8,128)S(1)} collective-permute-done((f32[8,120,128]{2,1,0:T(8,128)S(1)}, f32[8,120,128]{2,1,0:T(8,128)S(1)}, u32[]{:S(2)}, u32[]{:S(2)}) %collective-permute-start) | collective-permute-done | bytes 491552 | tf_op jit(solution)/shard_map/ppermute | solution.py:423
  17.5 2.9 %collective-permute-start.3 = (f32[60,48,128]{2,1,0:T(8,128)S(1)}, f32[60,48,128]{2,1,0:T(8,128)S(1)}, u32[]{:S(2)}, u32[]{:S(2)}) collective-permute-start(f32[60,48,128]{2,1,0:T(8,128)S(1)} %slice.9), channel_id=1, source_target_pairs={{1,2},{2,1},{3,4},{4,3},{5,6},{6,5},{7,8},{8,7},{9,10},{10,9},{11,... | collective-permute-start | bytes 4423688 | tf_op jit(solution)/shard_map/ppermute | solution.py:423
  20.4 16.5 %collective-permute-done.2.refs_5_ = f32[60,40,128]{2,1,0:T(8,128)S(1)} collective-permute-done((f32[60,40,128]{2,1,0:T(8,128)}, f32[60,40,128]{2,1,0:T(8,128)S(1)}, u32[]{:S(2)}, u32[]{:S(2)}) %collective-permute-start.2) | collective-permute-done | bytes 1228832 | tf_op jit(solution)/shard_map/ppermute | solution.py:426
  36.9 1.2 collective-permute-start.5
  38.1 9.8 %gathered.2 = (f32[60,32,128]{2,1,0:T(8,128)S(1)}, f32[60,32,128]{2,1,0:T(8,128)}, f32[60,32,128]{2,1,0:T(8,128)}) custom-call(f32[60,120,128]{2,1,0:T(8,128)} %bitcast.13, f32[8,120,128]{2,1,0:T(8,128)S(1)} %maximum_bitcast_fusion.refs_1_.refs_3_, f32[8,120,128]{2,1,0:T(8,128)S(1)} %collective-permute-done.refs_2_.refs_4_, ...), custom_call_target="tpu_custom_call" | custom-call | flops 1209600 | bytes 32768 | tf_op jit(solution)/shard_map/gathered/pallas_call | solution.py:527
  47.9 6.5 %collective-permute-done.3.refs_1_ = f32[60,48,128]{2,1,0:T(8,128)S(1)} collective-permute-done((f32[60,48,128]{2,1,0:T(8,128)S(1)}, f32[60,48,128]{2,1,0:T(8,128)S(1)}, u32[]{:S(2)}, u32[]{:S(2)}) %collective-permute-start.3) | collective-permute-done | bytes 1474592 | tf_op jit(solution)/shard_map/ppermute | solution.py:423
  54.4 2.5 %collective-permute-start.6 = (f32[60,32,128]{2,1,0:T(8,128)}, f32[60,32,128]{2,1,0:T(8,128)S(1)}, u32[]{:S(2)}, u32[]{:S(2)}) collective-permute-start(f32[60,32,128]{2,1,0:T(8,128)} %get-tuple-element.59), channel_id=1, source_target_pairs={{1,2},{2,1},{3,4},{4,3},{5,6},{6,5},{7,8},{8,7},{9,10},{10,9},{11,... | collective-permute-start | bytes 2949128 | tf_op jit(solution)/shard_map/ppermute | solution.py:423
  57.0 7.7 %partial.2 = (f32[60,24,128]{2,1,0:T(8,128)S(1)}, f32[60,24,128]{2,1,0:T(8,128)}) custom-call(f32[60,120,128]{2,1,0:T(8,128)} %bitcast.14, f32[60,48,128]{2,1,0:T(8,128)S(1)} %collective-permute-done.3.refs_1_, f32[60,48,128]{2,1,0:T(8,128)} %copy-done.1, f32[8,120,128]{2,1,0:T(8,128)S(1)} %maximum_bitcast_fusion.refs_1_.refs_3_, ...), custom_call_target="tpu_custom_call" | custom-call | flops 907200 | bytes 24576 | tf_op jit(solution)/shard_map/partial/pallas_call | solution.py:498
  64.7 11.2 %collective-permute-start.8 = (f32[60,24,128]{2,1,0:T(8,128)}, f32[60,24,128]{2,1,0:T(8,128)S(1)}, u32[]{:S(2)}, u32[]{:S(2)}) collective-permute-start(f32[60,24,128]{2,1,0:T(8,128)} %get-tuple-element.61), channel_id=1, source_target_pairs={{0,16},{16,0},{1,17},{17,1},{2,18},{18,2},{3,19},{19,3},{4,20},{20... | collective-permute-start | bytes 2211848 | tf_op jit(solution)/shard_map/ppermute | solution.py:426
  75.9 11.8 %gathered.3 = (f32[60,40,128]{2,1,0:T(8,128)S(1)}, f32[60,40,128]{2,1,0:T(8,128)S(1)}, f32[60,40,128]{2,1,0:T(8,128)}) custom-call(f32[60,120,128]{2,1,0:T(8,128)} %bitcast.15, f32[8,120,128]{2,1,0:T(8,128)S(1)} %maximum_bitcast_fusion.refs_1_.refs_3_, f32[8,120,128]{2,1,0:T(8,128)S(1)} %collective-permute-done.refs_2_.refs_4_, ...), custom_call_target="tpu_custom_call" | custom-call | flops 1512000 | bytes 40960 | tf_op jit(solution)/shard_map/gathered/pallas_call | solution.py:527
  87.7 3.9 %collective-permute-start.9 = (f32[60,40,128]{2,1,0:T(8,128)S(1)}, f32[60,40,128]{2,1,0:T(8,128)S(1)}, u32[]{:S(2)}, u32[]{:S(2)}) collective-permute-start(f32[60,40,128]{2,1,0:T(8,128)S(1)} %get-tuple-element.67), channel_id=1, source_target_pairs={{1,2},{2,1},{3,4},{4,3},{5,6},{6,5},{7,8},{8,7},{9,10},{10,9},{11,... | collective-permute-start | bytes 3686408 | tf_op jit(solution)/shard_map/ppermute | solution.py:423
  91.8 0.7 collective-permute-done.8.refs_4_
  92.6 7.0 %partial.3 = (f32[60,24,128]{2,1,0:T(8,128)S(1)}, f32[60,24,128]{2,1,0:T(8,128)S(1)}) custom-call(f32[60,120,128]{2,1,0:T(8,128)} %bitcast.16, f32[60,48,128]{2,1,0:T(8,128)S(1)} %collective-permute-done.3.refs_1_, f32[60,48,128]{2,1,0:T(8,128)} %copy-done.1, f32[8,120,128]{2,1,0:T(8,128)S(1)} %maximum_bitcast_fusion.refs_1_.refs_3_, ...), custom_call_target="tpu_custom_call" | custom-call | flops 907200 | bytes 24576 | tf_op jit(solution)/shard_map/partial/pallas_call | solution.py:498
  99.5 1.2 collective-permute-start.11
  100.7 3.9 %place.2.refs_0_ = f32[60,120,128]{2,1,0:T(8,128)} custom-call(f32[60,32,128]{2,1,0:T(8,128)S(1)} %get-tuple-element.46.refs_0_, f32[60,32,128]{2,1,0:T(8,128)S(1)} %collective-permute-done.6.refs_1_, f32[60,32,128]{2,1,0:T(8,128)S(1)} %collective-permute-done.7.refs_2_, f32[60,24,128]{2,1,0:T(8,128)S(1)} %get-tuple-element.64.refs_3_, ...), custom_call_target="tpu_custom_call" | custom-call | tf_op jit(solution)/shard_map/place/pallas_call | solution.py:396
  104.6 14.6 %collective-permute-done.9.refs_2_ = f32[60,40,128]{2,1,0:T(8,128)S(1)} collective-permute-done((f32[60,40,128]{2,1,0:T(8,128)S(1)}, f32[60,40,128]{2,1,0:T(8,128)S(1)}, u32[]{:S(2)}, u32[]{:S(2)}) %collective-permute-start.9) | collective-permute-done | bytes 1228832 | tf_op jit(solution)/shard_map/ppermute | solution.py:423
  119.2 3.0 %place.3 = f32[60,120,128]{2,1,0:T(8,128)} custom-call(f32[60,120,128]{2,1,0:T(8,128)} %place.2.refs_0_, f32[60,40,128]{2,1,0:T(8,128)S(1)} %get-tuple-element.66.refs_1_, f32[60,40,128]{2,1,0:T(8,128)S(1)} %collective-permute-done.9.refs_2_, f32[60,40,128]{2,1,0:T(8,128)S(1)} %collective-permute-done.10.refs_3_, ...), custom_call_target="tpu_custom_call", output_to_operand_aliasing={{}: (0, {})} | custom-call | tf_op jit(solution)/shard_map/place/pallas_call | solution.py:396
  (26 shorter events, 0.8 us)
Async XLA Ops:
  1.1 8.4 %copy-start.3 = (f32[7,120,120]{2,1,0:T(8,128)S(1)}, f32[7,120,120]{2,1,0:T(8,128)}, u32[]{:S(2)}) copy-start(f32[7,120,120]{2,1,0:T(8,128)} %param.7) | copy-start | bytes 1209604
  1.1 10.8 %collective-permute-start.1 = (f32[8,120,128]{2,1,0:T(8,128)S(1)}, f32[8,120,128]{2,1,0:T(8,128)S(1)}, u32[]{:S(2)}, u32[]{:S(2)}) collective-permute-start(f32[8,120,128]{2,1,0:T(8,128)S(1)} %maximum_bitcast_fusion.refs_1_.refs_3_), channel_id=1, source_target_pairs={{0,1},{1,0},{2,3},{3,2},{4,5},{5,4},{6,7},{7,6},{8,9},{9,8},{10,11... | collective-permute-start | bytes 1474568 | tf_op jit(solution)/shard_map/ppermute | solution.py:423
  1.8 15.7 %collective-permute-start = (f32[8,120,128]{2,1,0:T(8,128)S(1)}, f32[8,120,128]{2,1,0:T(8,128)S(1)}, u32[]{:S(2)}, u32[]{:S(2)}) collective-permute-start(f32[8,120,128]{2,1,0:T(8,128)S(1)} %maximum_bitcast_fusion.refs_1_.refs_3_), channel_id=1, source_target_pairs={{1,2},{2,1},{3,4},{4,3},{5,6},{6,5},{7,8},{8,7},{9,10},{10,9},{11,... | collective-permute-start | bytes 1474568 | tf_op jit(solution)/shard_map/ppermute | solution.py:423
  8.3 28.6 %collective-permute-start.2 = (f32[60,40,128]{2,1,0:T(8,128)}, f32[60,40,128]{2,1,0:T(8,128)S(1)}, u32[]{:S(2)}, u32[]{:S(2)}) collective-permute-start(f32[60,40,128]{2,1,0:T(8,128)} %get-tuple-element.73), channel_id=1, source_target_pairs={{0,16},{16,0},{1,17},{17,1},{2,18},{18,2},{3,19},{19,3},{4,20},{20... | collective-permute-start | bytes 3686408 | tf_op jit(solution)/shard_map/ppermute | solution.py:426
  11.6 25.3 %copy-start.2 = (f32[60,40,128]{2,1,0:T(8,128)S(1)}, f32[60,40,128]{2,1,0:T(8,128)}, u32[]{:S(2)}) copy-start(f32[60,40,128]{2,1,0:T(8,128)} %get-tuple-element.56) | copy-start | bytes 3686404
  17.5 30.4 %collective-permute-start.4 = (f32[60,48,128]{2,1,0:T(8,128)S(1)}, f32[60,48,128]{2,1,0:T(8,128)S(1)}, u32[]{:S(2)}, u32[]{:S(2)}) collective-permute-start(f32[60,48,128]{2,1,0:T(8,128)S(1)} %slice.9), channel_id=1, source_target_pairs={{0,1},{1,0},{2,3},{3,2},{4,5},{5,4},{6,7},{7,6},{8,9},{9,8},{10,11... | collective-permute-start | bytes 4423688 | tf_op jit(solution)/shard_map/ppermute | solution.py:423
  17.5 36.9 %collective-permute-start.3 = (f32[60,48,128]{2,1,0:T(8,128)S(1)}, f32[60,48,128]{2,1,0:T(8,128)S(1)}, u32[]{:S(2)}, u32[]{:S(2)}) collective-permute-start(f32[60,48,128]{2,1,0:T(8,128)S(1)} %slice.9), channel_id=1, source_target_pairs={{1,2},{2,1},{3,4},{4,3},{5,6},{6,5},{7,8},{8,7},{9,10},{10,9},{11,... | collective-permute-start | bytes 4423688 | tf_op jit(solution)/shard_map/ppermute | solution.py:423
  36.9 11.0 %copy-start = (f32[60,40,128]{2,1,0:T(8,128)}, f32[60,40,128]{2,1,0:T(8,128)S(1)}, u32[]{:S(2)}) copy-start(f32[60,40,128]{2,1,0:T(8,128)S(1)} %collective-permute-done.2.refs_5_) | copy-start | bytes 3686404
  36.9 39.0 %collective-permute-start.5 = (f32[60,40,128]{2,1,0:T(8,128)S(1)}, f32[60,40,128]{2,1,0:T(8,128)}, u32[]{:S(2)}, u32[]{:S(2)}) collective-permute-start(f32[60,40,128]{2,1,0:T(8,128)S(1)} %copy-done.2), channel_id=1, source_target_pairs={{0,16},{16,0},{1,17},{17,1},{2,18},{18,2},{3,19},{19,3},{4,20},{20... | collective-permute-start | bytes 3686408 | tf_op jit(solution)/shard_map/ppermute | solution.py:426
  47.9 9.0 %copy-start.1 = (f32[60,48,128]{2,1,0:T(8,128)}, f32[60,48,128]{2,1,0:T(8,128)S(1)}, u32[]{:S(2)}) copy-start(f32[60,48,128]{2,1,0:T(8,128)S(1)} %collective-permute-done.4.refs_2_) | copy-start | bytes 4423684
  54.4 38.1 %collective-permute-start.6 = (f32[60,32,128]{2,1,0:T(8,128)}, f32[60,32,128]{2,1,0:T(8,128)S(1)}, u32[]{:S(2)}, u32[]{:S(2)}) collective-permute-start(f32[60,32,128]{2,1,0:T(8,128)} %get-tuple-element.59), channel_id=1, source_target_pairs={{1,2},{2,1},{3,4},{4,3},{5,6},{6,5},{7,8},{8,7},{9,10},{10,9},{11,... | collective-permute-start | bytes 2949128 | tf_op jit(solution)/shard_map/ppermute | solution.py:423
  56.9 35.7 %collective-permute-start.7 = (f32[60,32,128]{2,1,0:T(8,128)}, f32[60,32,128]{2,1,0:T(8,128)S(1)}, u32[]{:S(2)}, u32[]{:S(2)}) collective-permute-start(f32[60,32,128]{2,1,0:T(8,128)} %get-tuple-element.60), channel_id=1, source_target_pairs={{0,1},{1,0},{2,3},{3,2},{4,5},{5,4},{6,7},{7,6},{8,9},{9,8},{10,11... | collective-permute-start | bytes 2949128 | tf_op jit(solution)/shard_map/ppermute | solution.py:423
  64.7 27.9 %collective-permute-start.8 = (f32[60,24,128]{2,1,0:T(8,128)}, f32[60,24,128]{2,1,0:T(8,128)S(1)}, u32[]{:S(2)}, u32[]{:S(2)}) collective-permute-start(f32[60,24,128]{2,1,0:T(8,128)} %get-tuple-element.61), channel_id=1, source_target_pairs={{0,16},{16,0},{1,17},{17,1},{2,18},{18,2},{3,19},{19,3},{4,20},{20... | collective-permute-start | bytes 2211848 | tf_op jit(solution)/shard_map/ppermute | solution.py:426
  87.7 31.5 %collective-permute-start.9 = (f32[60,40,128]{2,1,0:T(8,128)S(1)}, f32[60,40,128]{2,1,0:T(8,128)S(1)}, u32[]{:S(2)}, u32[]{:S(2)}) collective-permute-start(f32[60,40,128]{2,1,0:T(8,128)S(1)} %get-tuple-element.67), channel_id=1, source_target_pairs={{1,2},{2,1},{3,4},{4,3},{5,6},{6,5},{7,8},{8,7},{9,10},{10,9},{11,... | collective-permute-start | bytes 3686408 | tf_op jit(solution)/shard_map/ppermute | solution.py:423
  91.6 27.6 %collective-permute-start.10 = (f32[60,40,128]{2,1,0:T(8,128)}, f32[60,40,128]{2,1,0:T(8,128)S(1)}, u32[]{:S(2)}, u32[]{:S(2)}) collective-permute-start(f32[60,40,128]{2,1,0:T(8,128)} %get-tuple-element.68), channel_id=1, source_target_pairs={{0,1},{1,0},{2,3},{3,2},{4,5},{5,4},{6,7},{7,6},{8,9},{9,8},{10,11... | collective-permute-start | bytes 3686408 | tf_op jit(solution)/shard_map/ppermute | solution.py:423
  99.5 19.7 %collective-permute-start.11 = (f32[60,24,128]{2,1,0:T(8,128)S(1)}, f32[60,24,128]{2,1,0:T(8,128)S(1)}, u32[]{:S(2)}, u32[]{:S(2)}) collective-permute-start(f32[60,24,128]{2,1,0:T(8,128)S(1)} %get-tuple-element.72), channel_id=1, source_target_pairs={{0,16},{16,0},{1,17},{17,1},{2,18},{18,2},{3,19},{19,3},{4,20},{20... | collective-permute-start | bytes 2211848 | tf_op jit(solution)/shard_map/ppermute | solution.py:426
